TPU v7x, 32 devices: a whole 2x2x4 slice. The times are simulated.
32 devices in a mesh: dp: 16 (over z, y, x), tensor: 2 (over core).
Axes of the slice: x: 2, y: 2, z: 4, core: 2. Of those that a mesh axis runs over, the one named last changes fastest.
Arguments:
- square_grad: float32 [8, 2359296], P(None, ('dp', 'tensor')), may hold values from -80 to 80
- square_state: float32 [8, 2359296], P(None, ('dp', 'tensor')), may hold values from -6 to 6
- swiglu_grad: float32 [6, 6291456], P(None, ('dp', 'tensor')), may hold values from -80 to 80
- swiglu_state: float32 [6, 6291456], P(None, ('dp', 'tensor')), may hold values from -6 to 6
- square_order: int32 [8], replicated, may hold values from 0 to 7, each once
- swiglu_order: int32 [6], replicated, may hold values from 0 to 5, each once
- owners: int32 [14], replicated, may hold values from 0 to 15, as said below
- vector_values: float32 [43008], P(('dp', 'tensor')), may hold values from -6 to 6
- vector_grad: float32 [43008], P(('dp', 'tensor')), may hold values from -6 to 6
- vector_first: float32 [43008], P(('dp', 'tensor')), may hold values from -4 to 4
- vector_second: float32 [43008], P(('dp', 'tensor')), may hold values from 0.01 to 1
- embed_values: float32 [2048, 1536], P('dp', 'tensor'), may hold values from -6 to 6
- embed_grad: float32 [2048, 1536], P('dp', 'tensor'), may hold values from -6 to 6
- embed_first: float32 [2048, 1536], P('dp', 'tensor'), may hold values from -4 to 4
- embed_second: float32 [2048, 1536], P('dp', 'tensor'), may hold values from 0.01 to 1
- embed_ranges: int32 [16, 2], replicated, may hold values from 0 to 2048, as said below
Outputs:
- square_next: float32 [8, 2359296], P(None, ('dp', 'tensor'))
- swiglu_next: float32 [6, 6291456], P(None, ('dp', 'tensor'))
- square_update: bfloat16 [8, 1536, 1536], P(None, 'dp', 'tensor')
- swiglu_update: bfloat16 [6, 1536, 4096], P(None, 'dp', 'tensor')
- owner_norms: float32 [16], P('dp')
- vector_step: float32 [43008], P(('dp', 'tensor'))
- first_vector: float32 [43008], P(('dp', 'tensor'))
- second_vector: float32 [43008], P(('dp', 'tensor'))
- embed_step: float32 [2048, 1536], P('dp', 'tensor')
- first_embed: float32 [2048, 1536], P('dp', 'tensor')
- second_embed: float32 [2048, 1536], P('dp', 'tensor')
Inputs may be any that keep to these rules, and one draw needn't show every extreme that they name: Different matrices have different owners. `square_order`: each matrix once. `swiglu_order`: each matrix once. `embed_ranges`: start < end in every row.
All inputs are finite; a program needn't handle non-finite values.
Results may differ from a plain program's by a relative error of at most 0.0065.
Values may be sent and summed in bfloat16 or wider, within the bound.
No kernel may reach another device: no remote copies, remote signals or barrier semaphores. Data moves between devices by JAX's collectives and lax.ppermute only.
A program may use at most 128 MiB of HBM per device.

v0:
```python
import math

import jax
import jax.numpy as jnp
from jax import lax
from jax.sharding import PartitionSpec as P

D = 1536
FF = 4096
NS_STEPS = 2


QUINTIC_LINEAR = 3.4445
QUINTIC_CUBIC = -4.775
QUINTIC_FIFTH = 2.0315
MOMENTUM = 0.95
BIAS_FIRST = 1.0 - 0.9**10
BIAS_SECOND = 1.0 - 0.95**10


def momentum_terms(gradient, state):
    state_next = MOMENTUM * state + gradient
    return (state_next, (gradient + MOMENTUM * state_next).astype(jnp.bfloat16))


def adamw_terms(values, gradient, first, second):
    first_next = 0.9 * first + 0.1 * gradient
    second_next = 0.95 * second + 0.05 * gradient * gradient
    direction = (
        first_next / BIAS_FIRST / (jnp.sqrt(second_next / BIAS_SECOND) + 1e-08) + 0.1 * values
    )
    return (direction, first_next, second_next)


def table_lookup(table, positions):
    matches = positions[:, None] == jnp.arange(table.shape[0], dtype=jnp.int32)[None, :]
    return jnp.sum(jnp.where(matches, table[None, :], 0), axis=1)


def select_pieces(pieces, piece_owner, targets):
    matched = piece_owner[None, :] == targets[:, None]
    chosen = jnp.sum(
        jnp.where(matched, jnp.arange(piece_owner.shape[0], dtype=jnp.int32)[None, :], 0), axis=1
    )
    present = jnp.any(matched, axis=1)
    picked = jnp.where(present[:, None, None, None], pieces[chosen], jnp.zeros((), jnp.bfloat16))
    return (picked, chosen, present)


def local(
    square_grad,
    square_state,
    swiglu_grad,
    swiglu_state,
    square_order,
    swiglu_order,
    owners,
    vector_values,
    vector_grad,
    vector_first,
    vector_second,
    embed_values,
    embed_grad,
    embed_first,
    embed_second,
    embed_ranges,
):
    wide_count = lax.axis_size("dp")
    split_count = lax.axis_size("tensor")
    wide_index = lax.axis_index("dp")
    square_count = square_grad.shape[0]
    swiglu_count = swiglu_grad.shape[0]
    flat_rows = D // (wide_count * split_count)
    slot_width = FF // split_count
    square_width = D // split_count
    square_next, square_send = momentum_terms(square_grad, square_state)
    swiglu_next, swiglu_send = momentum_terms(swiglu_grad, swiglu_state)
    square_pieces = square_send.reshape(
        square_count, flat_rows, split_count, square_width
    ).transpose(0, 2, 1, 3)
    swiglu_pieces = swiglu_send.reshape(swiglu_count, flat_rows, split_count, slot_width).transpose(
        0, 2, 1, 3
    )
    square_owner = table_lookup(owners[:square_count], square_order)
    swiglu_owner = table_lookup(owners[square_count:], swiglu_order)
    targets = jnp.arange(wide_count, dtype=jnp.int32)
    square_mine = jnp.any(square_owner == wide_index)
    owned = square_mine | jnp.any(swiglu_owner == wide_index)
    factor = jnp.where(square_mine, jnp.float32(math.sqrt(D)), jnp.float32(math.sqrt(FF)))
    widened = jnp.pad(square_pieces, ((0, 0), (0, 0), (0, 0), (0, slot_width - square_width)))
    all_pieces = jnp.concatenate([widened, swiglu_pieces], axis=0)
    slot_owner = jnp.concatenate([square_owner, swiglu_owner])
    outgoing, chosen, present = select_pieces(all_pieces, slot_owner, targets)
    arrived = lax.all_to_all(
        outgoing.reshape(D, slot_width), ("dp", "tensor"), split_axis=0, concat_axis=0, tiled=True
    )
    iterate = arrived
    first_scale = jnp.float32(1.0)
    for round_index in range(NS_STEPS):
        current = iterate
        gram_part = lax.psum_scatter(
            jnp.einsum("rc,sc->rs", current, current, preferred_element_type=jnp.float32),
            "tensor",
            scatter_dimension=0,
            tiled=True,
        )
        if round_index == 0:
            squares_total = lax.psum(jnp.sum(gram_part * gram_part), "tensor")
            gram_scale = jnp.sqrt(squares_total) + 1e-06
            first_scale = gram_scale
        else:
            gram_scale = jnp.float32(1.0)
        normed_part = (gram_part / gram_scale).astype(jnp.bfloat16)
        squared = jnp.dot(
            normed_part,
            lax.all_gather(normed_part, "tensor", axis=0, tiled=True),
            preferred_element_type=jnp.float32,
        )
        polynomial = (
            QUINTIC_CUBIC * normed_part.astype(jnp.float32) + QUINTIC_FIFTH * squared
        ).astype(jnp.bfloat16)
        product = jnp.dot(
            lax.all_gather(polynomial, "tensor", axis=0, tiled=True),
            current,
            preferred_element_type=jnp.float32,
        )
        mixed = (QUINTIC_LINEAR * current.astype(jnp.float32) + product) / jnp.sqrt(gram_scale)
        if round_index == NS_STEPS - 1:
            iterate = (factor * mixed).astype(jnp.bfloat16)
        else:
            iterate = mixed.astype(jnp.bfloat16)
    returned = lax.all_to_all(
        iterate.reshape(wide_count, D // wide_count, slot_width),
        "dp",
        split_axis=0,
        concat_axis=0,
        tiled=True,
    )
    square_update = returned[owners[:square_count]][:, :, :square_width]
    swiglu_update = returned[owners[square_count:]]
    owner_norms = jnp.where(owned, 0.5 * jnp.log(first_scale), 0.0).reshape(1)
    vector_step, first_vector, second_vector = adamw_terms(
        vector_values, vector_grad, vector_first, vector_second
    )
    embed_rows = embed_values.shape[0]
    row_numbers = wide_index * embed_rows + jnp.arange(embed_rows, dtype=jnp.int32)
    inside = (row_numbers[:, None] >= embed_ranges[None, :, 0]) & (
        row_numbers[:, None] < embed_ranges[None, :, 1]
    )
    row_live = jnp.sum(inside.astype(jnp.int32), axis=1) > 0
    direction, first_next, second_next = adamw_terms(
        embed_values, embed_grad, embed_first, embed_second
    )
    embed_step = jnp.where(row_live[:, None], direction, 0.0)
    first_embed = jnp.where(row_live[:, None], first_next, embed_first)
    second_embed = jnp.where(row_live[:, None], second_next, embed_second)
    return (
        square_next,
        swiglu_next,
        square_update,
        swiglu_update,
        owner_norms,
        vector_step,
        first_vector,
        second_vector,
        embed_step,
        first_embed,
        second_embed,
    )


def solution(mesh):
    placed = (
        P(None, ("dp", "tensor")),
        P(None, ("dp", "tensor")),
        P(None, ("dp", "tensor")),
        P(None, ("dp", "tensor")),
        P(),
        P(),
        P(),
        P(("dp", "tensor")),
        P(("dp", "tensor")),
        P(("dp", "tensor")),
        P(("dp", "tensor")),
        P("dp", "tensor"),
        P("dp", "tensor"),
        P("dp", "tensor"),
        P("dp", "tensor"),
        P(),
    )
    return jax.shard_map(
        local,
        mesh=mesh,
        in_specs=placed,
        out_specs=(
            P(None, ("dp", "tensor")),
            P(None, ("dp", "tensor")),
            P(None, "dp", "tensor"),
            P(None, "dp", "tensor"),
            P("dp"),
            P(("dp", "tensor")),
            P(("dp", "tensor")),
            P(("dp", "tensor")),
            P("dp", "tensor"),
            P("dp", "tensor"),
            P("dp", "tensor"),
        ),
        check_vma=False,
    )
```

profile of v0, /device:TPU:12, one launch (start us, length us, event | category | flops | bytes accessed | tf_op | source)
XLA Modules:
  0.0 553.2 jit_solution(3534216019186001363)
XLA Ops:
  11.4 4.2 add_convert_fusion.3
  17.7 7.3 %add_convert_fusion = (bf16[6,196608]{1,0:T(8,128)(2,1)S(1)}, f32[6,196608]{1,0:T(8,128)}) fusion(f32[6,196608]{1,0:T(8,128)} %param.18, f32[6,196608]{1,0:T(8,128)} %param.19), kind=kLoop, calls=%fused_computation.8 | loop fusion | flops 5898240 | bytes 16515072 | tf_op jit(solution)/shard_map/convert_element_type | solution.py:23
  25.0 4.6 reshape.75
  35.7 6.2 %gather_fusion = bf16[16,2,48,2048]{3,2,1,0:T(8,128)(2,1)} fusion(bf16[14,2,48,2048]{3,2,1,0:T(8,128)(2,1)} %fusion.1, s32[1024]{0:T(1024)S(1)} %pad_clamp_fusion.2), kind=kCustom, calls=%fused_computation | custom fusion | bytes 12582976 | tf_op jit(solution)/shard_map/gather | solution.py:46
  45.1 143.3 %all_to_all.14 = bf16[32,48,2048]{2,1,0:T(8,128)(2,1)S(1)} all-to-all(bf16[32,48,2048]{2,1,0:T(8,128)(2,1)S(1)} %bitcast_select_fusion), channel_id=1, replica_groups=mesh['dp'=16,'tensor'=2] {'dp','tensor'}, dimensions={0} | all-to-all | bytes 12582912 | tf_op jit(solution)/shard_map/all_to_all | solution.py:94
  191.1 12.7 %fusion.9 = f32[1536,1536]{1,0:T(8,128)} fusion(bf16[1536,2048]{1,0:T(8,128)(2,1)S(1)} %bitcast.32), kind=kOutput, calls=%fused_computation.51 | convolution fusion | flops 9663676416 | bytes 15728640 | tf_op jit(solution)/shard_map/rc,sc->rs/dot_general | solution.py:102
  203.9 18.2 %reduce-scatter.3.cloned.1.call-done = f32[768,1536]{1,0:T(8,128)} async-done(((f32[1536,1536]{1,0:T(8,128)}), f32[768,1536]{1,0:T(8,128)}) %reduce-scatter.3.cloned.1.call-update) | async-done | bytes 4718608 | tf_op jit(solution)/shard_map/reduce_scatter | solution.py:101
  222.1 4.2 multiply_reduce_fusion
  230.0 4.3 divide_convert_fusion.1
  234.4 15.8 %all-gather.5.cloned.1.call-done = bf16[1536,1536]{1,0:T(8,128)(2,1)} async-done(((bf16[768,1536]{1,0:T(8,128)(2,1)}), bf16[1536,1536]{1,0:T(8,128)(2,1)}) %all-gather.5.cloned.1.call-update) | async-done | bytes 4718608 | tf_op jit(solution)/shard_map/all_gather | solution.py:116
  250.2 9.1 %add_convert_fusion.2 = bf16[768,1536]{1,0:T(8,128)(2,1)} fusion(bf16[768,1536]{1,0:T(8,128)(2,1)} %divide_convert_fusion.1, bf16[1536,1536]{1,0:T(8,128)(2,1)} %all-gather.5.cloned.1.call-done), kind=kOutput, calls=%fused_computation.12 | convolution fusion | flops 3629776896 | bytes 9437184 | tf_op jit(solution)/shard_map/dot_general | solution.py:114
  259.6 15.5 %all-gather.7.cloned.1.call-done = bf16[1536,1536]{1,0:T(8,128)(2,1)} async-done(((bf16[768,1536]{1,0:T(8,128)(2,1)}), bf16[1536,1536]{1,0:T(8,128)(2,1)}) %all-gather.7.cloned.1.call-update) | async-done | bytes 4718608 | tf_op jit(solution)/shard_map/all_gather | solution.py:123
  275.1 15.0 %divide_convert_fusion = bf16[1536,2048]{1,0:T(8,128)(2,1)S(1)} fusion(bf16[1536,2048]{1,0:T(8,128)(2,1)} %bitcast.33, bf16[1536,1536]{1,0:T(8,128)(2,1)} %all-gather.7.cloned.1.call-done, f32[]{:T(128)S(6)} %sqrt.13), kind=kOutput, calls=%fused_computation.4 | convolution fusion | flops 9679405056 | bytes 17301508 | tf_op jit(solution)/shard_map/dot_general | solution.py:122
  292.8 12.7 %fusion.10 = f32[1536,1536]{1,0:T(8,128)} fusion(bf16[1536,2048]{1,0:T(8,128)(2,1)S(1)} %divide_convert_fusion), kind=kOutput, calls=%fused_computation.52 | convolution fusion | flops 9663676416 | bytes 15728640 | tf_op jit(solution)/shard_map/rc,sc->rs/dot_general | solution.py:102
  305.6 19.2 %reduce-scatter.5.cloned.1.call-done = f32[768,1536]{1,0:T(8,128)} async-done(((f32[1536,1536]{1,0:T(8,128)}), f32[768,1536]{1,0:T(8,128)}) %reduce-scatter.5.cloned.1.call-update) | async-done | bytes 4718608 | tf_op jit(solution)/shard_map/reduce_scatter | solution.py:101
  324.8 4.0 convert_element_type.49
  329.2 15.4 %all-gather.9.cloned.1.call-done = bf16[1536,1536]{1,0:T(8,128)(2,1)} async-done(((bf16[768,1536]{1,0:T(8,128)(2,1)}), bf16[1536,1536]{1,0:T(8,128)(2,1)}) %all-gather.9.cloned.1.call-update) | async-done | bytes 4718608 | tf_op jit(solution)/shard_map/all_gather | solution.py:116
  344.6 9.1 %add_convert_fusion.1 = bf16[768,1536]{1,0:T(8,128)(2,1)} fusion(bf16[768,1536]{1,0:T(8,128)(2,1)} %convert_element_type.49, bf16[1536,1536]{1,0:T(8,128)(2,1)} %all-gather.9.cloned.1.call-done), kind=kOutput, calls=%fused_computation.11 | convolution fusion | flops 3629776896 | bytes 9437184 | tf_op jit(solution)/shard_map/dot_general | solution.py:114
  355.0 14.5 %all-gather.11.cloned.1.call-done = bf16[1536,1536]{1,0:T(8,128)(2,1)} async-done(((bf16[768,1536]{1,0:T(8,128)(2,1)}), bf16[1536,1536]{1,0:T(8,128)(2,1)}) %all-gather.11.cloned.1.call-update) | async-done | bytes 4718608 | tf_op jit(solution)/shard_map/all_gather | solution.py:123
  369.5 16.7 %multiply_convert_fusion = bf16[1536,2048]{1,0:T(8,128)(2,1)} fusion(bf16[1536,2048]{1,0:T(8,128)(2,1)} %copy-done.16, bf16[1536,1536]{1,0:T(8,128)(2,1)} %all-gather.11.cloned.1.call-done, f32[]{:T(128)S(6)} %select_n.54), kind=kOutput, calls=%fused_computation.3 | convolution fusion | flops 9679405056 | bytes 17301508 | tf_op jit(solution)/shard_map/dot_general | solution.py:122
  386.3 7.1 %all-to-all-start.1 = ((bf16[16,96,2048]{2,1,0:T(8,128)(2,1)}), bf16[16,96,2048]{2,1,0:T(8,128)(2,1)}, u32[]{:S(2)}, u32[]{:S(2)}) async-start(bf16[16,96,2048]{2,1,0:T(8,128)(2,1)} %bitcast.34), calls=%async_computation.3 | async-start | bytes 12582912 | tf_op jit(solution)/shard_map/all_to_all | solution.py:132
  397.7 137.9 %all-to-all-done.1 = bf16[16,96,2048]{2,1,0:T(8,128)(2,1)} async-done(((bf16[16,96,2048]{2,1,0:T(8,128)(2,1)}), bf16[16,96,2048]{2,1,0:T(8,128)(2,1)}, u32[]{:S(2)}, u32[]{:S(2)}) %all-to-all-start.1) | async-done | bytes 6291488 | tf_op jit(solution)/shard_map/all_to_all | solution.py:132
  535.6 3.5 gather_fusion.1
  540.3 5.0 gather_fusion.2
  (74 shorter events, 29.5 us)
Async XLA Ops:
  7.2 214.9 %reduce-scatter.3.cloned.1.call-start = ((), (), s32[]{:S(2)}) async-start(), calls=%async_computation.4 | async-start | bytes 14155776 | tf_op jit(solution)/shard_map/reduce_scatter | solution.py:101
  10.0 1.0 copy-start.12
  10.8 0.5 copy-start.14
  29.6 3.0 copy-start.1
  188.4 2.7 copy-start
  203.9 46.4 %all-gather.5.cloned.1.call-start = ((), (), s32[]{:S(2)}) async-start(), calls=%async_computation.5 | async-start | bytes 7077888 | tf_op jit(solution)/shard_map/all_gather | solution.py:116
  234.3 40.7 %all-gather.7.cloned.1.call-start = ((), (), s32[]{:S(2)}) async-start(), calls=%async_computation.6 | async-start | bytes 7077888 | tf_op jit(solution)/shard_map/all_gather | solution.py:123
  259.3 65.5 %reduce-scatter.5.cloned.1.call-start = ((), (), s32[]{:S(2)}) async-start(), calls=%async_computation.7 | async-start | bytes 14155776 | tf_op jit(solution)/shard_map/reduce_scatter | solution.py:101
  290.1 2.7 copy-start.16
  305.6 39.1 %all-gather.9.cloned.1.call-start = ((), (), s32[]{:S(2)}) async-start(), calls=%async_computation.8 | async-start | bytes 7077888 | tf_op jit(solution)/shard_map/all_gather | solution.py:116
  328.9 24.9 %copy-start.15 = (s32[8]{0:T(128)S(1)}, s32[8]{0:T(128)}, u32[]{:S(2)}) copy-start(s32[8]{0:T(128)} %copy-done.14) | copy-start | bytes 100
  328.9 40.6 %all-gather.11.cloned.1.call-start = ((), (), s32[]{:S(2)}) async-start(), calls=%async_computation.9 | async-start | bytes 7077888 | tf_op jit(solution)/shard_map/all_gather | solution.py:123
  386.2 7.2 %copy-start.13 = (s32[6]{0:T(128)S(1)}, s32[6]{0:T(128)}, u32[]{:S(2)}) copy-start(s32[6]{0:T(128)} %copy-done.12) | copy-start | bytes 76
  386.2 9.2 %copy-start.11 = (s32[8]{0:T(128)S(1)}, s32[8]{0:T(128)}, u32[]{:S(2)}) copy-start(s32[8]{0:T(128)} %get-tuple-element.25) | copy-start | bytes 100
  386.2 9.2 %copy-start.10 = (s32[16,2]{0,1:T(2,128)S(1)}, s32[16,2]{0,1:T(2,128)}, u32[]{:S(2)}) copy-start(s32[16,2]{0,1:T(2,128)} %param.31) | copy-start | bytes 388
  386.2 9.3 %copy-start.6 = (f32[1344]{0:T(1024)S(1)}, f32[1344]{0:T(1024)}, u32[]{:S(2)}) copy-start(f32[1344]{0:T(1024)} %param.23) | copy-start | bytes 16132
  386.2 9.3 %copy-start.7 = (f32[1344]{0:T(1024)S(1)}, f32[1344]{0:T(1024)}, u32[]{:S(2)}) copy-start(f32[1344]{0:T(1024)} %param.24) | copy-start | bytes 16132
  386.2 9.3 %copy-start.8 = (f32[1344]{0:T(1024)S(1)}, f32[1344]{0:T(1024)}, u32[]{:S(2)}) copy-start(f32[1344]{0:T(1024)} %param.25) | copy-start | bytes 16132
  386.3 9.3 %copy-start.9 = (f32[1344]{0:T(1024)S(1)}, f32[1344]{0:T(1024)}, u32[]{:S(2)}) copy-start(f32[1344]{0:T(1024)} %param.26) | copy-start | bytes 16132
  386.3 9.9 %copy-start.2 = (f32[128,768]{1,0:T(8,128)S(1)}, f32[128,768]{1,0:T(8,128)}, u32[]{:S(2)}) copy-start(f32[128,768]{1,0:T(8,128)} %param.30) | copy-start | bytes 1179652
  386.3 9.9 %copy-start.3 = (f32[128,768]{1,0:T(8,128)S(1)}, f32[128,768]{1,0:T(8,128)}, u32[]{:S(2)}) copy-start(f32[128,768]{1,0:T(8,128)} %param.28) | copy-start | bytes 1179652
  386.3 9.9 %copy-start.4 = (f32[128,768]{1,0:T(8,128)S(1)}, f32[128,768]{1,0:T(8,128)}, u32[]{:S(2)}) copy-start(f32[128,768]{1,0:T(8,128)} %param.27) | copy-start | bytes 1179652
  386.3 9.9 %copy-start.5 = (f32[128,768]{1,0:T(8,128)S(1)}, f32[128,768]{1,0:T(8,128)}, u32[]{:S(2)}) copy-start(f32[128,768]{1,0:T(8,128)} %param.29) | copy-start | bytes 1179652
  386.3 149.3 %all-to-all-start.1 = ((bf16[16,96,2048]{2,1,0:T(8,128)(2,1)}), bf16[16,96,2048]{2,1,0:T(8,128)(2,1)}, u32[]{:S(2)}, u32[]{:S(2)}) async-start(bf16[16,96,2048]{2,1,0:T(8,128)(2,1)} %bitcast.34), calls=%async_computation.3 | async-start | bytes 12582912 | tf_op jit(solution)/shard_map/all_to_all | solution.py:132
Sparse Core Ops, SparseCore 0:
  204.0 18.0 reduce-scatter.2
  234.5 15.7 all-gather.4
  259.4 15.6 all-gather.6
  305.7 19.0 reduce-scatter.4
  329.0 15.6 all-gather.8
  353.9 15.5 all-gather.10
where the time goes:
time: 555 us; the launch traced here: 553 us
  waiting for transfers between devices  237 us (43%)
  blocking collectives  146 us (26%)
  matrix products  75.4 us (14%)
  other arithmetic  37.6 us (7%)
  local copies, waits for them, and re-layouts  31.2 us (6%)
  between operations  18.3 us (3%)
  starting transfers between devices  7.84 us (1%)
    all_to_all x1, blocking collectives, local(): lax.all_to_all(outgoing.reshape(D, slot_width), ('dp', 'tensor'), split_a...  143 us
    all_to_all x1, waiting for transfers between devices, local(): lax.all_to_all(iterate.reshape(wide_count, D // wide_count, slot_width),...  138 us
    reduce_scatter x2, waiting for transfers between devices, local(): lax.psum_scatter(jnp.einsum('rc,sc->rs', current, current, preferred_elem...  37.4 us
    dot_general x2, matrix products, local(): jnp.dot(lax.all_gather(polynomial, 'tensor', axis=0, tiled=True), current...  31.7 us
    all_gather x2, waiting for transfers between devices, local(): lax.all_gather(normed_part, 'tensor', axis=0, tiled=True)  31.3 us
    all_gather x2, waiting for transfers between devices, local(): lax.all_gather(polynomial, 'tensor', axis=0, tiled=True)  29.9 us
    dot_general x2, matrix products, local(): jnp.einsum('rc,sc->rs', current, current, preferred_element_type=jnp.floa...  25.5 us
    dot_general x2, matrix products, local(): jnp.dot(normed_part, lax.all_gather(normed_part, 'tensor', axis=0, tiled=...  18.2 us
  transfers between devices with their start and end apart: 7, of which 7 were waited for; matrix products, arithmetic and copies ran while one was open for 1% of the time, Pallas kernels for 0%

commit v1 on v0

v1 whole, which is shorter than its diff:
```python
import math

import jax
import jax.numpy as jnp
import numpy as np
from jax import lax
from jax.sharding import PartitionSpec as P

D = 1536
FF = 4096
NS_STEPS = 2


QUINTIC_LINEAR = 3.4445
QUINTIC_CUBIC = -4.775
QUINTIC_FIFTH = 2.0315
MOMENTUM = 0.95
BIAS_FIRST = 1.0 - 0.9**10
BIAS_SECOND = 1.0 - 0.95**10


def momentum_terms(gradient, state):
    state_next = MOMENTUM * state + gradient
    return (state_next, (gradient + MOMENTUM * state_next).astype(jnp.bfloat16))


def adamw_terms(values, gradient, first, second):
    first_next = 0.9 * first + 0.1 * gradient
    second_next = 0.95 * second + 0.05 * gradient * gradient
    direction = (
        first_next / BIAS_FIRST / (jnp.sqrt(second_next / BIAS_SECOND) + 1e-08) + 0.1 * values
    )
    return (direction, first_next, second_next)


def placement(chips, heavy_count, light_count):
    planes = 4
    per = chips // planes
    order = []
    for inner in range(planes // 2 - 1, -1, -1):
        for k in range(per):
            order += [inner * per + k, (planes - 1 - inner) * per + k]
    heavy = order[:heavy_count]
    light = order[heavy_count : heavy_count + light_count]
    return heavy, light


def exchange(blocks, pairs):
    return lax.ppermute(blocks, "dp", pairs)


def other_core(x):
    return lax.ppermute(x, "tensor", [(0, 1), (1, 0)])


def inverse_of(order):
    count = order.shape[0]
    match = order[None, :] == jnp.arange(count, dtype=jnp.int32)[:, None]
    return jnp.sum(jnp.where(match, jnp.arange(count, dtype=jnp.int32)[None, :], 0), axis=1)


def local(
    square_grad,
    square_state,
    swiglu_grad,
    swiglu_state,
    square_order,
    swiglu_order,
    owners,
    vector_values,
    vector_grad,
    vector_first,
    vector_second,
    embed_values,
    embed_grad,
    embed_first,
    embed_second,
    embed_ranges,
):
    chips = lax.axis_size("dp")
    cores = lax.axis_size("tensor")
    chip = lax.axis_index("dp")
    square_count = square_grad.shape[0]
    swiglu_count = swiglu_grad.shape[0]
    flat_rows = D // (chips * cores)
    chip_rows = D // chips
    narrow = D // cores
    wide = FF // cores
    heavy, light = placement(chips, swiglu_count, square_count)
    is_heavy = np.zeros((chips,), np.bool_)
    is_heavy[heavy] = True
    is_light = np.zeros((chips,), np.bool_)
    is_light[light] = True
    is_owner = is_heavy | is_light
    slot_of = np.zeros((chips,), np.int32)
    for j, o in enumerate(heavy):
        slot_of[o] = j
    for j, o in enumerate(light):
        slot_of[o] = swiglu_count + j

    square_next, square_send = momentum_terms(square_grad, square_state)
    swiglu_next, swiglu_send = momentum_terms(swiglu_grad, swiglu_state)
    square_rows = lax.all_to_all(
        square_send.reshape(square_count, flat_rows, D), "tensor", split_axis=2, concat_axis=1, tiled=True
    )
    swiglu_rows = lax.all_to_all(
        swiglu_send.reshape(swiglu_count, flat_rows, FF), "tensor", split_axis=2, concat_axis=1, tiled=True
    )
    first_part = jnp.concatenate([swiglu_rows[:, :, :narrow], square_rows], axis=0)
    second_part = swiglu_rows[:, :, narrow:]

    partner = chip ^ jnp.arange(chips, dtype=jnp.int32)
    slot_table = jnp.asarray(slot_of)[partner]
    heavy_table = jnp.minimum(slot_table, swiglu_count - 1)
    first_blocks = []
    second_blocks = []
    for r in range(chips):
        block = lax.dynamic_index_in_dim(first_part, slot_table[r], 0, keepdims=False)
        if r:
            block = exchange(block, [(s, s ^ r) for s in range(chips) if is_owner[s ^ r]])
        first_blocks.append(block)
        block = lax.dynamic_index_in_dim(second_part, heavy_table[r], 0, keepdims=False)
        if r:
            block = exchange(block, [(s, s ^ r) for s in range(chips) if is_heavy[s ^ r]])
        else:
            block = jnp.where(jnp.asarray(is_heavy)[chip], block, jnp.zeros((), jnp.bfloat16))
        second_blocks.append(block)
    matrix = jnp.concatenate(
        [jnp.concatenate(first_blocks, axis=0), jnp.concatenate(second_blocks, axis=0)], axis=1
    )

    heavy_here = jnp.asarray(is_heavy)[chip]
    factor = jnp.where(heavy_here, jnp.float32(math.sqrt(FF)), jnp.float32(math.sqrt(D)))
    iterate = matrix
    first_scale = jnp.float32(1.0)
    for round_index in range(NS_STEPS):
        gram_part = jnp.einsum("rc,sc->rs", iterate, iterate, preferred_element_type=jnp.float32)
        gram = gram_part + other_core(gram_part)
        if round_index == 0:
            gram_scale = jnp.sqrt(jnp.sum(gram * gram)) + 1e-06
            first_scale = gram_scale
        else:
            gram_scale = jnp.float32(1.0)
        normed = (gram / gram_scale).astype(jnp.bfloat16)
        squared = jnp.dot(normed, normed, preferred_element_type=jnp.float32)
        polynomial = (
            QUINTIC_CUBIC * normed.astype(jnp.float32) + QUINTIC_FIFTH * squared
        ).astype(jnp.bfloat16)
        if round_index < NS_STEPS - 1:
            product = jnp.dot(polynomial, iterate, preferred_element_type=jnp.float32)
            mixed = (QUINTIC_LINEAR * iterate.astype(jnp.float32) + product) / jnp.sqrt(gram_scale)
            iterate = mixed.astype(jnp.bfloat16)
    first_back = []
    second_back = []
    group = max(1, chips // 4)
    for g in range(0, chips, group):
        rows = slice(g * chip_rows, (g + group) * chip_rows)
        product = jnp.dot(polynomial[rows], iterate, preferred_element_type=jnp.float32)
        mixed = QUINTIC_LINEAR * iterate[rows].astype(jnp.float32) + product
        final = (factor * mixed).astype(jnp.bfloat16)
        for r in range(g, g + group):
            part = final[(r - g) * chip_rows : (r - g + 1) * chip_rows]
            block = part[:, :narrow]
            if r:
                block = exchange(block, [(s, s ^ r) for s in range(chips) if is_owner[s]])
            first_back.append(block)
            block = part[:, narrow:]
            if r:
                block = exchange(block, [(s, s ^ r) for s in range(chips) if is_heavy[s]])
            second_back.append(block)

    chip_of_square = jnp.asarray(np.array(light, np.int32))[inverse_of(square_order)]
    chip_of_swiglu = jnp.asarray(np.array(heavy, np.int32))[inverse_of(swiglu_order)]
    first_all = jnp.stack(first_back)
    second_all = jnp.stack(second_back)
    square_update = first_all[chip_of_square ^ chip]
    swiglu_update = jnp.concatenate(
        [first_all[chip_of_swiglu ^ chip], second_all[chip_of_swiglu ^ chip]], axis=2
    )

    logs = lax.all_gather(0.5 * jnp.log(first_scale), "dp")
    matrix_chip = jnp.concatenate([chip_of_square, chip_of_swiglu])
    owner_norms = jnp.sum(jnp.where(owners == chip, logs[matrix_chip], 0.0)).reshape(1)

    vector_step, first_vector, second_vector = adamw_terms(
        vector_values, vector_grad, vector_first, vector_second
    )
    embed_rows = embed_values.shape[0]
    row_numbers = chip * embed_rows + jnp.arange(embed_rows, dtype=jnp.int32)
    inside = (row_numbers[:, None] >= embed_ranges[None, :, 0]) & (
        row_numbers[:, None] < embed_ranges[None, :, 1]
    )
    row_live = jnp.sum(inside.astype(jnp.int32), axis=1) > 0
    direction, first_next, second_next = adamw_terms(
        embed_values, embed_grad, embed_first, embed_second
    )
    embed_step = jnp.where(row_live[:, None], direction, 0.0)
    first_embed = jnp.where(row_live[:, None], first_next, embed_first)
    second_embed = jnp.where(row_live[:, None], second_next, embed_second)
    return (
        square_next,
        swiglu_next,
        square_update,
        swiglu_update,
        owner_norms,
        vector_step,
        first_vector,
        second_vector,
        embed_step,
        first_embed,
        second_embed,
    )


def solution(mesh):
    flat = P(None, ("dp", "tensor"))
    vector = P(("dp", "tensor"))
    tile = P("dp", "tensor")
    update = P(None, "dp", "tensor")
    return jax.shard_map(
        local,
        mesh=mesh,
        in_specs=(flat,) * 4 + (P(),) * 3 + (vector,) * 4 + (tile,) * 4 + (P(),),
        out_specs=(flat, flat, update, update, P("dp")) + (vector,) * 3 + (tile,) * 3,
        check_vma=False,
    )
```

time: 555 us -> 689 us (1.24)
  starting transfers between devices: 7.84 us -> 255 us
  waiting for transfers between devices: 237 us -> 89.4 us
  blocking collectives: 146 us -> 27.5 us
  local copies, waits for them, and re-layouts: 31.2 us -> 115 us
  between operations: 18.3 us -> 64 us
  matrix products: 75.4 us -> 97.8 us
    ppermute x0 -> x62, starting transfers between devices: none -> 247 us  [the longest x60 247 us: exchange(): return lax.ppermute(blocks, 'dp', pairs)]
    all_to_all x1 -> x0, blocking collectives: 143 us -> none  [local(): lax.all_to_all(outgoing.reshape(D, slot_width), ('dp', 'tensor'), split_a...]
    all_to_all x1 -> x2, waiting for transfers between devices: 138 us -> 0.01 us  [the longest x1 0.01 us: local(): lax.all_to_all(swiglu_send.reshape(swiglu_count, flat_rows, FF), 'tensor'...]
    ppermute x0 -> x62, waiting for transfers between devices: none -> 89.4 us  [the longest x60 74.6 us: exchange(): return lax.ppermute(blocks, 'dp', pairs)]
    unnamed x34 -> x171, local copies, waits for them, and re-layouts: 5.75 us -> 68.2 us
    all_gather x4 -> x0, waiting for transfers between devices: 61.2 us -> none  [the longest x2 31.3 us: local(): lax.all_gather(normed_part, 'tensor', axis=0, tiled=True)]
    reduce_scatter x2 -> x0, waiting for transfers between devices: 37.4 us -> none  [local(): lax.psum_scatter(jnp.einsum('rc,sc->rs', current, current, preferred_elem...]
    unnamed x0 -> x1, blocking collectives: none -> 27.5 us
  transfers between devices with their start and end apart: 7 -> 64, of which waited for: 7 -> 18; matrix products, arithmetic and copies ran while one was open for 1% -> 9% of each run, Pallas kernels for 0% -> 0%
where the time goes in v1:
time: 689 us; the launch traced here: 680 us
  starting transfers between devices  255 us (37%)
  local copies, waits for them, and re-layouts  115 us (17%)
  matrix products  97.8 us (14%)
  waiting for transfers between devices  89.4 us (13%)
  between operations  64 us (9%)
  other arithmetic  31 us (4%)
  blocking collectives  27.5 us (4%)
    ppermute x60, starting transfers between devices, exchange(): return lax.ppermute(blocks, 'dp', pairs)  247 us
    ppermute x60, waiting for transfers between devices, exchange(): return lax.ppermute(blocks, 'dp', pairs)  74.6 us
    unnamed x171, local copies, waits for them, and re-layouts  68.2 us
    dot_general x1, matrix products, local(): product = jnp.dot(polynomial, iterate, preferred_element_type=jnp.float32)  29.4 us
    unnamed x1, blocking collectives  27.5 us
    dot_general x2, matrix products, local(): jnp.einsum('rc,sc->rs', iterate, iterate, preferred_element_type=jnp.floa...  26.2 us
    dot_general x1, matrix products, local(): squared = jnp.dot(normed, normed, preferred_element_type=jnp.float32)  24.6 us
    dot_general x4, matrix products, local(): jnp.dot(polynomial[rows], iterate, preferred_element_type=jnp.float32)  17.6 us
  transfers between devices with their start and end apart: 64, of which 18 were waited for; matrix products, arithmetic and copies ran while one was open for 9% of the time, Pallas kernels for 0%

profile of v1, /device:TPU:12, one launch (start us, length us, event | category | flops | bytes accessed | tf_op | source)
XLA Modules:
  0.0 680.4 jit_solution(14772780266409120196)
XLA Ops:
  0.6 7.3 %add_convert_fusion.3 = (bf16[6,196608]{1,0:T(8,128)(2,1)S(1)}, f32[6,196608]{1,0:T(8,128)}) fusion(f32[6,196608]{1,0:T(8,128)} %param.22, f32[6,196608]{1,0:T(8,128)} %param.23), kind=kLoop, calls=%fused_computation.32 | loop fusion | flops 5898240 | bytes 16515072 | tf_op jit(solution)/shard_map/convert_element_type | solution.py:24
  9.2 7.6 %copy.47 = bf16[6,48,4096]{1,0,2:T(8,128)(2,1)} copy(bf16[6,48,4096]{2,1,0:T(8,128)(2,1)S(1)} %bitcast.229) | data formatting | bytes 4718592 | tf_op jit(solution)/shard_map/reshape | solution.py:107
  16.8 12.6 %reshape.266 = bf16[2,2,294912]{2,1,0:T(2,128)(2,1)} reshape(bf16[4096,6,48]{2,1,0:T(8,128)(2,1)} %bitcast.217) | data formatting | bytes 4718592
  54.4 12.8 %reshape.267 = bf16[4096,6,48]{2,1,0:T(8,128)(2,1)} reshape(bf16[2,2,294912]{2,1,0:T(2,128)(2,1)S(1)} %all-to-all-done) | data formatting | bytes 4718592
  67.2 12.2 %copy.52 = bf16[6,48,2,2048]{3,2,1,0:T(2,128)(2,1)S(1)} copy(bf16[6,48,2,2048]{1,0,3,2:T(8,128)(2,1)} %bitcast.218) | data formatting | bytes 4718592 | tf_op jit(solution)/shard_map/all_to_all | solution.py:106
  172.9 7.8 %collective-permute-start.2 = (bf16[96,768]{1,0:T(8,128)(2,1)S(1)}, bf16[96,768]{1,0:T(8,128)(2,1)S(1)}, u32[]{:S(2)}, u32[]{:S(2)}) collective-permute-start(bf16[96,768]{1,0:T(8,128)(2,1)S(1)} %copy-done.30), channel_id=1, source_target_pairs={{2,4},{4,2},{6,0},{8,14},{10,12},{12,10},{14,8},{16,22},{18,20},{2... | collective-permute-start | bytes 442376 | tf_op jit(solution)/shard_map/ppermute | solution.py:49
  181.6 7.0 %collective-permute-start.3 = (bf16[96,768]{1,0:T(8,128)(2,1)S(1)}, bf16[96,768]{1,0:T(8,128)(2,1)S(1)}, u32[]{:S(2)}, u32[]{:S(2)}) collective-permute-start(bf16[96,768]{1,0:T(8,128)(2,1)S(1)} %copy-done.29), channel_id=1, source_target_pairs={{0,8},{2,10},{4,12},{6,14},{8,0},{10,2},{12,4},{16,24},{18,26},{20... | collective-permute-start | bytes 442376 | tf_op jit(solution)/shard_map/ppermute | solution.py:49
  196.1 7.7 %collective-permute-start.5 = (bf16[96,768]{1,0:T(8,128)(2,1)}, bf16[96,768]{1,0:T(8,128)(2,1)S(1)}, u32[]{:S(2)}, u32[]{:S(2)}) collective-permute-start(bf16[96,768]{1,0:T(8,128)(2,1)} %get-tuple-element.27), channel_id=1, source_target_pairs={{0,12},{2,14},{4,8},{6,10},{8,4},{12,0},{14,2},{16,28},{20,24},{22... | collective-permute-start | bytes 442376 | tf_op jit(solution)/shard_map/ppermute | solution.py:49
  203.9 7.1 %collective-permute-start.6 = (bf16[96,768]{1,0:T(8,128)(2,1)S(1)}, bf16[96,768]{1,0:T(8,128)(2,1)S(1)}, u32[]{:S(2)}, u32[]{:S(2)}) collective-permute-start(bf16[96,768]{1,0:T(8,128)(2,1)S(1)} %copy-done.34), channel_id=1, source_target_pairs={{0,14},{2,12},{4,10},{6,8},{10,4},{12,2},{14,0},{18,28},{20,26},{2... | collective-permute-start | bytes 442376 | tf_op jit(solution)/shard_map/ppermute | solution.py:49
  211.1 7.1 %collective-permute-start.7 = (bf16[96,768]{1,0:T(8,128)(2,1)S(1)}, bf16[96,768]{1,0:T(8,128)(2,1)S(1)}, u32[]{:S(2)}, u32[]{:S(2)}) collective-permute-start(bf16[96,768]{1,0:T(8,128)(2,1)S(1)} %copy-done.33), channel_id=1, source_target_pairs={{0,16},{2,18},{4,20},{6,22},{8,24},{10,26},{12,28},{16,0},{18,2},{... | collective-permute-start | bytes 442376 | tf_op jit(solution)/shard_map/ppermute | solution.py:49
  225.1 7.4 %collective-permute-start.9 = (bf16[96,768]{1,0:T(8,128)(2,1)S(1)}, bf16[96,768]{1,0:T(8,128)(2,1)S(1)}, u32[]{:S(2)}, u32[]{:S(2)}) collective-permute-start(bf16[96,768]{1,0:T(8,128)(2,1)S(1)} %copy-done.31), channel_id=1, source_target_pairs={{0,20},{2,22},{4,16},{6,18},{8,28},{12,24},{14,26},{16,4},{20,0},{... | collective-permute-start | bytes 442376 | tf_op jit(solution)/shard_map/ppermute | solution.py:49
  232.9 7.2 %collective-permute-start.10 = (bf16[96,768]{1,0:T(8,128)(2,1)S(1)}, bf16[96,768]{1,0:T(8,128)(2,1)S(1)}, u32[]{:S(2)}, u32[]{:S(2)}) collective-permute-start(bf16[96,768]{1,0:T(8,128)(2,1)S(1)} %get-tuple-element.33), channel_id=1, source_target_pairs={{0,22},{2,20},{4,18},{6,16},{10,28},{12,26},{14,24},{18,4},{20,2},... | collective-permute-start | bytes 442376 | tf_op jit(solution)/shard_map/ppermute | solution.py:49
  250.1 7.9 %collective-permute-start.12 = (bf16[96,768]{1,0:T(8,128)(2,1)S(1)}, bf16[96,768]{1,0:T(8,128)(2,1)S(1)}, u32[]{:S(2)}, u32[]{:S(2)}) collective-permute-start(bf16[96,768]{1,0:T(8,128)(2,1)S(1)} %get-tuple-element.32), channel_id=1, source_target_pairs={{0,26},{2,24},{6,28},{8,18},{10,16},{12,22},{14,20},{16,10},{18,8}... | collective-permute-start | bytes 442376 | tf_op jit(solution)/shard_map/ppermute | solution.py:49
  294.8 7.3 %collective-permute-done.20 = bf16[96,1280]{1,0:T(8,128)(2,1)S(1)} collective-permute-done((bf16[96,1280]{1,0:T(8,128)(2,1)S(1)}, bf16[96,1280]{1,0:T(8,128)(2,1)S(1)}, u32[]{:S(2)}, u32[]{:S(2)}) %collective-permute-start.20) | collective-permute-done | bytes 245792 | tf_op jit(solution)/shard_map/ppermute | solution.py:49
  324.5 13.1 %collective-permute-done.28 = bf16[96,1280]{1,0:T(8,128)(2,1)S(1)} collective-permute-done((bf16[96,1280]{1,0:T(8,128)(2,1)S(1)}, bf16[96,1280]{1,0:T(8,128)(2,1)S(1)}, u32[]{:S(2)}, u32[]{:S(2)}) %collective-permute-start.28) | collective-permute-done | bytes 245792 | tf_op jit(solution)/shard_map/ppermute | solution.py:49
  337.6 10.0 %fusion.5 = f32[1536,1536]{1,0:T(8,128)S(1)} fusion(bf16[1536,1280]{1,0:T(8,128)(2,1)S(1)} %constant_dynamic-update-slice_fusion.15, bf16[1536,768]{1,0:T(8,128)(2,1)S(1)} %copy-done.38), kind=kOutput, calls=%fused_computation.54 | convolution fusion | flops 9676259328 | bytes 15728640 | tf_op jit(solution)/shard_map/rc,sc->rs/dot_general | solution.py:137
  351.2 14.8 %collective-permute-done.30 = f32[1536,1536]{1,0:T(8,128)} collective-permute-done((f32[1536,1536]{1,0:T(8,128)S(1)}, f32[1536,1536]{1,0:T(8,128)}, u32[]{:S(2)}, u32[]{:S(2)}) %collective-permute-start.30) | collective-permute-done | bytes 9437216 | tf_op jit(solution)/shard_map/ppermute | solution.py:53
  366.0 13.1 %multiply_reduce_fusion = (f32[]{:T(128)}, f32[1536,1536]{1,0:T(8,128)}) fusion(f32[1536,1536]{1,0:T(8,128)} %copy-done.4, f32[1536,1536]{1,0:T(8,128)} %collective-permute-done.30), kind=kLoop, calls=%fused_computation.14 | loop fusion | flops 7077887 | bytes 28311556 | tf_op jit(solution)/shard_map/reduce_sum | solution.py:140
  379.9 29.4 %divide_convert_fusion = bf16[1536,2048]{1,0:T(8,128)(2,1)} fusion(f32[]{:T(128)S(6)} %sqrt.13, f32[1536,1536]{1,0:T(8,128)} %get-tuple-element.15, f32[]{:T(128)S(6)} %add.284, bf16[1536,1280]{1,0:T(8,128)(2,1)} %copy-done.36, bf16[1536,768]{1,0:T(8,128)(2,1)S(1)} %copy-done.38), kind=kOutput, calls=%fused_computation.7 | convolution fusion | flops 16970416128 | bytes 22020104 | tf_op jit(solution)/shard_map/dot_general | solution.py:150
  409.4 16.2 %fusion.81 = f32[1536,1536]{1,0:T(8,128)} fusion(bf16[1536,2048]{1,0:T(8,128)(2,1)} %divide_convert_fusion), kind=kOutput, calls=%fused_computation.238 | convolution fusion | flops 9663676416 | bytes 15728640 | tf_op jit(solution)/shard_map/rc,sc->rs/dot_general | solution.py:137
  431.7 27.5 %all-reduce = f32[16]{0:T(128)S(1)} all-reduce(f32[16]{0:T(128)S(1)} %dynamic-update-slice), channel_id=1, replica_groups=mesh['dp'=16,'tensor'=2] {'dp'}, use_global_device_ids=true, to_apply=%add | all-reduce | flops 16 | bytes 128
  460.5 24.6 %add_convert_fusion = bf16[1536,1536]{1,0:T(8,128)(2,1)} fusion(f32[1536,1536]{1,0:T(8,128)} %fusion.81, f32[1536,1536]{1,0:T(8,128)} %collective-permute-done.31), kind=kOutput, calls=%fused_computation.10 | convolution fusion | flops 7268990976 | bytes 23592960 | tf_op jit(solution)/shard_map/dot_general | solution.py:145
  630.5 16.2 %collective-permute-done.53 = bf16[96,1280]{1,0:T(8,128)(2,1)S(1)} collective-permute-done((bf16[96,1280]{1,0:T(8,128)(2,1)}, bf16[96,1280]{1,0:T(8,128)(2,1)S(1)}, u32[]{:S(2)}, u32[]{:S(2)}) %collective-permute-start.53) | collective-permute-done | bytes 245792 | tf_op jit(solution)/shard_map/ppermute | solution.py:49
  652.3 8.7 %collective-permute-start.60 = (bf16[96,1280]{1,0:T(8,128)(2,1)S(1)}, bf16[96,1280]{1,0:T(8,128)(2,1)S(1)}, u32[]{:S(2)}, u32[]{:S(2)}) collective-permute-start(bf16[96,1280]{1,0:T(8,128)(2,1)S(1)} %get-tuple-element.36), channel_id=1, source_target_pairs={{8,20},{10,22},{12,16},{16,12},{18,14},{20,8},{9,21},{11,23},{13,1... | collective-permute-start | bytes 737288 | tf_op jit(solution)/shard_map/ppermute | solution.py:49
  (345 shorter events, 323.7 us)
Async XLA Ops:
  93.5 189.6 %collective-permute-start.15 = (bf16[96,1280]{1,0:T(8,128)(2,1)}, bf16[96,1280]{1,0:T(8,128)(2,1)}, u32[]{:S(2)}, u32[]{:S(2)}) collective-permute-start(bf16[96,1280]{1,0:T(8,128)(2,1)} %get-tuple-element.79), channel_id=1, source_target_pairs={{8,10},{10,8},{14,12},{16,18},{18,16},{22,20},{9,11},{11,9},{15,13... | collective-permute-start | bytes 737288 | tf_op jit(solution)/shard_map/ppermute | solution.py:49
  95.0 191.7 %collective-permute-start.16 = (bf16[96,1280]{1,0:T(8,128)(2,1)}, bf16[96,1280]{1,0:T(8,128)(2,1)}, u32[]{:S(2)}, u32[]{:S(2)}) collective-permute-start(bf16[96,1280]{1,0:T(8,128)(2,1)} %get-tuple-element.78), channel_id=1, source_target_pairs={{8,12},{12,8},{14,10},{16,20},{20,16},{22,18},{9,13},{13,9},{15,11... | collective-permute-start | bytes 737288 | tf_op jit(solution)/shard_map/ppermute | solution.py:49
  99.6 189.5 %collective-permute-start.17 = (bf16[96,1280]{1,0:T(8,128)(2,1)}, bf16[96,1280]{1,0:T(8,128)(2,1)}, u32[]{:S(2)}, u32[]{:S(2)}) collective-permute-start(bf16[96,1280]{1,0:T(8,128)(2,1)} %get-tuple-element.77), channel_id=1, source_target_pairs={{10,12},{12,10},{14,8},{18,20},{20,18},{22,16},{11,13},{13,11},{15... | collective-permute-start | bytes 737288 | tf_op jit(solution)/shard_map/ppermute | solution.py:49
  139.5 33.3 %collective-permute-start = (bf16[96,768]{1,0:T(8,128)(2,1)}, bf16[96,768]{1,0:T(8,128)(2,1)}, u32[]{:S(2)}, u32[]{:S(2)}) collective-permute-start(bf16[96,768]{1,0:T(8,128)(2,1)} %get-tuple-element.21), channel_id=1, source_target_pairs={{0,2},{2,0},{6,4},{8,10},{10,8},{12,14},{14,12},{16,18},{18,16},{2... | collective-permute-start | bytes 442376 | tf_op jit(solution)/shard_map/ppermute | solution.py:49
  143.6 38.0 %collective-permute-start.1 = (bf16[96,768]{1,0:T(8,128)(2,1)}, bf16[96,768]{1,0:T(8,128)(2,1)}, u32[]{:S(2)}, u32[]{:S(2)}) collective-permute-start(bf16[96,768]{1,0:T(8,128)(2,1)} %get-tuple-element.22), channel_id=1, source_target_pairs={{0,4},{4,0},{6,2},{8,12},{10,14},{12,8},{14,10},{16,20},{18,22},{2... | collective-permute-start | bytes 442376 | tf_op jit(solution)/shard_map/ppermute | solution.py:49
  293.5 27.8 %collective-permute-start.24 = (bf16[96,1280]{1,0:T(8,128)(2,1)S(1)}, bf16[96,1280]{1,0:T(8,128)(2,1)S(1)}, u32[]{:S(2)}, u32[]{:S(2)}) collective-permute-start(bf16[96,1280]{1,0:T(8,128)(2,1)S(1)} %copy-done.17), channel_id=1, source_target_pairs={{0,20},{4,16},{6,18},{24,12},{28,8},{30,10},{1,21},{5,17},{7,19},{... | collective-permute-start | bytes 737288 | tf_op jit(solution)/shard_map/ppermute | solution.py:49
  309.6 28.0 %collective-permute-start.28 = (bf16[96,1280]{1,0:T(8,128)(2,1)S(1)}, bf16[96,1280]{1,0:T(8,128)(2,1)S(1)}, u32[]{:S(2)}, u32[]{:S(2)}) collective-permute-start(bf16[96,1280]{1,0:T(8,128)(2,1)S(1)} %copy-done.13), channel_id=1, source_target_pairs={{8,20},{12,16},{14,18},{16,12},{20,8},{22,10},{9,21},{13,17},{15,1... | collective-permute-start | bytes 737288 | tf_op jit(solution)/shard_map/ppermute | solution.py:49
  425.6 34.9 %collective-permute-start.31 = (f32[1536,1536]{1,0:T(8,128)}, f32[1536,1536]{1,0:T(8,128)}, u32[]{:S(2)}, u32[]{:S(2)}) collective-permute-start(f32[1536,1536]{1,0:T(8,128)} %fusion.81), channel_id=1, source_target_pairs={{0,1},{1,0},{2,3},{3,2},{4,5},{5,4},{6,7},{7,6},{8,9},{9,8},{10,11... | collective-permute-start | bytes 28311560 | tf_op jit(solution)/shard_map/ppermute | solution.py:53
  511.5 27.6 %collective-permute-start.33 = (bf16[96,768]{1,0:T(8,128)(2,1)S(1)}, bf16[96,768]{1,0:T(8,128)(2,1)S(1)}, u32[]{:S(2)}, u32[]{:S(2)}) collective-permute-start(bf16[96,768]{1,0:T(8,128)(2,1)S(1)} %get-tuple-element.63), channel_id=1, source_target_pairs={{0,4},{2,6},{4,0},{8,12},{10,14},{12,8},{14,10},{16,20},{18,22},{2... | collective-permute-start | bytes 442376 | tf_op jit(solution)/shard_map/ppermute | solution.py:49
  514.9 30.6 %collective-permute-start.34 = (bf16[96,768]{1,0:T(8,128)(2,1)S(1)}, bf16[96,768]{1,0:T(8,128)(2,1)S(1)}, u32[]{:S(2)}, u32[]{:S(2)}) collective-permute-start(bf16[96,768]{1,0:T(8,128)(2,1)S(1)} %get-tuple-element.62), channel_id=1, source_target_pairs={{0,6},{2,4},{4,2},{8,14},{10,12},{12,10},{14,8},{16,22},{18,20},{2... | collective-permute-start | bytes 442376 | tf_op jit(solution)/shard_map/ppermute | solution.py:49
  520.0 31.9 %collective-permute-start.35 = (bf16[96,768]{1,0:T(8,128)(2,1)S(1)}, bf16[96,768]{1,0:T(8,128)(2,1)S(1)}, u32[]{:S(2)}, u32[]{:S(2)}) collective-permute-start(bf16[96,768]{1,0:T(8,128)(2,1)S(1)} %get-tuple-element.61), channel_id=1, source_target_pairs={{0,8},{2,10},{4,12},{8,0},{10,2},{12,4},{14,6},{16,24},{18,26},{20... | collective-permute-start | bytes 442376 | tf_op jit(solution)/shard_map/ppermute | solution.py:49
  526.3 32.0 %collective-permute-start.36 = (bf16[96,768]{1,0:T(8,128)(2,1)S(1)}, bf16[96,768]{1,0:T(8,128)(2,1)S(1)}, u32[]{:S(2)}, u32[]{:S(2)}) collective-permute-start(bf16[96,768]{1,0:T(8,128)(2,1)S(1)} %get-tuple-element.60), channel_id=1, source_target_pairs={{0,10},{2,8},{4,14},{8,2},{10,0},{12,6},{14,4},{16,26},{18,24},{20... | collective-permute-start | bytes 442376 | tf_op jit(solution)/shard_map/ppermute | solution.py:49
  532.7 32.0 %collective-permute-start.37 = (bf16[96,768]{1,0:T(8,128)(2,1)S(1)}, bf16[96,768]{1,0:T(8,128)(2,1)S(1)}, u32[]{:S(2)}, u32[]{:S(2)}) collective-permute-start(bf16[96,768]{1,0:T(8,128)(2,1)S(1)} %get-tuple-element.59), channel_id=1, source_target_pairs={{0,12},{2,14},{4,8},{8,4},{10,6},{12,0},{14,2},{16,28},{18,30},{20... | collective-permute-start | bytes 442376 | tf_op jit(solution)/shard_map/ppermute | solution.py:49
  539.1 32.0 %collective-permute-start.38 = (bf16[96,768]{1,0:T(8,128)(2,1)S(1)}, bf16[96,768]{1,0:T(8,128)(2,1)S(1)}, u32[]{:S(2)}, u32[]{:S(2)}) collective-permute-start(bf16[96,768]{1,0:T(8,128)(2,1)S(1)} %get-tuple-element.58), channel_id=1, source_target_pairs={{0,14},{2,12},{4,10},{8,6},{10,4},{12,2},{14,0},{16,30},{18,28},{2... | collective-permute-start | bytes 442376 | tf_op jit(solution)/shard_map/ppermute | solution.py:49
  545.5 29.0 %collective-permute-start.39 = (bf16[96,768]{1,0:T(8,128)(2,1)S(1)}, bf16[96,768]{1,0:T(8,128)(2,1)S(1)}, u32[]{:S(2)}, u32[]{:S(2)}) collective-permute-start(bf16[96,768]{1,0:T(8,128)(2,1)S(1)} %get-tuple-element.57), channel_id=1, source_target_pairs={{0,16},{2,18},{4,20},{8,24},{10,26},{12,28},{14,30},{16,0},{18,2},... | collective-permute-start | bytes 442376 | tf_op jit(solution)/shard_map/ppermute | solution.py:49
  551.9 27.8 %collective-permute-start.40 = (bf16[96,768]{1,0:T(8,128)(2,1)S(1)}, bf16[96,768]{1,0:T(8,128)(2,1)S(1)}, u32[]{:S(2)}, u32[]{:S(2)}) collective-permute-start(bf16[96,768]{1,0:T(8,128)(2,1)S(1)} %get-tuple-element.56), channel_id=1, source_target_pairs={{0,18},{2,16},{4,22},{8,26},{10,24},{12,30},{14,28},{16,2},{18,0},... | collective-permute-start | bytes 442376 | tf_op jit(solution)/shard_map/ppermute | solution.py:49
  558.3 28.0 %collective-permute-start.41 = (bf16[96,768]{1,0:T(8,128)(2,1)S(1)}, bf16[96,768]{1,0:T(8,128)(2,1)S(1)}, u32[]{:S(2)}, u32[]{:S(2)}) collective-permute-start(bf16[96,768]{1,0:T(8,128)(2,1)S(1)} %get-tuple-element.55), channel_id=1, source_target_pairs={{0,20},{2,22},{4,16},{8,28},{10,30},{12,24},{14,26},{16,4},{18,6},... | collective-permute-start | bytes 442376 | tf_op jit(solution)/shard_map/ppermute | solution.py:49
  564.7 28.0 %collective-permute-start.42 = (bf16[96,768]{1,0:T(8,128)(2,1)S(1)}, bf16[96,768]{1,0:T(8,128)(2,1)S(1)}, u32[]{:S(2)}, u32[]{:S(2)}) collective-permute-start(bf16[96,768]{1,0:T(8,128)(2,1)S(1)} %get-tuple-element.54), channel_id=1, source_target_pairs={{0,22},{2,20},{4,18},{8,30},{10,28},{12,26},{14,24},{16,6},{18,4},... | collective-permute-start | bytes 442376 | tf_op jit(solution)/shard_map/ppermute | solution.py:49
  571.1 25.7 %collective-permute-start.43 = (bf16[96,768]{1,0:T(8,128)(2,1)S(1)}, bf16[96,768]{1,0:T(8,128)(2,1)S(1)}, u32[]{:S(2)}, u32[]{:S(2)}) collective-permute-start(bf16[96,768]{1,0:T(8,128)(2,1)S(1)} %get-tuple-element.53), channel_id=1, source_target_pairs={{0,24},{2,26},{4,28},{8,16},{10,18},{12,20},{14,22},{16,8},{18,10}... | collective-permute-start | bytes 442376 | tf_op jit(solution)/shard_map/ppermute | solution.py:49
  616.6 30.1 %collective-permute-start.53 = (bf16[96,1280]{1,0:T(8,128)(2,1)}, bf16[96,1280]{1,0:T(8,128)(2,1)S(1)}, u32[]{:S(2)}, u32[]{:S(2)}) collective-permute-start(bf16[96,1280]{1,0:T(8,128)(2,1)} %get-tuple-element.43), channel_id=1, source_target_pairs={{8,6},{10,4},{12,2},{16,30},{18,28},{20,26},{9,7},{11,5},{13,3},{1... | collective-permute-start | bytes 737288 | tf_op jit(solution)/shard_map/ppermute | solution.py:49
  619.5 30.8 %collective-permute-start.54 = (bf16[96,1280]{1,0:T(8,128)(2,1)}, bf16[96,1280]{1,0:T(8,128)(2,1)S(1)}, u32[]{:S(2)}, u32[]{:S(2)}) collective-permute-start(bf16[96,1280]{1,0:T(8,128)(2,1)} %get-tuple-element.42), channel_id=1, source_target_pairs={{8,24},{10,26},{12,28},{16,0},{18,2},{20,4},{9,25},{11,27},{13,29}... | collective-permute-start | bytes 737288 | tf_op jit(solution)/shard_map/ppermute | solution.py:49
  622.5 29.8 %collective-permute-start.55 = (bf16[96,1280]{1,0:T(8,128)(2,1)S(1)}, bf16[96,1280]{1,0:T(8,128)(2,1)S(1)}, u32[]{:S(2)}, u32[]{:S(2)}) collective-permute-start(bf16[96,1280]{1,0:T(8,128)(2,1)S(1)} %copy-done.26), channel_id=1, source_target_pairs={{8,26},{10,24},{12,30},{16,2},{18,0},{20,6},{9,27},{11,25},{13,31}... | collective-permute-start | bytes 737288 | tf_op jit(solution)/shard_map/ppermute | solution.py:49
  625.5 36.3 %collective-permute-start.56 = (bf16[96,1280]{1,0:T(8,128)(2,1)S(1)}, bf16[96,1280]{1,0:T(8,128)(2,1)S(1)}, u32[]{:S(2)}, u32[]{:S(2)}) collective-permute-start(bf16[96,1280]{1,0:T(8,128)(2,1)S(1)} %copy-done.25), channel_id=1, source_target_pairs={{8,28},{10,30},{12,24},{16,4},{18,6},{20,0},{9,29},{11,31},{13,25}... | collective-permute-start | bytes 737288 | tf_op jit(solution)/shard_map/ppermute | solution.py:49
  628.5 35.9 %collective-permute-start.57 = (bf16[96,1280]{1,0:T(8,128)(2,1)S(1)}, bf16[96,1280]{1,0:T(8,128)(2,1)S(1)}, u32[]{:S(2)}, u32[]{:S(2)}) collective-permute-start(bf16[96,1280]{1,0:T(8,128)(2,1)S(1)} %get-tuple-element.39), channel_id=1, source_target_pairs={{8,30},{10,28},{12,26},{16,6},{18,4},{20,2},{9,31},{11,29},{13,27}... | collective-permute-start | bytes 737288 | tf_op jit(solution)/shard_map/ppermute | solution.py:49
  (92 other events, 2888.2 us)

commit v2 on v1

v2 whole, which is shorter than its diff:
```python
import math

import jax
import jax.numpy as jnp
import numpy as np
from jax import lax
from jax.experimental import pallas as pl
from jax.experimental.pallas import tpu as pltpu
from jax.sharding import PartitionSpec as P

D = 1536
FF = 4096
NS_STEPS = 2


QUINTIC_LINEAR = 3.4445
QUINTIC_CUBIC = -4.775
QUINTIC_FIFTH = 2.0315
MOMENTUM = 0.95
BIAS_FIRST = 1.0 - 0.9**10
BIAS_SECOND = 1.0 - 0.95**10


def momentum_terms(gradient, state):
    state_next = MOMENTUM * state + gradient
    return (state_next, (gradient + MOMENTUM * state_next).astype(jnp.bfloat16))


def adamw_terms(values, gradient, first, second):
    first_next = 0.9 * first + 0.1 * gradient
    second_next = 0.95 * second + 0.05 * gradient * gradient
    direction = (
        first_next / BIAS_FIRST / (jnp.sqrt(second_next / BIAS_SECOND) + 1e-08) + 0.1 * values
    )
    return (direction, first_next, second_next)


LANE = 128
GRANULE = 256


class Plan:
    def __init__(self, chips, cores, square_count, swiglu_count):
        planes = 4
        per = chips // planes
        side = max(1, int(round(math.sqrt(per))))

        def coords(i):
            return (i % side, (i // side) % max(1, per // side), i // per)

        def hops(a, b):
            return sum(abs(p - q) for p, q in zip(coords(a), coords(b)))

        low = [i for i in range(chips) if coords(i)[2] < planes // 2]
        low.sort(key=lambda i: (-(sum(coords(i)) % 2), -coords(i)[2], i))
        high = [i for i in range(chips) if coords(i)[2] >= planes // 2]
        high.sort(key=lambda i: (-(sum(coords(i)) % 2), coords(i)[2], i))
        order = [c for pair in zip(low, high) for c in pair]
        self.heavy = order[:swiglu_count]
        rest = order[swiglu_count:]
        self.light = rest[:square_count]
        helpers = rest
        narrow = D // cores
        wide = FF // cores
        self.granules = (wide - narrow) // GRANULE
        self.passes = self.granules - 2
        count = len(helpers)
        take = [
            [helpers[(k + p * swiglu_count) % count] for k in range(swiglu_count)]
            for p in range(self.passes)
        ]
        cost = lambda p, k, h: hops(h, self.heavy[k]) ** 2
        better = True
        while better:
            better = False
            places = [(p, k) for p in range(self.passes) for k in range(swiglu_count)]
            for p, k in places:
                for h in helpers:
                    used = sum(row.count(h) for row in take)
                    if used < 2 and h not in take[p] and cost(p, k, h) < cost(p, k, take[p][k]):
                        take[p][k] = h
                        better = True
                for q, m in places:
                    a, b = take[p][k], take[q][m]
                    if a == b or (q != p and (b in take[p] or a in take[q])):
                        continue
                    if cost(p, k, b) + cost(q, m, a) < cost(p, k, a) + cost(q, m, b):
                        take[p][k], take[q][m] = b, a
                        better = True
        self.take = take
        self.held = {o: [(j, 0), (j, 1)] for j, o in enumerate(self.heavy)}
        self.place = {}
        for p in range(self.passes):
            for k in range(swiglu_count):
                h = take[p][k]
                self.held.setdefault(h, []).append((k, 2 + p))
        for chip, list_of in self.held.items():
            for where, item in enumerate(list_of):
                self.place[item] = (chip, where)
        self.is_heavy = np.array([c in self.heavy for c in range(chips)])
        self.slot_in_pass = np.zeros((max(1, self.passes), chips), np.bool_)
        for p in range(self.passes):
            for k in range(swiglu_count):
                self.slot_in_pass[p, take[p][k]] = self.place[(k, 2 + p)][1] == 1
        self.idle = [c for c in range(chips) if c not in self.heavy and c not in self.light]


def prepare_kernel(plan, cores, sg, ss, wg, ws, sn, wn, first, second):
    narrow_tiles = D // cores // LANE
    wide_tiles = FF // cores // LANE
    square_next = MOMENTUM * ss[...] + sg[...]
    sn[...] = square_next
    swiglu_next = MOMENTUM * ws[...] + wg[...]
    wn[...] = swiglu_next

    def piece(grad, state, row_tile, slot):
        g = grad[:, row_tile, slot, :]
        return (g + MOMENTUM * (MOMENTUM * state[:, row_tile, slot, :] + g)).astype(jnp.bfloat16)

    for j, owner in enumerate(plan.heavy):
        for core in range(cores):
            for t in range(wide_tiles):
                value = piece(wg, ws, core * wide_tiles + t, j)
                if t < narrow_tiles:
                    first[owner * cores + core, :, t * LANE : (t + 1) * LANE] = value
                else:
                    b, part = divmod(t - narrow_tiles, GRANULE // LANE)
                    chip, where = plan.place[(j, b)]
                    at = where * GRANULE + part * LANE
                    second[chip * cores + core, :, at : at + LANE] = value
    for j, owner in enumerate(plan.light):
        for core in range(cores):
            for t in range(narrow_tiles):
                value = piece(sg, ss, core * narrow_tiles + t, j)
                first[owner * cores + core, :, t * LANE : (t + 1) * LANE] = value
    for chip in range(len(plan.is_heavy)):
        for core in range(cores):
            if chip in plan.idle:
                first[chip * cores + core] = jnp.zeros(first.shape[1:], first.dtype)
            for where in range(len(plan.held.get(chip, [])), 2):
                second[chip * cores + core, :, where * GRANULE : (where + 1) * GRANULE] = jnp.zeros(
                    (first.shape[1], GRANULE), first.dtype
                )


def prepare(plan, chips, cores, square_grad, square_state, swiglu_grad, swiglu_state):
    rows = D // (chips * cores)
    chunk = 16 if rows % 16 == 0 else rows
    square_count, swiglu_count = square_grad.shape[0], swiglu_grad.shape[0]

    def tiles(x, width):
        count = x.shape[0]
        return x.reshape(count, rows, width // LANE, LANE).transpose(1, 2, 0, 3)

    def flat(x, width):
        return x.transpose(2, 0, 1, 3).reshape(x.shape[2], rows * width)

    narrow = D // cores
    square_block = pl.BlockSpec((chunk, D // LANE, square_count, LANE), lambda i: (i, 0, 0, 0))
    swiglu_block = pl.BlockSpec((chunk, FF // LANE, swiglu_count, LANE), lambda i: (i, 0, 0, 0))
    devices = chips * cores
    out = pl.pallas_call(
        lambda *refs: prepare_kernel(plan, cores, *refs),
        grid=(rows // chunk,),
        in_specs=[square_block, square_block, swiglu_block, swiglu_block],
        out_specs=[
            square_block,
            swiglu_block,
            pl.BlockSpec((devices, chunk, narrow), lambda i: (0, i, 0)),
            pl.BlockSpec((devices, chunk, 2 * GRANULE), lambda i: (0, i, 0)),
        ],
        out_shape=[
            jax.ShapeDtypeStruct((rows, D // LANE, square_count, LANE), jnp.float32),
            jax.ShapeDtypeStruct((rows, FF // LANE, swiglu_count, LANE), jnp.float32),
            jax.ShapeDtypeStruct((devices, rows, narrow), jnp.bfloat16),
            jax.ShapeDtypeStruct((devices, rows, 2 * GRANULE), jnp.bfloat16),
        ],
        compiler_params=pltpu.CompilerParams(vmem_limit_bytes=56 * 1024 * 1024),
        name="prepare",
    )(tiles(square_grad, D), tiles(square_state, D), tiles(swiglu_grad, FF), tiles(swiglu_state, FF))
    return flat(out[0], D), flat(out[1], FF), out[2], out[3]


def other_core(x):
    return lax.ppermute(x, "tensor", [(0, 1), (1, 0)])


def inverse_of(order):
    count = order.shape[0]
    match = order[None, :] == jnp.arange(count, dtype=jnp.int32)[:, None]
    return jnp.sum(jnp.where(match, jnp.arange(count, dtype=jnp.int32)[None, :], 0), axis=1)


def local(
    square_grad,
    square_state,
    swiglu_grad,
    swiglu_state,
    square_order,
    swiglu_order,
    owners,
    vector_values,
    vector_grad,
    vector_first,
    vector_second,
    embed_values,
    embed_grad,
    embed_first,
    embed_second,
    embed_ranges,
):
    chips = lax.axis_size("dp")
    cores = lax.axis_size("tensor")
    chip = lax.axis_index("dp")
    square_count = square_grad.shape[0]
    swiglu_count = swiglu_grad.shape[0]
    chip_rows = D // chips
    narrow = D // cores
    plan = Plan(chips, cores, square_count, swiglu_count)

    square_next, swiglu_next, first_send, second_send = prepare(
        plan, chips, cores, square_grad, square_state, swiglu_grad, swiglu_state
    )
    both = ("dp", "tensor")
    second_got = lax.all_to_all(
        second_send.reshape(D, 2 * GRANULE), both, split_axis=0, concat_axis=0, tiled=True
    )
    first_got = lax.all_to_all(
        first_send.reshape(D, narrow), both, split_axis=0, concat_axis=0, tiled=True
    )
    heavy_here = jnp.asarray(plan.is_heavy)[chip]
    pieces = [second_got[:, :GRANULE], second_got[:, GRANULE:]]
    relayed = []
    for p in range(plan.passes):
        pick = jnp.asarray(plan.slot_in_pass[p])[chip]
        pairs = [(plan.take[p][k], plan.heavy[k]) for k in range(swiglu_count)]
        relayed.append(lax.ppermute(jnp.where(pick, pieces[1], pieces[0]), "dp", pairs))
    kept = jnp.where(heavy_here, second_got, jnp.zeros((), jnp.bfloat16))
    matrix = jnp.concatenate([first_got, kept] + relayed, axis=1)

    factor = jnp.where(heavy_here, jnp.float32(math.sqrt(FF)), jnp.float32(math.sqrt(D)))
    iterate = matrix
    first_scale = jnp.float32(1.0)
    for round_index in range(NS_STEPS):
        gram_part = jnp.einsum("rc,sc->rs", iterate, iterate, preferred_element_type=jnp.float32)
        gram = gram_part + other_core(gram_part)
        if round_index == 0:
            gram_scale = jnp.sqrt(jnp.sum(gram * gram)) + 1e-06
            first_scale = gram_scale
        else:
            gram_scale = jnp.float32(1.0)
        normed = (gram / gram_scale).astype(jnp.bfloat16)
        squared = jnp.dot(normed, normed, preferred_element_type=jnp.float32)
        polynomial = (
            QUINTIC_CUBIC * normed.astype(jnp.float32) + QUINTIC_FIFTH * squared
        ).astype(jnp.bfloat16)
        if round_index < NS_STEPS - 1:
            product = jnp.dot(polynomial, iterate, preferred_element_type=jnp.float32)
            mixed = (QUINTIC_LINEAR * iterate.astype(jnp.float32) + product) / jnp.sqrt(gram_scale)
            iterate = mixed.astype(jnp.bfloat16)

    def finish(columns):
        part = iterate[:, columns]
        product = jnp.dot(polynomial, part, preferred_element_type=jnp.float32)
        return (factor * (QUINTIC_LINEAR * part.astype(jnp.float32) + product)).astype(jnp.bfloat16)

    def send_back(x):
        return lax.all_to_all(
            x.reshape(chips, chip_rows, -1), "dp", split_axis=0, concat_axis=0, tiled=True
        )

    first_back = send_back(finish(slice(0, narrow)))
    rest = finish(slice(narrow, None))
    handed = []
    for p in range(plan.passes):
        pairs = [(plan.heavy[k], plan.take[p][k]) for k in range(swiglu_count)]
        at = (2 + p) * GRANULE
        handed.append(lax.ppermute(rest[:, at : at + GRANULE], "dp", pairs))
    halves = []
    for where in range(2):
        value = rest[:, where * GRANULE : (where + 1) * GRANULE]
        for p in range(plan.passes):
            mine = np.zeros((chips,), np.bool_)
            for k in range(swiglu_count):
                if plan.place[(k, 2 + p)][1] == where:
                    mine[plan.take[p][k]] = True
            value = jnp.where(jnp.asarray(mine)[chip], handed[p], value)
        halves.append(value)
    second_back = send_back(jnp.concatenate(halves, axis=1))

    slot_of_square = inverse_of(square_order)
    slot_of_swiglu = inverse_of(swiglu_order)
    chip_of_square = jnp.asarray(np.array(plan.light, np.int32))[slot_of_square]
    chip_of_swiglu = jnp.asarray(np.array(plan.heavy, np.int32))[slot_of_swiglu]
    square_update = first_back[chip_of_square]
    parts = [first_back[np.array(plan.heavy, np.int32)]]
    for b in range(plan.granules):
        parts.append(
            jnp.stack(
                [
                    second_back[plan.place[(j, b)][0], :, plan.place[(j, b)][1] * GRANULE :][:, :GRANULE]
                    for j in range(swiglu_count)
                ]
            )
        )
    swiglu_update = jnp.concatenate(parts, axis=2)[slot_of_swiglu]

    logs = lax.all_gather(0.5 * jnp.log(first_scale), "dp")
    matrix_chip = jnp.concatenate([chip_of_square, chip_of_swiglu])
    owner_norms = jnp.sum(jnp.where(owners == chip, logs[matrix_chip], 0.0)).reshape(1)

    vector_step, first_vector, second_vector = adamw_terms(
        vector_values, vector_grad, vector_first, vector_second
    )
    embed_rows = embed_values.shape[0]
    row_numbers = chip * embed_rows + jnp.arange(embed_rows, dtype=jnp.int32)
    inside = (row_numbers[:, None] >= embed_ranges[None, :, 0]) & (
        row_numbers[:, None] < embed_ranges[None, :, 1]
    )
    row_live = jnp.sum(inside.astype(jnp.int32), axis=1) > 0
    direction, first_next, second_next = adamw_terms(
        embed_values, embed_grad, embed_first, embed_second
    )
    embed_step = jnp.where(row_live[:, None], direction, 0.0)
    first_embed = jnp.where(row_live[:, None], first_next, embed_first)
    second_embed = jnp.where(row_live[:, None], second_next, embed_second)
    return (
        square_next,
        swiglu_next,
        square_update,
        swiglu_update,
        owner_norms,
        vector_step,
        first_vector,
        second_vector,
        embed_step,
        first_embed,
        second_embed,
    )


def solution(mesh):
    flat = P(None, ("dp", "tensor"))
    vector = P(("dp", "tensor"))
    tile = P("dp", "tensor")
    update = P(None, "dp", "tensor")
    return jax.shard_map(
        local,
        mesh=mesh,
        in_specs=(flat,) * 4 + (P(),) * 3 + (vector,) * 4 + (tile,) * 4 + (P(),),
        out_specs=(flat, flat, update, update, P("dp")) + (vector,) * 3 + (tile,) * 3,
        check_vma=False,
    )
```

time: 689 us -> 478 us (0.69)
  starting transfers between devices: 255 us -> 39.4 us
  blocking collectives: 27.5 us -> 113 us
  local copies, waits for them, and re-layouts: 115 us -> 47.7 us
  between operations: 64 us -> 2.99 us
  waiting for transfers between devices: 89.4 us -> 122 us
  Pallas kernels: 0 us -> 20.7 us
  other arithmetic: 31 us -> 24.1 us
    ppermute x60 -> x6, starting transfers between devices: 247 us -> 9.48 us  [the longest x3 6.18 us: local(): lax.ppermute(jnp.where(pick, pieces[1], pieces[0]), 'dp', pairs)]
    all_to_all x2 -> x3, waiting for transfers between devices: 0.01 us -> 69.2 us  [the longest x1 41.3 us: local(): lax.all_to_all(first_send.reshape(D, narrow), both, split_axis=0, concat_...]
    ppermute x60 -> x6, waiting for transfers between devices: 74.6 us -> 24.2 us  [the longest x3 24.2 us: local(): handed.append(lax.ppermute(rest[:, at:at + GRANULE], 'dp', pairs))]
    all_to_all x0 -> x1, blocking collectives: none -> 42.9 us  [local(): lax.all_to_all(second_send.reshape(D, 2 * GRANULE), both, split_axis=0, c...]
    unnamed x1, blocking collectives: 27.5 us -> 69.8 us
    unnamed x171 -> x80, local copies, waits for them, and re-layouts: 68.2 us -> 31.6 us
    all_to_all x2 -> x3, starting transfers between devices: 8.24 us -> 29.8 us  [the longest x2 25.1 us: send_back(): lax.all_to_all(x.reshape(chips, chip_rows, -1), 'dp', split_axis=0, conca...]
    pallas_call x0 -> x1, Pallas kernels: none -> 20.7 us  [prepare(): pl.pallas_call(lambda *refs: prepare_kernel(plan, cores, *refs), grid=(ro...]
  transfers between devices with their start and end apart: 64 -> 11, of which waited for: 18 -> 6; matrix products, arithmetic and copies ran while one was open for 9% -> 6% of each run, Pallas kernels for 0% -> 0%
where the time goes in v2:
time: 478 us; the launch traced here: 470 us
  waiting for transfers between devices  122 us (26%)
  blocking collectives  113 us (24%)
  matrix products  100 us (21%)
  local copies, waits for them, and re-layouts  47.7 us (10%)
  starting transfers between devices  39.4 us (8%)
  other arithmetic  24.1 us (5%)
  Pallas kernels  20.7 us (4%)
    unnamed x1, blocking collectives  69.8 us
    all_to_all x1, blocking collectives, local(): lax.all_to_all(second_send.reshape(D, 2 * GRANULE), both, split_axis=0, c...  42.9 us
    all_to_all x1, waiting for transfers between devices, local(): lax.all_to_all(first_send.reshape(D, narrow), both, split_axis=0, concat_...  41.3 us
    unnamed x80, local copies, waits for them, and re-layouts  31.6 us
    dot_general x1, matrix products, local(): product = jnp.dot(polynomial, iterate, preferred_element_type=jnp.float32)  30.1 us
    ppermute x2, waiting for transfers between devices, other_core(): return lax.ppermute(x, 'tensor', [(0, 1), (1, 0)])  29 us
    all_to_all x2, waiting for transfers between devices, send_back(): lax.all_to_all(x.reshape(chips, chip_rows, -1), 'dp', split_axis=0, conca...  27.9 us
    dot_general x2, matrix products, local(): jnp.einsum('rc,sc->rs', iterate, iterate, preferred_element_type=jnp.floa...  26.4 us
  transfers between devices with their start and end apart: 11, of which 6 were waited for; matrix products, arithmetic and copies ran while one was open for 6% of the time, Pallas kernels for 0%

profile of v2, /device:TPU:12, one launch (start us, length us, event | category | flops | bytes accessed | tf_op | source)
XLA Modules:
  0.0 470.1 jit_solution(9418907204858578202)
XLA Ops:
  0.6 20.7 %prepare.1 = (f32[48,12,8,128]{3,2,1,0:T(8,128)}, f32[48,32,6,128]{3,2,1,0:T(8,128)}, bf16[32,48,768]{2,1,0:T(8,128)(2,1)}, bf16[32,48,512]{2,1,0:T(8,128)(2,1)}) custom-call(f32[48,12,8,128]{3,2,1,0:T(8,128)} %bitcast.157, f32[48,12,8,128]{3,2,1,0:T(8,128)} %bitcast.158, f32[48,32,6,128]{3,2,1,0:T(8,128)} %bitcast.154, f32[48,32,6,128]{3,2,1,0:T(8,128)} %bitcast.155), custom_call_target="tpu_custom_call" | custom-call | tf_op jit(solution)/shard_map/prepare/pallas_call | solution.py:162
  21.3 42.9 %all_to_all.28 = bf16[32,48,512]{2,1,0:T(8,128)(2,1)S(1)} all-to-all(bf16[32,48,512]{2,1,0:T(8,128)(2,1)} %get-tuple-element.18), channel_id=1, replica_groups=mesh['dp'=16,'tensor'=2] {'dp','tensor'}, dimensions={0} | all-to-all | bytes 3145728 | tf_op jit(solution)/shard_map/all_to_all | solution.py:225
  64.2 4.7 all-to-all-start
  70.7 2.9 broadcast_select_fusion
  73.5 3.3 collective-permute-start
  79.7 41.3 %all-to-all-done = bf16[32,48,768]{2,1,0:T(8,128)(2,1)} async-done(((bf16[32,48,768]{2,1,0:T(8,128)(2,1)}), bf16[32,48,768]{2,1,0:T(8,128)(2,1)}, u32[]{:S(2)}, u32[]{:S(2)}) %all-to-all-start) | async-done | bytes 2359328 | tf_op jit(solution)/shard_map/all_to_all | solution.py:228
  125.5 10.1 %fusion.25 = f32[1536,1536]{1,0:T(8,128)S(1)} fusion(bf16[1536,2048]{1,0:T(8,128)(2,1)S(1)} %constant_dynamic-update-slice_fusion), kind=kOutput, calls=%fused_computation.135 | convolution fusion | flops 9663676416 | bytes 15728640 | tf_op jit(solution)/shard_map/rc,sc->rs/dot_general | solution.py:245
  135.6 3.6 copy-done.2
  139.2 14.8 %collective-permute-done.3 = f32[1536,1536]{1,0:T(8,128)} collective-permute-done((f32[1536,1536]{1,0:T(8,128)S(1)}, f32[1536,1536]{1,0:T(8,128)}, u32[]{:S(2)}, u32[]{:S(2)}) %collective-permute-start.3) | collective-permute-done | bytes 9437216 | tf_op jit(solution)/shard_map/ppermute | solution.py:185
  154.0 13.1 %multiply_reduce_fusion = (f32[]{:T(128)}, f32[1536,1536]{1,0:T(8,128)}) fusion(f32[1536,1536]{1,0:T(8,128)} %copy-done.2, f32[1536,1536]{1,0:T(8,128)} %collective-permute-done.3), kind=kLoop, calls=%fused_computation.13 | loop fusion | flops 7077887 | bytes 28311556 | tf_op jit(solution)/shard_map/reduce_sum | solution.py:248
  167.8 30.1 %divide_convert_fusion = bf16[1536,2048]{1,0:T(8,128)(2,1)} fusion(bf16[1536,2048]{1,0:T(8,128)(2,1)} %copy-done.3, f32[]{:T(128)S(6)} %sqrt.13, f32[1536,1536]{1,0:T(8,128)} %get-tuple-element.23, f32[]{:T(128)S(6)} %add.122), kind=kOutput, calls=%fused_computation.6 | convolution fusion | flops 16948396032 | bytes 22020104 | tf_op jit(solution)/shard_map/dot_general | solution.py:258
  197.9 16.3 %fusion.26 = f32[1536,1536]{1,0:T(8,128)} fusion(bf16[1536,2048]{1,0:T(8,128)(2,1)} %divide_convert_fusion), kind=kOutput, calls=%fused_computation.136 | convolution fusion | flops 9663676416 | bytes 15728640 | tf_op jit(solution)/shard_map/rc,sc->rs/dot_general | solution.py:245
  215.0 14.2 %collective-permute-done.4 = f32[1536,1536]{1,0:T(8,128)} collective-permute-done((f32[1536,1536]{1,0:T(8,128)}, f32[1536,1536]{1,0:T(8,128)}, u32[]{:S(2)}, u32[]{:S(2)}) %collective-permute-start.4) | collective-permute-done | bytes 9437216 | tf_op jit(solution)/shard_map/ppermute | solution.py:185
  229.2 24.3 %add_convert_fusion = bf16[1536,1536]{1,0:T(8,128)(2,1)} fusion(f32[1536,1536]{1,0:T(8,128)} %fusion.26, f32[1536,1536]{1,0:T(8,128)} %collective-permute-done.4), kind=kOutput, calls=%fused_computation.9 | convolution fusion | flops 7268990976 | bytes 23592960 | tf_op jit(solution)/shard_map/dot_general | solution.py:253
  253.5 10.3 %multiply_convert_fusion = bf16[1536,1280]{1,0:T(8,128)(2,1)S(1)} fusion(f32[]{:T(128)S(6)} %select_n.148, bf16[1536,2048]{1,0:T(8,128)(2,1)} %divide_convert_fusion, bf16[1536,1536]{1,0:T(8,128)(2,1)} %add_convert_fusion), kind=kOutput, calls=%fused_computation.14 | convolution fusion | flops 6049628160 | bytes 16515076 | tf_op jit(solution)/shard_map/dot_general | solution.py:264
  268.5 19.7 %collective-permute-done.7 = bf16[1536,256]{1,0:T(8,128)(2,1)S(1)} collective-permute-done((bf16[1536,256]{1,0:T(8,128)(2,1)S(1)}, bf16[1536,256]{1,0:T(8,128)(2,1)S(1)}, u32[]{:S(2)}, u32[]{:S(2)}) %collective-permute-start.7) | collective-permute-done | bytes 786464 | tf_op jit(solution)/shard_map/ppermute | solution.py:278
  288.2 4.5 collective-permute-done.5
  296.7 20.5 %all-to-all-start.3 = ((bf16[16,96,512]{2,1,0:T(8,128)(2,1)}), bf16[16,96,512]{2,1,0:T(8,128)(2,1)S(1)}, u32[]{:S(2)}, u32[]{:S(2)}) async-start(bf16[16,96,512]{2,1,0:T(8,128)(2,1)} %bitcast.24), calls=%async_computation.3 | async-start | bytes 3145728 | tf_op jit(solution)/shard_map/all_to_all | solution.py:268
  317.2 9.1 %multiply_convert_fusion.1 = bf16[1536,768]{1,0:T(8,128)(2,1)} fusion(bf16[1536,1536]{1,0:T(8,128)(2,1)} %add_convert_fusion, bf16[1536,2048]{1,0:T(8,128)(2,1)} %divide_convert_fusion, f32[]{:T(128)S(6)} %select_n.148), kind=kOutput, calls=%fused_computation.16 | convolution fusion | flops 3629776896 | bytes 11796484 | tf_op jit(solution)/shard_map/dot_general | solution.py:264
  326.3 27.9 %all-to-all-done.3 = bf16[16,96,512]{2,1,0:T(8,128)(2,1)S(1)} async-done(((bf16[16,96,512]{2,1,0:T(8,128)(2,1)}), bf16[16,96,512]{2,1,0:T(8,128)(2,1)S(1)}, u32[]{:S(2)}, u32[]{:S(2)}) %all-to-all-start.3) | async-done | bytes 1572896 | tf_op jit(solution)/shard_map/all_to_all | solution.py:268
  354.4 4.6 all-to-all-start.2
  364.4 69.8 %all-reduce = f32[16]{0:T(128)S(1)} all-reduce(f32[16]{0:T(128)S(1)} %dynamic-update-slice), channel_id=1, replica_groups=mesh['dp'=16,'tensor'=2] {'dp'}, use_global_device_ids=true, to_apply=%add | all-reduce | flops 16 | bytes 128
  462.5 3.8 gather_fusion.3
  466.3 3.3 gather_fusion.1
  (124 shorter events, 51.4 us)
Async XLA Ops:
  64.2 56.8 %all-to-all-start = ((bf16[32,48,768]{2,1,0:T(8,128)(2,1)}), bf16[32,48,768]{2,1,0:T(8,128)(2,1)}, u32[]{:S(2)}, u32[]{:S(2)}) async-start(bf16[32,48,768]{2,1,0:T(8,128)(2,1)} %get-tuple-element.17), calls=%async_computation | async-start | bytes 4718592 | tf_op jit(solution)/shard_map/all_to_all | solution.py:228
  73.5 50.5 %collective-permute-start = (bf16[1536,256]{1,0:T(8,128)(2,1)}, bf16[1536,256]{1,0:T(8,128)(2,1)}, u32[]{:S(2)}, u32[]{:S(2)}) collective-permute-start(bf16[1536,256]{1,0:T(8,128)(2,1)} %get-tuple-element.47), channel_id=1, source_target_pairs={{12,8},{22,18},{10,14},{16,20},{6,2},{28,24},{13,9},{23,19},{11,15... | collective-permute-start | bytes 2359304 | tf_op jit(solution)/shard_map/ppermute | solution.py:237
  76.9 48.4 %collective-permute-start.1 = (bf16[1536,256]{1,0:T(8,128)(2,1)}, bf16[1536,256]{1,0:T(8,128)(2,1)S(1)}, u32[]{:S(2)}, u32[]{:S(2)}) collective-permute-start(bf16[1536,256]{1,0:T(8,128)(2,1)} %get-tuple-element.46), channel_id=1, source_target_pairs={{0,8},{26,18},{6,14},{28,20},{4,2},{30,24},{1,9},{27,19},{7,15},{2... | collective-permute-start | bytes 2359304 | tf_op jit(solution)/shard_map/ppermute | solution.py:237
  77.6 47.8 %collective-permute-start.2 = (bf16[1536,256]{1,0:T(8,128)(2,1)}, bf16[1536,256]{1,0:T(8,128)(2,1)S(1)}, u32[]{:S(2)}, u32[]{:S(2)}) collective-permute-start(bf16[1536,256]{1,0:T(8,128)(2,1)} %get-tuple-element.45), channel_id=1, source_target_pairs={{10,8},{16,18},{12,14},{22,20},{0,2},{26,24},{11,9},{17,19},{13,15... | collective-permute-start | bytes 2359304 | tf_op jit(solution)/shard_map/ppermute | solution.py:237
  125.5 10.1 %copy-start.3 = (bf16[1536,2048]{1,0:T(8,128)(2,1)}, bf16[1536,2048]{1,0:T(8,128)(2,1)S(1)}, u32[]{:S(2)}) copy-start(bf16[1536,2048]{1,0:T(8,128)(2,1)S(1)} %constant_dynamic-update-slice_fusion) | copy-start | bytes 18874372
  139.2 14.8 %collective-permute-start.3 = (f32[1536,1536]{1,0:T(8,128)S(1)}, f32[1536,1536]{1,0:T(8,128)}, u32[]{:S(2)}, u32[]{:S(2)}) collective-permute-start(f32[1536,1536]{1,0:T(8,128)S(1)} %fusion.25), channel_id=1, source_target_pairs={{0,1},{1,0},{2,3},{3,2},{4,5},{5,4},{6,7},{7,6},{8,9},{9,8},{10,11... | collective-permute-start | bytes 28311560 | tf_op jit(solution)/shard_map/ppermute | solution.py:185
  214.2 15.0 %collective-permute-start.4 = (f32[1536,1536]{1,0:T(8,128)}, f32[1536,1536]{1,0:T(8,128)}, u32[]{:S(2)}, u32[]{:S(2)}) collective-permute-start(f32[1536,1536]{1,0:T(8,128)} %fusion.26), channel_id=1, source_target_pairs={{0,1},{1,0},{2,3},{3,2},{4,5},{5,4},{6,7},{7,6},{8,9},{9,8},{10,11... | collective-permute-start | bytes 28311560 | tf_op jit(solution)/shard_map/ppermute | solution.py:185
  264.0 4.5 collective-permute-start.6
  264.7 23.4 %collective-permute-start.7 = (bf16[1536,256]{1,0:T(8,128)(2,1)S(1)}, bf16[1536,256]{1,0:T(8,128)(2,1)S(1)}, u32[]{:S(2)}, u32[]{:S(2)}) collective-permute-start(bf16[1536,256]{1,0:T(8,128)(2,1)S(1)} %get-tuple-element.26), channel_id=1, source_target_pairs={{8,12},{18,22},{14,10},{20,16},{2,6},{24,28},{9,13},{19,23},{15,11... | collective-permute-start | bytes 2359304 | tf_op jit(solution)/shard_map/ppermute | solution.py:278
  266.0 26.7 %collective-permute-start.5 = (bf16[1536,256]{1,0:T(8,128)(2,1)S(1)}, bf16[1536,256]{1,0:T(8,128)(2,1)S(1)}, u32[]{:S(2)}, u32[]{:S(2)}) collective-permute-start(bf16[1536,256]{1,0:T(8,128)(2,1)S(1)} %get-tuple-element.28), channel_id=1, source_target_pairs={{8,10},{18,16},{14,12},{20,22},{2,0},{24,26},{9,11},{19,17},{15,13... | collective-permute-start | bytes 2359304 | tf_op jit(solution)/shard_map/ppermute | solution.py:278
  296.7 57.5 %all-to-all-start.3 = ((bf16[16,96,512]{2,1,0:T(8,128)(2,1)}), bf16[16,96,512]{2,1,0:T(8,128)(2,1)S(1)}, u32[]{:S(2)}, u32[]{:S(2)}) async-start(bf16[16,96,512]{2,1,0:T(8,128)(2,1)} %bitcast.24), calls=%async_computation.3 | async-start | bytes 3145728 | tf_op jit(solution)/shard_map/all_to_all | solution.py:268
  354.3 6.2 %copy-start.15 = (s32[6]{0:T(128)S(1)}, s32[6]{0:T(128)}, u32[]{:S(2)}) copy-start(s32[6]{0:T(128)} %param.35) | copy-start | bytes 76
  354.3 6.3 %copy-start = (s32[6]{0:T(128)S(1)}, s32[6]{0:T(128)}, u32[]{:S(2)}) copy-start(s32[6]{0:T(128)} %constant.27.clone) | copy-start | bytes 76
  354.3 7.1 %copy-start.12 = (s32[16,2]{0,1:T(2,128)S(1)}, s32[16,2]{0,1:T(2,128)}, u32[]{:S(2)}) copy-start(s32[16,2]{0,1:T(2,128)} %param.45) | copy-start | bytes 388
  354.3 7.2 %copy-start.8 = (f32[1344]{0:T(1024)S(1)}, f32[1344]{0:T(1024)}, u32[]{:S(2)}) copy-start(f32[1344]{0:T(1024)} %param.37) | copy-start | bytes 16132
  354.3 7.2 %copy-start.9 = (f32[1344]{0:T(1024)S(1)}, f32[1344]{0:T(1024)}, u32[]{:S(2)}) copy-start(f32[1344]{0:T(1024)} %param.38) | copy-start | bytes 16132
  354.3 7.2 %copy-start.10 = (f32[1344]{0:T(1024)S(1)}, f32[1344]{0:T(1024)}, u32[]{:S(2)}) copy-start(f32[1344]{0:T(1024)} %param.39) | copy-start | bytes 16132
  354.3 7.2 %copy-start.11 = (f32[1344]{0:T(1024)S(1)}, f32[1344]{0:T(1024)}, u32[]{:S(2)}) copy-start(f32[1344]{0:T(1024)} %param.40) | copy-start | bytes 16132
  354.3 7.8 %copy-start.4 = (f32[128,768]{1,0:T(8,128)S(1)}, f32[128,768]{1,0:T(8,128)}, u32[]{:S(2)}) copy-start(f32[128,768]{1,0:T(8,128)} %param.44) | copy-start | bytes 1179652
  354.3 7.8 %copy-start.5 = (f32[128,768]{1,0:T(8,128)S(1)}, f32[128,768]{1,0:T(8,128)}, u32[]{:S(2)}) copy-start(f32[128,768]{1,0:T(8,128)} %param.42) | copy-start | bytes 1179652
  354.4 7.8 %copy-start.6 = (f32[128,768]{1,0:T(8,128)S(1)}, f32[128,768]{1,0:T(8,128)}, u32[]{:S(2)}) copy-start(f32[128,768]{1,0:T(8,128)} %param.41) | copy-start | bytes 1179652
  354.4 7.8 %copy-start.7 = (f32[128,768]{1,0:T(8,128)S(1)}, f32[128,768]{1,0:T(8,128)}, u32[]{:S(2)}) copy-start(f32[128,768]{1,0:T(8,128)} %param.43) | copy-start | bytes 1179652
  354.4 81.9 %all-to-all-start.2 = ((bf16[16,96,768]{2,1,0:T(8,128)(2,1)}), bf16[16,96,768]{2,1,0:T(8,128)(2,1)}, u32[]{:S(2)}, u32[]{:S(2)}) async-start(bf16[16,96,768]{2,1,0:T(8,128)(2,1)} %bitcast.156), calls=%async_computation.2 | async-start | bytes 4718592 | tf_op jit(solution)/shard_map/all_to_all | solution.py:268
  359.0 75.8 %copy-start.13 = (s32[14]{0:T(128)S(1)}, s32[14]{0:T(128)}, u32[]{:S(2)}) copy-start(s32[14]{0:T(128)} %param.36) | copy-start | bytes 172
  (9 other events, 42.4 us)

commit v3 on v2

--- a/solution.py
+++ b/solution.py
@@ -185,10 +185,235 @@
     return lax.ppermute(x, "tensor", [(0, 1), (1, 0)])
 
 
-def inverse_of(order):
-    count = order.shape[0]
-    match = order[None, :] == jnp.arange(count, dtype=jnp.int32)[:, None]
-    return jnp.sum(jnp.where(match, jnp.arange(count, dtype=jnp.int32)[None, :], 0), axis=1)
+BLOCK = 256
+EDGE = D // BLOCK
+NEAR = EDGE // 2
+PACKED = EDGE * NEAR + NEAR
+VMEM_LIMIT = 58 * 1024 * 1024
+
+
+def each_pair(body):
+    def row(i, carry):
+        for d in range(NEAR):
+            j = lax.rem(i + d, EDGE)
+            body(i * NEAR + d, i, j, d == 0)
+        return carry
+
+    lax.fori_loop(0, EDGE, row, 0)
+
+    def far(i, carry):
+        body(EDGE * NEAR + i, i, i + NEAR, False)
+        return carry
+
+    lax.fori_loop(0, NEAR, far, 0)
+
+
+def span(i):
+    return pl.ds(pl.multiple_of(i * BLOCK, BLOCK), BLOCK)
+
+
+def nt(a, b):
+    return lax.dot_general(a, b, (((1,), (1,)), ((), ())), preferred_element_type=jnp.float32)
+
+
+def gram_blocks(parts, out):
+    def body(slot, i, j, diagonal):
+        total = nt(parts[0][span(i), :], parts[0][span(j), :])
+        for part in parts[1:]:
+            total += nt(part[span(i), :], part[span(j), :])
+        out[slot] = total
+
+    each_pair(body)
+
+
+def mirror(out, i, j, diagonal, value):
+    out[span(i), span(j)] = value.astype(out.dtype)
+    if not diagonal:
+        out[span(j), span(i)] = value.T.astype(out.dtype)
+
+
+def polynomial_blocks(normed, out):
+    def body(slot, i, j, diagonal):
+        squared = jnp.dot(normed[span(i), :], normed[:, span(j)], preferred_element_type=jnp.float32)
+        value = QUINTIC_CUBIC * normed[span(i), span(j)].astype(jnp.float32) + QUINTIC_FIFTH * squared
+        mirror(out, i, j, diagonal, value)
+
+    each_pair(body)
+
+
+def mixed_rows(polynomial, part, scale, targets):
+    def row(i, carry):
+        at = 0
+        for target in targets:
+            for c in range(0, target.shape[1], BLOCK):
+                columns = slice(at, at + BLOCK)
+                product = jnp.dot(
+                    polynomial[span(i), :], part[:, columns], preferred_element_type=jnp.float32
+                )
+                mixed = QUINTIC_LINEAR * part[span(i), columns].astype(jnp.float32) + product
+                target[span(i), c : c + BLOCK] = (mixed * scale).astype(target.dtype)
+                at += BLOCK
+        return carry
+
+    lax.fori_loop(0, EDGE, row, 0)
+
+
+def gram_kernel(flag, first, second, *rest):
+    relayed, out = rest[:-1], rest[-1]
+    heavy = flag[0] > 0
+
+    @pl.when(heavy)
+    def _():
+        gram_blocks([first, second, *relayed], out)
+
+    @pl.when(jnp.logical_not(heavy))
+    def _():
+        gram_blocks([first], out)
+
+
+def middle_kernel(flag, own, other, first, second, *rest):
+    count = len(rest) - 6
+    relayed = rest[:count]
+    first_out, second_out, packed, scale_out, normed, polynomial = rest[count:]
+    heavy = flag[0] > 0
+
+    def add(slot, total):
+        gram = own[slot] + other[slot]
+        packed[slot] = gram
+        return total + jnp.sum(gram * gram)
+
+    def row(i, carry):
+        once, twice = carry
+        once = add(i * NEAR, once)
+        for d in range(1, NEAR):
+            twice = add(i * NEAR + d, twice)
+        return once, twice
+
+    once, twice = lax.fori_loop(0, EDGE, row, (jnp.float32(0.0), jnp.float32(0.0)))
+    twice = lax.fori_loop(0, NEAR, lambda i, t: add(EDGE * NEAR + i, t), twice)
+    total = jnp.full((8, LANE), once + 2.0 * twice, jnp.float32)
+    scale = jnp.sqrt(total) + 1e-06
+    scale_out[...] = scale
+    inverse = (1.0 / scale)[0:1, 0:1]
+    root = (1.0 / jnp.sqrt(scale))[0:1, 0:1]
+
+    def norm(slot, i, j, diagonal):
+        mirror(normed, i, j, diagonal, packed[slot] * inverse)
+
+    each_pair(norm)
+    polynomial_blocks(normed, polynomial)
+    mixed_rows(polynomial, first, root, [first_out])
+
+    @pl.when(heavy)
+    def _():
+        at = 0
+        for part in (second, *relayed):
+            width = part.shape[1]
+            mixed_rows(polynomial, part, root, [second_out.at[:, at : at + width]])
+            at += width
+        gram_blocks([first_out, second_out], packed)
+
+    @pl.when(jnp.logical_not(heavy))
+    def _():
+        gram_blocks([first_out], packed)
+
+
+def last_kernel(factor, own, other, first, polynomial, out, normed):
+    def norm(slot, i, j, diagonal):
+        mirror(normed, i, j, diagonal, own[slot] + other[slot])
+
+    each_pair(norm)
+    polynomial_blocks(normed, polynomial)
+    mixed_rows(polynomial, first, factor[0], [out])
+
+
+def rest_kernel(flag, factor, polynomial, second, *outs):
+    @pl.when(flag[0] > 0)
+    def _():
+        mixed_rows(polynomial, second, factor[0], outs)
+
+
+def call(kernel, name, scalars, arrays, outs, scratch=(), flops=0):
+    moved = sum(x.size * x.dtype.itemsize for x in arrays)
+    moved += sum(math.prod(o.shape) * o.dtype.itemsize for o in outs)
+    smem = pl.BlockSpec(memory_space=pltpu.SMEM)
+    return pl.pallas_call(
+        kernel,
+        in_specs=[smem] * len(scalars) + [pl.BlockSpec(memory_space=pltpu.VMEM)] * len(arrays),
+        out_specs=[pl.BlockSpec(memory_space=pltpu.VMEM)] * len(outs),
+        out_shape=list(outs),
+        scratch_shapes=list(scratch),
+        compiler_params=pltpu.CompilerParams(vmem_limit_bytes=VMEM_LIMIT),
+        cost_estimate=pl.CostEstimate(flops=flops, bytes_accessed=moved, transcendentals=0),
+        name=name,
+    )(*scalars, *arrays)
+
+
+def assemble_squares(plan, square_order, first_back):
+    count = square_order.shape[0]
+
+    def kernel(order, source, out, sems):
+        copies = [
+            pltpu.make_async_copy(source.at[plan.light[j]], out.at[order[j]], sems.at[j])
+            for j in range(count)
+        ]
+        for copy in copies:
+            copy.start()
+        for copy in copies:
+            copy.wait()
+
+    return pl.pallas_call(
+        kernel,
+        in_specs=[pl.BlockSpec(memory_space=pltpu.SMEM), pl.BlockSpec(memory_space=pl.ANY)],
+        out_specs=pl.BlockSpec(memory_space=pl.ANY),
+        out_shape=jax.ShapeDtypeStruct((count,) + first_back.shape[1:], jnp.bfloat16),
+        scratch_shapes=[pltpu.SemaphoreType.DMA((count,))],
+        name="assemble_squares",
+    )(square_order, first_back)
+
+
+def assemble_swiglu(plan, swiglu_order, first_back, second_back):
+    count = swiglu_order.shape[0]
+    narrow = first_back.shape[2]
+    rows = first_back.shape[1]
+    wide = narrow + plan.granules * GRANULE
+
+    def kernel(order, first, second, out, sems):
+        copies = []
+
+        def move(source, j, at, width):
+            copies.append(
+                pltpu.make_async_copy(
+                    source, out.at[order[j], :, pl.ds(at, width)], sems.at[len(copies)]
+                )
+            )
+
+        for j in range(count):
+            owner = plan.heavy[j]
+            move(first.at[owner], j, 0, narrow)
+            move(second.at[owner], j, narrow, 2 * GRANULE)
+            for b in range(2, plan.granules):
+                chip, where = plan.place[(j, b)]
+                source = second.at[chip, :, pl.ds(where * GRANULE, GRANULE)]
+                move(source, j, narrow + b * GRANULE, GRANULE)
+        for copy in copies:
+            copy.start()
+        for copy in copies:
+            copy.wait()
+
+    return pl.pallas_call(
+        kernel,
+        in_specs=[pl.BlockSpec(memory_space=pltpu.SMEM)] + [pl.BlockSpec(memory_space=pl.ANY)] * 2,
+        out_specs=pl.BlockSpec(memory_space=pl.ANY),
+        out_shape=jax.ShapeDtypeStruct((count, rows, wide), jnp.bfloat16),
+        scratch_shapes=[pltpu.SemaphoreType.DMA((count * plan.granules,))],
+        name="assemble_swiglu",
+    )(swiglu_order, first_back, second_back)
+
+
+def lookup(table, positions):
+    matches = positions[:, None] == jnp.arange(table.shape[0], dtype=jnp.int32)[None, :]
+    return jnp.sum(jnp.where(matches, table[None, :], 0), axis=1)
 
 
 def local(
@@ -235,50 +460,60 @@
         pick = jnp.asarray(plan.slot_in_pass[p])[chip]
         pairs = [(plan.take[p][k], plan.heavy[k]) for k in range(swiglu_count)]
         relayed.append(lax.ppermute(jnp.where(pick, pieces[1], pieces[0]), "dp", pairs))
-    kept = jnp.where(heavy_here, second_got, jnp.zeros((), jnp.bfloat16))
-    matrix = jnp.concatenate([first_got, kept] + relayed, axis=1)
-
-    factor = jnp.where(heavy_here, jnp.float32(math.sqrt(FF)), jnp.float32(math.sqrt(D)))
-    iterate = matrix
-    first_scale = jnp.float32(1.0)
-    for round_index in range(NS_STEPS):
-        gram_part = jnp.einsum("rc,sc->rs", iterate, iterate, preferred_element_type=jnp.float32)
-        gram = gram_part + other_core(gram_part)
-        if round_index == 0:
-            gram_scale = jnp.sqrt(jnp.sum(gram * gram)) + 1e-06
-            first_scale = gram_scale
-        else:
-            gram_scale = jnp.float32(1.0)
-        normed = (gram / gram_scale).astype(jnp.bfloat16)
-        squared = jnp.dot(normed, normed, preferred_element_type=jnp.float32)
-        polynomial = (
-            QUINTIC_CUBIC * normed.astype(jnp.float32) + QUINTIC_FIFTH * squared
-        ).astype(jnp.bfloat16)
-        if round_index < NS_STEPS - 1:
-            product = jnp.dot(polynomial, iterate, preferred_element_type=jnp.float32)
-            mixed = (QUINTIC_LINEAR * iterate.astype(jnp.float32) + product) / jnp.sqrt(gram_scale)
-            iterate = mixed.astype(jnp.bfloat16)
-
-    def finish(columns):
-        part = iterate[:, columns]
-        product = jnp.dot(polynomial, part, preferred_element_type=jnp.float32)
-        return (factor * (QUINTIC_LINEAR * part.astype(jnp.float32) + product)).astype(jnp.bfloat16)
+    flag = heavy_here.astype(jnp.int32).reshape(1)
+    factor = jnp.where(heavy_here, jnp.float32(math.sqrt(FF)), jnp.float32(math.sqrt(D))).reshape(1)
+    packed = jax.ShapeDtypeStruct((PACKED, BLOCK, BLOCK), jnp.float32)
+    whole_square = jax.ShapeDtypeStruct((D, D), jnp.bfloat16)
+    first_shape = jax.ShapeDtypeStruct((D, narrow), jnp.bfloat16)
+    extra = plan.granules * GRANULE
+    second_shape = jax.ShapeDtypeStruct((D, extra), jnp.bfloat16)
+    square_buffer = pltpu.VMEM((D, D), jnp.bfloat16)
+    half = D * D * (narrow + extra)
+    (own,) = call(
+        gram_kernel, "gram", [flag], [first_got, second_got, *relayed], [packed], flops=half
+    )
+    first_mid, second_mid, own_mid, scale = call(
+        middle_kernel,
+        "middle",
+        [flag],
+        [own, other_core(own), first_got, second_got, *relayed],
+        [first_shape, second_shape, packed, jax.ShapeDtypeStruct((8, LANE), jnp.float32)],
+        [square_buffer, square_buffer],
+        flops=3 * half + D * D * D,
+    )
+    logs = lax.all_gather(scale, "dp")
+    polynomial, first_done = call(
+        last_kernel,
+        "last",
+        [factor],
+        [own_mid, other_core(own_mid), first_mid],
+        [whole_square, first_shape],
+        [square_buffer],
+        flops=D * D * D + 2 * D * D * narrow,
+    )
+    piece_shape = jax.ShapeDtypeStruct((D, GRANULE), jnp.bfloat16)
+    rest = call(
+        rest_kernel,
+        "rest",
+        [flag, factor],
+        [polynomial, second_mid],
+        [jax.ShapeDtypeStruct((D, 2 * GRANULE), jnp.bfloat16)] + [piece_shape] * plan.passes,
+        flops=2 * D * D * extra,
+    )
 
     def send_back(x):
         return lax.all_to_all(
             x.reshape(chips, chip_rows, -1), "dp", split_axis=0, concat_axis=0, tiled=True
         )
 
-    first_back = send_back(finish(slice(0, narrow)))
-    rest = finish(slice(narrow, None))
+    first_back = send_back(first_done)
     handed = []
     for p in range(plan.passes):
         pairs = [(plan.heavy[k], plan.take[p][k]) for k in range(swiglu_count)]
-        at = (2 + p) * GRANULE
-        handed.append(lax.ppermute(rest[:, at : at + GRANULE], "dp", pairs))
+        handed.append(lax.ppermute(rest[1 + p], "dp", pairs))
     halves = []
     for where in range(2):
-        value = rest[:, where * GRANULE : (where + 1) * GRANULE]
+        value = rest[0][:, where * GRANULE : (where + 1) * GRANULE]
         for p in range(plan.passes):
             mine = np.zeros((chips,), np.bool_)
             for k in range(swiglu_count):
@@ -286,28 +521,18 @@
                     mine[plan.take[p][k]] = True
             value = jnp.where(jnp.asarray(mine)[chip], handed[p], value)
         halves.append(value)
-    second_back = send_back(jnp.concatenate(halves, axis=1))
-
-    slot_of_square = inverse_of(square_order)
-    slot_of_swiglu = inverse_of(swiglu_order)
-    chip_of_square = jnp.asarray(np.array(plan.light, np.int32))[slot_of_square]
-    chip_of_swiglu = jnp.asarray(np.array(plan.heavy, np.int32))[slot_of_swiglu]
-    square_update = first_back[chip_of_square]
-    parts = [first_back[np.array(plan.heavy, np.int32)]]
-    for b in range(plan.granules):
-        parts.append(
-            jnp.stack(
-                [
-                    second_back[plan.place[(j, b)][0], :, plan.place[(j, b)][1] * GRANULE :][:, :GRANULE]
-                    for j in range(swiglu_count)
-                ]
-            )
-        )
-    swiglu_update = jnp.concatenate(parts, axis=2)[slot_of_swiglu]
-
-    logs = lax.all_gather(0.5 * jnp.log(first_scale), "dp")
-    matrix_chip = jnp.concatenate([chip_of_square, chip_of_swiglu])
-    owner_norms = jnp.sum(jnp.where(owners == chip, logs[matrix_chip], 0.0)).reshape(1)
+    second_out, first_back = lax.optimization_barrier((jnp.concatenate(halves, axis=1), first_back))
+    second_back = send_back(second_out)
+
+    square_update = assemble_squares(plan, square_order, first_back)
+    swiglu_update = assemble_swiglu(plan, swiglu_order, first_back, second_back)
+
+    slot_chips = np.array(plan.light + plan.heavy, np.int32)
+    slot_owner = jnp.concatenate(
+        [lookup(owners[:square_count], square_order), lookup(owners[square_count:], swiglu_order)]
+    )
+    slot_logs = 0.5 * jnp.log(logs[:, 0, 0])[slot_chips]
+    owner_norms = jnp.sum(jnp.where(slot_owner == chip, slot_logs, 0.0)).reshape(1)
 
     vector_step, first_vector, second_vector = adamw_terms(
         vector_values, vector_grad, vector_first, vector_second

time: 478 us -> 491 us (1.027); the launches traced: 470 us -> 488 us
  Pallas kernels: 20.7 us -> 196 us
  matrix products: 100 us -> 0 us
  local copies, waits for them, and re-layouts: 47.7 us -> 10.7 us
  starting transfers between devices: 39.4 us -> 73.6 us
  waiting for transfers between devices: 122 us -> 98.4 us
  blocking collectives: 113 us -> 91.7 us
  other arithmetic: 24.1 us -> 15.5 us
    pallas_call x0 -> x6, Pallas kernels: none -> 175 us  [the longest x1 73.5 us: assemble_swiglu(): pl.pallas_call(kernel, in_specs=[pl.BlockSpec(memory_space=pltpu.SMEM)] +...]
    dot_general x6 -> x0, matrix products: 100 us -> none  [the longest x1 30.1 us: local(): product = jnp.dot(polynomial, iterate, preferred_element_type=jnp.float32)]
    unnamed x1 -> x0, blocking collectives: 69.8 us -> none
    all_gather x0 -> x1, blocking collectives: none -> 48.9 us  [local(): logs = lax.all_gather(scale, 'dp')]
    all_to_all x2, starting transfers between devices: 25.1 us -> 59.5 us  [send_back(): lax.all_to_all(x.reshape(chips, chip_rows, -1), 'dp', split_axis=0, conca...]
    ppermute x3, waiting for transfers between devices: 0.01 us -> 30.1 us  [local(): lax.ppermute(jnp.where(pick, pieces[1], pieces[0]), 'dp', pairs)]
    all_to_all x1, waiting for transfers between devices: 41.3 us -> 12 us  [local(): lax.all_to_all(first_send.reshape(D, narrow), both, split_axis=0, concat_...]
    all_to_all x2, waiting for transfers between devices: 27.9 us -> 0.01 us  [send_back(): lax.all_to_all(x.reshape(chips, chip_rows, -1), 'dp', split_axis=0, conca...]
  transfers between devices with their start and end apart: 11 -> 11, of which waited for: 6 -> 6; matrix products, arithmetic and copies ran while one was open for 6% -> 4% of each run, Pallas kernels for 0% -> 9%
where the time goes in v3:
time: 491 us; the launch traced here: 488 us
  Pallas kernels  196 us (40%)
  waiting for transfers between devices  98.4 us (20%)
  blocking collectives  91.7 us (19%)
  starting transfers between devices  73.6 us (15%)
  other arithmetic  15.5 us (3%)
  local copies, waits for them, and re-layouts  10.7 us (2%)
    pallas_call x1, Pallas kernels, assemble_swiglu(): pl.pallas_call(kernel, in_specs=[pl.BlockSpec(memory_space=pltpu.SMEM)] +...  73.5 us
    pallas_call x4, Pallas kernels, call(): pl.pallas_call(kernel, in_specs=[smem] * len(scalars) + [pl.BlockSpec(mem...  63.9 us
    all_to_all x2, starting transfers between devices, send_back(): lax.all_to_all(x.reshape(chips, chip_rows, -1), 'dp', split_axis=0, conca...  59.5 us
    all_gather x1, blocking collectives, local(): logs = lax.all_gather(scale, 'dp')  48.9 us
    all_to_all x1, blocking collectives, local(): lax.all_to_all(second_send.reshape(D, 2 * GRANULE), both, split_axis=0, c...  42.9 us
    ppermute x3, waiting for transfers between devices, local(): handed.append(lax.ppermute(rest[1 + p], 'dp', pairs))  38.5 us
    pallas_call x1, Pallas kernels, assemble_squares(): pl.pallas_call(kernel, in_specs=[pl.BlockSpec(memory_space=pltpu.SMEM), p...  37.6 us
    ppermute x3, waiting for transfers between devices, local(): lax.ppermute(jnp.where(pick, pieces[1], pieces[0]), 'dp', pairs)  30.1 us
  transfers between devices with their start and end apart: 11, of which 6 were waited for; matrix products, arithmetic and copies ran while one was open for 4% of the time, Pallas kernels for 9%

profile of v3, /device:TPU:12, one launch (start us, length us, event | category | flops | bytes accessed | tf_op | source)
XLA Modules:
  0.0 488.0 jit_solution(9285893028695831065)
XLA Ops:
  0.6 20.7 %prepare.1 = (f32[48,12,8,128]{3,2,1,0:T(8,128)}, f32[48,32,6,128]{3,2,1,0:T(8,128)}, bf16[32,48,768]{2,1,0:T(8,128)(2,1)}, bf16[32,48,512]{2,1,0:T(8,128)(2,1)}) custom-call(f32[48,12,8,128]{3,2,1,0:T(8,128)} %bitcast.42, f32[48,12,8,128]{3,2,1,0:T(8,128)} %bitcast.43, f32[48,32,6,128]{3,2,1,0:T(8,128)} %bitcast.35, f32[48,32,6,128]{3,2,1,0:T(8,128)} %bitcast.36), custom_call_target="tpu_custom_call" | custom-call | tf_op jit(solution)/shard_map/prepare/pallas_call | solution.py:162
  21.3 42.9 %all_to_all.26 = bf16[32,48,512]{2,1,0:T(8,128)(2,1)S(1)} all-to-all(bf16[32,48,512]{2,1,0:T(8,128)(2,1)} %get-tuple-element.30), channel_id=1, replica_groups=mesh['dp'=16,'tensor'=2] {'dp','tensor'}, dimensions={0} | all-to-all | bytes 3145728 | tf_op jit(solution)/shard_map/all_to_all | solution.py:450
  64.2 4.7 all-to-all-start
  71.6 2.5 collective-permute-start
  74.8 2.8 collective-permute-start.2
  78.9 30.1 %collective-permute-done.rest_0_ = bf16[1536,256]{1,0:T(8,128)(2,1)S(1)} collective-permute-done((bf16[1536,256]{1,0:T(8,128)(2,1)S(1)}, bf16[1536,256]{1,0:T(8,128)(2,1)S(1)}, u32[]{:S(2)}, u32[]{:S(2)}) %collective-permute-start) | collective-permute-done | bytes 786464 | tf_op jit(solution)/shard_map/ppermute | solution.py:462
  109.0 12.0 %all-to-all-done = bf16[32,48,768]{2,1,0:T(8,128)(2,1)} async-done(((bf16[32,48,768]{2,1,0:T(8,128)(2,1)}), bf16[32,48,768]{2,1,0:T(8,128)(2,1)}, u32[]{:S(2)}, u32[]{:S(2)}) %all-to-all-start) | async-done | bytes 2359328 | tf_op jit(solution)/shard_map/all_to_all | solution.py:453
  121.0 9.2 %gram.1.own = f32[21,256,256]{2,1,0:T(8,128)} custom-call(s32[1]{0:T(128)S(6)} %convert_element_type.7.flag, bf16[1536,768]{1,0:T(8,128)(2,1)} %bitcast.13.first, bf16[1536,512]{1,0:T(8,128)(2,1)} %bitcast.38, bf16[1536,256]{1,0:T(8,128)(2,1)} %copy-done.12, bf16[1536,256]{1,0:T(8,128)(2,1)} %copy-done.13, bf16[1536,256]{1,0:T(8,128)(2,1)} %copy-done.14), custom_call_target="tpu_custom_call" | custom-call | flops 4831838208 | bytes 11796480 | tf_op jit(solution)/shard_map/gram/pallas_call | solution.py:340
  130.3 9.2 %collective-permute-done.3.other = f32[21,256,256]{2,1,0:T(8,128)S(1)} collective-permute-done((f32[21,256,256]{2,1,0:T(8,128)}, f32[21,256,256]{2,1,0:T(8,128)S(1)}, u32[]{:S(2)}, u32[]{:S(2)}) %collective-permute-start.3) | collective-permute-done | bytes 5505056 | tf_op jit(solution)/shard_map/ppermute | solution.py:185
  139.5 2.4 copy-done.10
  141.9 29.5 %middle.1 = (bf16[1536,768]{1,0:T(8,128)(2,1)}, bf16[1536,1280]{1,0:T(8,128)(2,1)}, f32[21,256,256]{2,1,0:T(8,128)}, f32[8,128]{1,0:T(8,128)}) custom-call(s32[1]{0:T(128)S(6)} %convert_element_type.7.flag, f32[21,256,256]{2,1,0:T(8,128)} %gram.1.own, f32[21,256,256]{2,1,0:T(8,128)} %copy-done.10, bf16[1536,768]{1,0:T(8,128)(2,1)} %bitcast.13.first, ...), custom_call_target="tpu_custom_call" | custom-call | flops 18119393280 | bytes 29102080 | tf_op jit(solution)/shard_map/middle/pallas_call | solution.py:340
  172.1 8.5 %collective-permute-done.4.other = f32[21,256,256]{2,1,0:T(8,128)S(1)} collective-permute-done((f32[21,256,256]{2,1,0:T(8,128)}, f32[21,256,256]{2,1,0:T(8,128)S(1)}, u32[]{:S(2)}, u32[]{:S(2)}) %collective-permute-start.4) | collective-permute-done | bytes 5505056 | tf_op jit(solution)/shard_map/ppermute | solution.py:185
  180.6 2.5 copy-done.11
  183.1 19.7 %last.1 = (bf16[1536,1536]{1,0:T(8,128)(2,1)}, bf16[1536,768]{1,0:T(8,128)(2,1)}) custom-call(f32[1]{0:T(128)S(6)} %select_n.101.factor, f32[21,256,256]{2,1,0:T(8,128)} %get-tuple-element.31.own, f32[21,256,256]{2,1,0:T(8,128)} %copy-done.11, bf16[1536,768]{1,0:T(8,128)(2,1)} %get-tuple-element.32.first), custom_call_target="tpu_custom_call" | custom-call | flops 7247757312 | bytes 20447232 | tf_op jit(solution)/shard_map/last/pallas_call | solution.py:340
  202.8 33.3 %all-to-all-start.2 = ((bf16[16,96,768]{2,1,0:T(8,128)(2,1)}), bf16[16,96,768]{2,1,0:T(8,128)(2,1)S(1)}, u32[]{:S(2)}, u32[]{:S(2)}) async-start(bf16[16,96,768]{2,1,0:T(8,128)(2,1)} %bitcast.41), calls=%async_computation.2 | async-start | bytes 4718592 | tf_op jit(solution)/shard_map/all_to_all | solution.py:505
  236.1 5.5 %rest.1 = (bf16[1536,512]{1,0:T(8,128)(2,1)}, bf16[1536,256]{1,0:T(8,128)(2,1)}, bf16[1536,256]{1,0:T(8,128)(2,1)}, bf16[1536,256]{1,0:T(8,128)(2,1)}) custom-call(s32[1]{0:T(128)S(6)} %convert_element_type.7.flag, f32[1]{0:T(128)S(6)} %select_n.101.factor, bf16[1536,1536]{1,0:T(8,128)(2,1)} %get-tuple-element.33.polynomial, ...), custom_call_target="tpu_custom_call" | custom-call | flops 6039797760 | bytes 12582912 | tf_op jit(solution)/shard_map/rest/pallas_call | solution.py:340
  246.1 32.9 %collective-permute-done.7 = bf16[1536,256]{1,0:T(8,128)(2,1)S(1)} collective-permute-done((bf16[1536,256]{1,0:T(8,128)(2,1)}, bf16[1536,256]{1,0:T(8,128)(2,1)S(1)}, u32[]{:S(2)}, u32[]{:S(2)}) %collective-permute-start.7) | collective-permute-done | bytes 786464 | tf_op jit(solution)/shard_map/ppermute | solution.py:513
  279.0 5.6 %collective-permute-done.5 = bf16[1536,256]{1,0:T(8,128)(2,1)S(1)} collective-permute-done((bf16[1536,256]{1,0:T(8,128)(2,1)}, bf16[1536,256]{1,0:T(8,128)(2,1)S(1)}, u32[]{:S(2)}, u32[]{:S(2)}) %collective-permute-start.5) | collective-permute-done | bytes 786464 | tf_op jit(solution)/shard_map/ppermute | solution.py:513
  284.7 4.2 select_select_fusion.1
  290.2 26.2 %all-to-all-start.3 = ((bf16[16,96,512]{2,1,0:T(8,128)(2,1)}), bf16[16,96,512]{2,1,0:T(8,128)(2,1)}, u32[]{:S(2)}, u32[]{:S(2)}) async-start(bf16[16,96,512]{2,1,0:T(8,128)(2,1)} %bitcast.40), calls=%async_computation.3 | async-start | bytes 3145728 | tf_op jit(solution)/shard_map/all_to_all | solution.py:505
  323.9 2.4 fusion.2
  326.3 48.9 %all-gather = f32[128,128]{1,0:T(8,128)S(1)} all-gather(f32[8,128]{1,0:T(8,128)S(1)} %copy-done.7), channel_id=2, replica_groups=mesh['dp'=16,'tensor'=2] {'dp'}, dimensions={0}, use_global_device_ids=true | all-gather | bytes 69632 | tf_op jit(solution)/shard_map/all_gather | solution.py:484
  376.7 37.6 %assemble_squares.1 = bf16[8,96,768]{2,1,0:T(8,128)(2,1)} custom-call(s32[8]{0:T(128)} %order.2, bf16[16,96,768]{2,1,0:T(8,128)(2,1)} %copy-done), custom_call_target="tpu_custom_call" | custom-call | tf_op jit(solution)/shard_map/assemble_squares/pallas_call | solution.py:365
  414.3 73.5 %assemble_swiglu.1 = bf16[6,96,2048]{2,1,0:T(8,128)(2,1)} custom-call(s32[6]{0:T(128)} %order.3, bf16[16,96,768]{2,1,0:T(8,128)(2,1)} %copy-done, bf16[16,96,512]{2,1,0:T(8,128)(2,1)} %all-to-all-done.3.second), custom_call_target="tpu_custom_call" | custom-call | tf_op jit(solution)/shard_map/assemble_swiglu/pallas_call | solution.py:404
  (70 shorter events, 18.8 us)
Async XLA Ops:
  64.2 56.8 %all-to-all-start = ((bf16[32,48,768]{2,1,0:T(8,128)(2,1)}), bf16[32,48,768]{2,1,0:T(8,128)(2,1)}, u32[]{:S(2)}, u32[]{:S(2)}) async-start(bf16[32,48,768]{2,1,0:T(8,128)(2,1)} %get-tuple-element.29), calls=%async_computation | async-start | bytes 4718592 | tf_op jit(solution)/shard_map/all_to_all | solution.py:453
  71.6 37.4 %collective-permute-start = (bf16[1536,256]{1,0:T(8,128)(2,1)S(1)}, bf16[1536,256]{1,0:T(8,128)(2,1)S(1)}, u32[]{:S(2)}, u32[]{:S(2)}) collective-permute-start(bf16[1536,256]{1,0:T(8,128)(2,1)S(1)} %get-tuple-element.50), channel_id=1, source_target_pairs={{12,8},{22,18},{10,14},{16,20},{6,2},{28,24},{13,9},{23,19},{11,15... | collective-permute-start | bytes 2359304 | tf_op jit(solution)/shard_map/ppermute | solution.py:462
  74.1 34.9 %collective-permute-start.1 = (bf16[1536,256]{1,0:T(8,128)(2,1)S(1)}, bf16[1536,256]{1,0:T(8,128)(2,1)S(1)}, u32[]{:S(2)}, u32[]{:S(2)}) collective-permute-start(bf16[1536,256]{1,0:T(8,128)(2,1)S(1)} %get-tuple-element.49), channel_id=1, source_target_pairs={{0,8},{26,18},{6,14},{28,20},{4,2},{30,24},{1,9},{27,19},{7,15},{2... | collective-permute-start | bytes 2359304 | tf_op jit(solution)/shard_map/ppermute | solution.py:462
  74.8 34.2 %collective-permute-start.2 = (bf16[1536,256]{1,0:T(8,128)(2,1)S(1)}, bf16[1536,256]{1,0:T(8,128)(2,1)S(1)}, u32[]{:S(2)}, u32[]{:S(2)}) collective-permute-start(bf16[1536,256]{1,0:T(8,128)(2,1)S(1)} %get-tuple-element.48), channel_id=1, source_target_pairs={{10,8},{16,18},{12,14},{22,20},{0,2},{26,24},{11,9},{17,19},{13,15... | collective-permute-start | bytes 2359304 | tf_op jit(solution)/shard_map/ppermute | solution.py:462
  109.0 12.1 %copy-start.12 = (bf16[1536,256]{1,0:T(8,128)(2,1)}, bf16[1536,256]{1,0:T(8,128)(2,1)S(1)}, u32[]{:S(2)}) copy-start(bf16[1536,256]{1,0:T(8,128)(2,1)S(1)} %collective-permute-done.rest_0_) | copy-start | bytes 2359300
  109.0 12.1 %copy-start.13 = (bf16[1536,256]{1,0:T(8,128)(2,1)}, bf16[1536,256]{1,0:T(8,128)(2,1)S(1)}, u32[]{:S(2)}) copy-start(bf16[1536,256]{1,0:T(8,128)(2,1)S(1)} %collective-permute-done.1.rest_1_) | copy-start | bytes 2359300
  109.0 12.1 %copy-start.14 = (bf16[1536,256]{1,0:T(8,128)(2,1)}, bf16[1536,256]{1,0:T(8,128)(2,1)S(1)}, u32[]{:S(2)}) copy-start(bf16[1536,256]{1,0:T(8,128)(2,1)S(1)} %collective-permute-done.2.rest_2_) | copy-start | bytes 2359300
  130.3 9.2 %collective-permute-start.3 = (f32[21,256,256]{2,1,0:T(8,128)}, f32[21,256,256]{2,1,0:T(8,128)S(1)}, u32[]{:S(2)}, u32[]{:S(2)}) collective-permute-start(f32[21,256,256]{2,1,0:T(8,128)} %gram.1.own), channel_id=1, source_target_pairs={{0,1},{1,0},{2,3},{3,2},{4,5},{5,4},{6,7},{7,6},{8,9},{9,8},{10,11... | collective-permute-start | bytes 16515080 | tf_op jit(solution)/shard_map/ppermute | solution.py:185
  171.3 9.2 %collective-permute-start.4 = (f32[21,256,256]{2,1,0:T(8,128)}, f32[21,256,256]{2,1,0:T(8,128)S(1)}, u32[]{:S(2)}, u32[]{:S(2)}) collective-permute-start(f32[21,256,256]{2,1,0:T(8,128)} %get-tuple-element.31.own), channel_id=1, source_target_pairs={{0,1},{1,0},{2,3},{3,2},{4,5},{5,4},{6,7},{7,6},{8,9},{9,8},{10,11... | collective-permute-start | bytes 16515080 | tf_op jit(solution)/shard_map/ppermute | solution.py:185
  202.8 87.4 %all-to-all-start.2 = ((bf16[16,96,768]{2,1,0:T(8,128)(2,1)}), bf16[16,96,768]{2,1,0:T(8,128)(2,1)S(1)}, u32[]{:S(2)}, u32[]{:S(2)}) async-start(bf16[16,96,768]{2,1,0:T(8,128)(2,1)} %bitcast.41), calls=%async_computation.2 | async-start | bytes 4718592 | tf_op jit(solution)/shard_map/all_to_all | solution.py:505
  236.1 8.8 %copy-start.16 = (pred[16]{0:T(512)(128)(4,1)S(1)}, pred[16]{0:T(512)(128)(4,1)}, u32[]{:S(2)}) copy-start(pred[16]{0:T(512)(128)(4,1)} %constant.69.clone) | copy-start | bytes 52
  236.1 9.4 %copy-start.15 = (pred[16]{0:T(512)(128)(4,1)S(1)}, pred[16]{0:T(512)(128)(4,1)}, u32[]{:S(2)}) copy-start(pred[16]{0:T(512)(128)(4,1)} %constant.70.clone) | copy-start | bytes 52
  241.6 4.5 collective-permute-start.6
  242.3 36.7 %collective-permute-start.7 = (bf16[1536,256]{1,0:T(8,128)(2,1)}, bf16[1536,256]{1,0:T(8,128)(2,1)S(1)}, u32[]{:S(2)}, u32[]{:S(2)}) collective-permute-start(bf16[1536,256]{1,0:T(8,128)(2,1)} %get-tuple-element.37), channel_id=1, source_target_pairs={{8,12},{18,22},{14,10},{20,16},{2,6},{24,28},{9,13},{19,23},{15,11... | collective-permute-start | bytes 2359304 | tf_op jit(solution)/shard_map/ppermute | solution.py:513
  243.6 41.0 %collective-permute-start.5 = (bf16[1536,256]{1,0:T(8,128)(2,1)}, bf16[1536,256]{1,0:T(8,128)(2,1)S(1)}, u32[]{:S(2)}, u32[]{:S(2)}) collective-permute-start(bf16[1536,256]{1,0:T(8,128)(2,1)} %get-tuple-element.35), channel_id=1, source_target_pairs={{8,10},{18,16},{14,12},{20,22},{2,0},{24,26},{9,11},{19,17},{15,13... | collective-permute-start | bytes 2359304 | tf_op jit(solution)/shard_map/ppermute | solution.py:513
  290.1 32.3 %copy-start.5 = (f32[1344]{0:T(1024)S(1)}, f32[1344]{0:T(1024)}, u32[]{:S(2)}) copy-start(f32[1344]{0:T(1024)} %param.35) | copy-start | bytes 16132
  290.2 32.3 %copy-start.6 = (f32[1344]{0:T(1024)S(1)}, f32[1344]{0:T(1024)}, u32[]{:S(2)}) copy-start(f32[1344]{0:T(1024)} %param.36) | copy-start | bytes 16132
  290.2 33.7 %copy-start.2 = (f32[128,768]{1,0:T(8,128)S(1)}, f32[128,768]{1,0:T(8,128)}, u32[]{:S(2)}) copy-start(f32[128,768]{1,0:T(8,128)} %param.42) | copy-start | bytes 1179652
  290.2 33.7 %copy-start.3 = (f32[128,768]{1,0:T(8,128)S(1)}, f32[128,768]{1,0:T(8,128)}, u32[]{:S(2)}) copy-start(f32[128,768]{1,0:T(8,128)} %param.40) | copy-start | bytes 1179652
  290.2 33.7 %copy-start.4 = (f32[128,768]{1,0:T(8,128)S(1)}, f32[128,768]{1,0:T(8,128)}, u32[]{:S(2)}) copy-start(f32[128,768]{1,0:T(8,128)} %param.39) | copy-start | bytes 1179652
  290.2 36.1 %copy-start = (bf16[16,96,768]{2,1,0:T(8,128)(2,1)}, bf16[16,96,768]{2,1,0:T(8,128)(2,1)S(1)}, u32[]{:S(2)}) copy-start(bf16[16,96,768]{2,1,0:T(8,128)(2,1)S(1)} %all-to-all-done.2.source.first) | copy-start | bytes 7077892
  290.2 124.1 %all-to-all-start.3 = ((bf16[16,96,512]{2,1,0:T(8,128)(2,1)}), bf16[16,96,512]{2,1,0:T(8,128)(2,1)}, u32[]{:S(2)}, u32[]{:S(2)}) async-start(bf16[16,96,512]{2,1,0:T(8,128)(2,1)} %bitcast.40), calls=%async_computation.3 | async-start | bytes 3145728 | tf_op jit(solution)/shard_map/all_to_all | solution.py:505
  323.8 52.2 %copy-start.8 = (s32[6]{0:T(128)S(1)}, s32[6]{0:T(128)}, u32[]{:S(2)}) copy-start(s32[6]{0:T(128)} %select_reduce_fusion) | copy-start | bytes 76
  323.9 52.2 %copy-start.9 = (s32[8]{0:T(128)S(1)}, s32[8]{0:T(128)}, u32[]{:S(2)}) copy-start(s32[8]{0:T(128)} %select_reduce_fusion.1) | copy-start | bytes 100
  (7 other events, 38.2 us)

commit v4 on v3

--- a/solution.py
+++ b/solution.py
@@ -105,22 +105,26 @@
         self.idle = [c for c in range(chips) if c not in self.heavy and c not in self.light]
 
 
-def prepare_kernel(plan, cores, sg, ss, wg, ws, sn, wn, first, second):
+def prepare_kernel(plan, cores, sg, ss, wg, ws, sn, wn, first, second, sv, wv):
     narrow_tiles = D // cores // LANE
     wide_tiles = FF // cores // LANE
-    square_next = MOMENTUM * ss[...] + sg[...]
-    sn[...] = square_next
-    swiglu_next = MOMENTUM * ws[...] + wg[...]
-    wn[...] = swiglu_next
-
-    def piece(grad, state, row_tile, slot):
-        g = grad[:, row_tile, slot, :]
-        return (g + MOMENTUM * (MOMENTUM * state[:, row_tile, slot, :] + g)).astype(jnp.bfloat16)
+    for grad, state, following, sent in ((wg, ws, wn, wv), (sg, ss, sn, sv)):
+
+        def row(r, carry):
+            after = MOMENTUM * state[r] + grad[r]
+            following[r] = after
+            sent[r] = grad[r] + MOMENTUM * after
+            return carry
+
+        lax.fori_loop(0, grad.shape[0], row, 0)
+
+    def piece(sent, row_tile, slot):
+        return sent[:, row_tile, slot, :].astype(jnp.bfloat16)
 
     for j, owner in enumerate(plan.heavy):
         for core in range(cores):
             for t in range(wide_tiles):
-                value = piece(wg, ws, core * wide_tiles + t, j)
+                value = piece(wv, core * wide_tiles + t, j)
                 if t < narrow_tiles:
                     first[owner * cores + core, :, t * LANE : (t + 1) * LANE] = value
                 else:
@@ -131,7 +135,7 @@
     for j, owner in enumerate(plan.light):
         for core in range(cores):
             for t in range(narrow_tiles):
-                value = piece(sg, ss, core * narrow_tiles + t, j)
+                value = piece(sv, core * narrow_tiles + t, j)
                 first[owner * cores + core, :, t * LANE : (t + 1) * LANE] = value
     for chip in range(len(plan.is_heavy)):
         for core in range(cores):
@@ -175,6 +179,10 @@
             jax.ShapeDtypeStruct((devices, rows, narrow), jnp.bfloat16),
             jax.ShapeDtypeStruct((devices, rows, 2 * GRANULE), jnp.bfloat16),
         ],
+        scratch_shapes=[
+            pltpu.VMEM((chunk, D // LANE, square_count, LANE), jnp.float32),
+            pltpu.VMEM((chunk, FF // LANE, swiglu_count, LANE), jnp.float32),
+        ],
         compiler_params=pltpu.CompilerParams(vmem_limit_bytes=56 * 1024 * 1024),
         name="prepare",
     )(tiles(square_grad, D), tiles(square_state, D), tiles(swiglu_grad, FF), tiles(swiglu_state, FF))
@@ -189,47 +197,61 @@
 EDGE = D // BLOCK
 NEAR = EDGE // 2
 PACKED = EDGE * NEAR + NEAR
-VMEM_LIMIT = 58 * 1024 * 1024
-
-
-def each_pair(body):
+GROUPS = EDGE + 1
+MIB = 1024 * 1024
+
+
+def each_pair(body, after=None):
     def row(i, carry):
         for d in range(NEAR):
             j = lax.rem(i + d, EDGE)
             body(i * NEAR + d, i, j, d == 0)
+        if after is not None:
+            after(i)
         return carry
 
     lax.fori_loop(0, EDGE, row, 0)
-
-    def far(i, carry):
+    for i in range(NEAR):
         body(EDGE * NEAR + i, i, i + NEAR, False)
-        return carry
-
-    lax.fori_loop(0, NEAR, far, 0)
+    if after is not None:
+        after(EDGE)
 
 
 def span(i):
+    if isinstance(i, int):
+        return pl.ds(i * BLOCK, BLOCK)
     return pl.ds(pl.multiple_of(i * BLOCK, BLOCK), BLOCK)
 
 
-def nt(a, b):
-    return lax.dot_general(a, b, (((1,), (1,)), ((), ())), preferred_element_type=jnp.float32)
-
-
-def gram_blocks(parts, out):
+def group(ref, g):
+    return ref.at[pl.ds(g * NEAR, NEAR)]
+
+
+def rows_of(ref, i):
+    return ref.at[span(i), :]
+
+
+def columns_of(ref, at, width):
+    return ref.at[:, pl.ds(at, width)]
+
+
+def gram_blocks(x, width, out, after):
     def body(slot, i, j, diagonal):
-        total = nt(parts[0][span(i), :], parts[0][span(j), :])
-        for part in parts[1:]:
-            total += nt(part[span(i), :], part[span(j), :])
-        out[slot] = total
-
-    each_pair(body)
+        out[slot] = lax.dot_general(
+            x[span(i), :width],
+            x[span(j), :width],
+            (((1,), (1,)), ((), ())),
+            preferred_element_type=jnp.float32,
+        )
+
+    each_pair(body, after)
 
 
 def mirror(out, i, j, diagonal, value):
-    out[span(i), span(j)] = value.astype(out.dtype)
+    rounded = value.astype(out.dtype)
+    out[span(i), span(j)] = rounded
     if not diagonal:
-        out[span(j), span(i)] = value.T.astype(out.dtype)
+        out[span(j), span(i)] = rounded.T
 
 
 def polynomial_blocks(normed, out):
@@ -241,109 +263,216 @@
     each_pair(body)
 
 
-def mixed_rows(polynomial, part, scale, targets):
+def mixed_rows(polynomial, x, width, scale, out, before=None, after=None):
     def row(i, carry):
-        at = 0
-        for target in targets:
-            for c in range(0, target.shape[1], BLOCK):
-                columns = slice(at, at + BLOCK)
-                product = jnp.dot(
-                    polynomial[span(i), :], part[:, columns], preferred_element_type=jnp.float32
-                )
-                mixed = QUINTIC_LINEAR * part[span(i), columns].astype(jnp.float32) + product
-                target[span(i), c : c + BLOCK] = (mixed * scale).astype(target.dtype)
-                at += BLOCK
+        if before is not None:
+            before(i)
+        for c in range(0, width, BLOCK):
+            product = jnp.dot(
+                polynomial[span(i), :], x[:, c : c + BLOCK], preferred_element_type=jnp.float32
+            )
+            mixed = QUINTIC_LINEAR * x[span(i), c : c + BLOCK].astype(jnp.float32) + product
+            out[span(i), c : c + BLOCK] = (mixed * scale).astype(out.dtype)
+        if after is not None:
+            after(i)
         return carry
 
     lax.fori_loop(0, EDGE, row, 0)
 
 
-def gram_kernel(flag, first, second, *rest):
-    relayed, out = rest[:-1], rest[-1]
-    heavy = flag[0] > 0
-
-    @pl.when(heavy)
+def column_copies(sources, x, sems):
+    copies, at = [], 0
+    for k, source in enumerate(sources):
+        width = source.shape[1]
+        copies.append(pltpu.make_async_copy(source, columns_of(x, at, width), sems.at[k]))
+        at += width
+    return copies
+
+
+def start_all(copies):
+    for copy in copies:
+        copy.start()
+
+
+def wait_all(copies):
+    for copy in copies:
+        copy.wait()
+
+
+def by_kind(flag, narrow, wide, body):
+    @pl.when(flag[0] > 0)
     def _():
-        gram_blocks([first, second, *relayed], out)
-
-    @pl.when(jnp.logical_not(heavy))
+        body(wide)
+
+    @pl.when(flag[0] <= 0)
     def _():
-        gram_blocks([first], out)
-
-
-def middle_kernel(flag, own, other, first, second, *rest):
-    count = len(rest) - 6
-    relayed = rest[:count]
-    first_out, second_out, packed, scale_out, normed, polynomial = rest[count:]
-    heavy = flag[0] > 0
-
-    def add(slot, total):
-        gram = own[slot] + other[slot]
-        packed[slot] = gram
-        return total + jnp.sum(gram * gram)
-
-    def row(i, carry):
-        once, twice = carry
-        once = add(i * NEAR, once)
-        for d in range(1, NEAR):
-            twice = add(i * NEAR + d, twice)
-        return once, twice
-
-    once, twice = lax.fori_loop(0, EDGE, row, (jnp.float32(0.0), jnp.float32(0.0)))
-    twice = lax.fori_loop(0, NEAR, lambda i, t: add(EDGE * NEAR + i, t), twice)
-    total = jnp.full((8, LANE), once + 2.0 * twice, jnp.float32)
+        body(narrow)
+
+
+def gram_kernel(flag, *refs):
+    parts, (out, x, blocks, in_sems, out_sems) = refs[:-5], refs[-5:]
+    copies = column_copies(parts, x, in_sems)
+
+    def send(g):
+        pltpu.make_async_copy(group(blocks, g), group(out, g), out_sems.at[g]).start()
+
+    def run(width):
+        used = copies[: 1 if width < x.shape[1] else len(copies)]
+        start_all(used)
+        wait_all(used)
+        gram_blocks(x, width, blocks, send)
+
+    by_kind(flag, parts[0].shape[1], x.shape[1], run)
+    wait_all(
+        [
+            pltpu.make_async_copy(group(blocks, g), group(out, g), out_sems.at[g])
+            for g in range(GROUPS)
+        ]
+    )
+
+
+def group_copies(source, target, sems):
+    return [
+        pltpu.make_async_copy(group(source, g), group(target, g), sems.at[g]) for g in range(GROUPS)
+    ]
+
+
+def middle_kernel(flag, own_in, other_in, *refs):
+    parts, refs = refs[:-15], refs[-15:]
+    first_out, second_out, packed_out, scale_out = refs[:4]
+    own, other, x, mixed, normed, polynomial = refs[4:10]
+    own_sems, other_sems, x_sems, mixed_sems, packed_sems = refs[10:]
+    narrow, wide = first_out.shape[1], x.shape[1]
+    own_copies = group_copies(own_in, own, own_sems)
+    other_copies = group_copies(other_in, other, other_sems)
+    x_copies = column_copies(parts, x, x_sems)
+    for a, b in zip(own_copies, other_copies):
+        a.start()
+        b.start()
+    by_kind(flag, 1, len(x_copies), lambda used: start_all(x_copies[:used]))
+
+    once = jnp.zeros((8, BLOCK), jnp.float32)
+    twice = jnp.zeros((8, BLOCK), jnp.float32)
+    for g in range(GROUPS):
+        own_copies[g].wait()
+        other_copies[g].wait()
+        for d in range(NEAR):
+            slot = g * NEAR + d
+            gram = own[slot] + other[slot]
+            own[slot] = gram
+            squares = jnp.sum((gram * gram).reshape(BLOCK // 8, 8, BLOCK), axis=0)
+            if d == 0 and g < EDGE:
+                once += squares
+            else:
+                twice += squares
+    total = jnp.full((8, LANE), jnp.sum(once + 2.0 * twice), jnp.float32)
     scale = jnp.sqrt(total) + 1e-06
     scale_out[...] = scale
     inverse = (1.0 / scale)[0:1, 0:1]
     root = (1.0 / jnp.sqrt(scale))[0:1, 0:1]
-
-    def norm(slot, i, j, diagonal):
-        mirror(normed, i, j, diagonal, packed[slot] * inverse)
-
-    each_pair(norm)
+    each_pair(lambda slot, i, j, diagonal: mirror(normed, i, j, diagonal, own[slot] * inverse))
     polynomial_blocks(normed, polynomial)
-    mixed_rows(polynomial, first, root, [first_out])
-
-    @pl.when(heavy)
-    def _():
-        at = 0
-        for part in (second, *relayed):
-            width = part.shape[1]
-            mixed_rows(polynomial, part, root, [second_out.at[:, at : at + width]])
+
+    def send(g):
+        pltpu.make_async_copy(group(other, g), group(packed_out, g), packed_sems.at[g]).start()
+
+    def run(width):
+        used = x_copies[: 1 if width < wide else len(x_copies)]
+        wait_all(used)
+        mixed_rows(polynomial, x, width, root, mixed)
+        sends = [pltpu.make_async_copy(columns_of(mixed, 0, narrow), first_out, mixed_sems.at[0])]
+        if width == wide:
+            rest = columns_of(mixed, narrow, wide - narrow)
+            sends.append(pltpu.make_async_copy(rest, second_out, mixed_sems.at[1]))
+        start_all(sends)
+        gram_blocks(mixed, width, other, send)
+        wait_all(sends)
+
+    by_kind(flag, narrow, wide, run)
+    wait_all(group_copies(other, packed_out, packed_sems))
+
+
+def last_kernel(factor, own_in, other_in, x_in, polynomial_out, out, *refs):
+    own, other, x, mixed, normed, polynomial = refs[:6]
+    own_sems, other_sems, x_sem, polynomial_sem, out_sems = refs[6:]
+    own_copies = group_copies(own_in, own, own_sems)
+    other_copies = group_copies(other_in, other, other_sems)
+    for a, b in zip(own_copies, other_copies):
+        a.start()
+        b.start()
+    x_copy = pltpu.make_async_copy(x_in, x, x_sem)
+    x_copy.start()
+    for g in range(GROUPS):
+        own_copies[g].wait()
+        other_copies[g].wait()
+        for d in range(NEAR):
+            slot = g * NEAR + d
+            i, j = (g, (g + d) % EDGE) if g < EDGE else (d, d + NEAR)
+            mirror(normed, i, j, i == j, own[slot] + other[slot])
+    polynomial_blocks(normed, polynomial)
+    polynomial_copy = pltpu.make_async_copy(polynomial, polynomial_out, polynomial_sem)
+    polynomial_copy.start()
+    x_copy.wait()
+
+    def out_copy(i):
+        return pltpu.make_async_copy(rows_of(mixed, i), rows_of(out, i), out_sems.at[i])
+
+    mixed_rows(
+        polynomial, x, x.shape[1], factor[0], mixed, after=lambda i: out_copy(i).start()
+    )
+    wait_all([out_copy(i) for i in range(EDGE)])
+    polynomial_copy.wait()
+
+
+def rest_kernel(flag, factor, polynomial_in, x_in, *refs):
+    outs, (x, mixed, polynomial, x_sem, polynomial_sems, out_sems) = refs[:-6], refs[-6:]
+    x_copy = pltpu.make_async_copy(x_in, x, x_sem)
+
+    def polynomial_copy(i):
+        return pltpu.make_async_copy(
+            rows_of(polynomial_in, i), rows_of(polynomial, i), polynomial_sems.at[i]
+        )
+
+    def out_copies(i):
+        copies, at = [], 0
+        for k, out in enumerate(outs):
+            width = out.shape[1]
+            source = mixed.at[span(i), pl.ds(at, width)]
+            copies.append(pltpu.make_async_copy(source, rows_of(out, i), out_sems.at[k, i]))
             at += width
-        gram_blocks([first_out, second_out], packed)
-
-    @pl.when(jnp.logical_not(heavy))
-    def _():
-        gram_blocks([first_out], packed)
-
-
-def last_kernel(factor, own, other, first, polynomial, out, normed):
-    def norm(slot, i, j, diagonal):
-        mirror(normed, i, j, diagonal, own[slot] + other[slot])
-
-    each_pair(norm)
-    polynomial_blocks(normed, polynomial)
-    mixed_rows(polynomial, first, factor[0], [out])
-
-
-def rest_kernel(flag, factor, polynomial, second, *outs):
+        return copies
+
     @pl.when(flag[0] > 0)
     def _():
-        mixed_rows(polynomial, second, factor[0], outs)
-
-
-def call(kernel, name, scalars, arrays, outs, scratch=(), flops=0):
+        x_copy.start()
+        start_all([polynomial_copy(i) for i in range(EDGE)])
+        x_copy.wait()
+        mixed_rows(
+            polynomial,
+            x,
+            x.shape[1],
+            factor[0],
+            mixed,
+            before=lambda i: polynomial_copy(i).wait(),
+            after=lambda i: start_all(out_copies(i)),
+        )
+        for i in range(EDGE):
+            wait_all(out_copies(i))
+
+
+def call(kernel, name, scalars, arrays, outs, scratch, limit, flops, small_outs=0):
     moved = sum(x.size * x.dtype.itemsize for x in arrays)
     moved += sum(math.prod(o.shape) * o.dtype.itemsize for o in outs)
     smem = pl.BlockSpec(memory_space=pltpu.SMEM)
+    anywhere = pl.BlockSpec(memory_space=pl.ANY)
+    vmem = pl.BlockSpec(memory_space=pltpu.VMEM)
     return pl.pallas_call(
         kernel,
-        in_specs=[smem] * len(scalars) + [pl.BlockSpec(memory_space=pltpu.VMEM)] * len(arrays),
-        out_specs=[pl.BlockSpec(memory_space=pltpu.VMEM)] * len(outs),
+        in_specs=[smem] * len(scalars) + [anywhere] * len(arrays),
+        out_specs=[anywhere] * (len(outs) - small_outs) + [vmem] * small_outs,
         out_shape=list(outs),
         scratch_shapes=list(scratch),
-        compiler_params=pltpu.CompilerParams(vmem_limit_bytes=VMEM_LIMIT),
+        compiler_params=pltpu.CompilerParams(vmem_limit_bytes=limit * MIB),
         cost_estimate=pl.CostEstimate(flops=flops, bytes_accessed=moved, transcendentals=0),
         name=name,
     )(*scalars, *arrays)
@@ -351,64 +480,72 @@
 
 def assemble_squares(plan, square_order, first_back):
     count = square_order.shape[0]
-
-    def kernel(order, source, out, sems):
-        copies = [
-            pltpu.make_async_copy(source.at[plan.light[j]], out.at[order[j]], sems.at[j])
-            for j in range(count)
-        ]
-        for copy in copies:
-            copy.start()
-        for copy in copies:
-            copy.wait()
+    shape = first_back.shape[1:]
+
+    def kernel(order, chip_of, source, out):
+        out[...] = source[...]
 
     return pl.pallas_call(
         kernel,
-        in_specs=[pl.BlockSpec(memory_space=pltpu.SMEM), pl.BlockSpec(memory_space=pl.ANY)],
-        out_specs=pl.BlockSpec(memory_space=pl.ANY),
-        out_shape=jax.ShapeDtypeStruct((count,) + first_back.shape[1:], jnp.bfloat16),
-        scratch_shapes=[pltpu.SemaphoreType.DMA((count,))],
+        grid_spec=pltpu.PrefetchScalarGridSpec(
+            num_scalar_prefetch=2,
+            grid=(count,),
+            in_specs=[pl.BlockSpec((1,) + shape, lambda j, order, chip_of: (chip_of[j], 0, 0))],
+            out_specs=pl.BlockSpec((1,) + shape, lambda j, order, chip_of: (order[j], 0, 0)),
+        ),
+        out_shape=jax.ShapeDtypeStruct((count,) + shape, jnp.bfloat16),
         name="assemble_squares",
-    )(square_order, first_back)
+    )(square_order, jnp.asarray(plan.light, jnp.int32), first_back)
 
 
 def assemble_swiglu(plan, swiglu_order, first_back, second_back):
     count = swiglu_order.shape[0]
-    narrow = first_back.shape[2]
-    rows = first_back.shape[1]
+    rows, narrow = first_back.shape[1:]
     wide = narrow + plan.granules * GRANULE
-
-    def kernel(order, first, second, out, sems):
-        copies = []
-
-        def move(source, j, at, width):
-            copies.append(
-                pltpu.make_async_copy(
-                    source, out.at[order[j], :, pl.ds(at, width)], sems.at[len(copies)]
-                )
-            )
-
-        for j in range(count):
-            owner = plan.heavy[j]
-            move(first.at[owner], j, 0, narrow)
-            move(second.at[owner], j, narrow, 2 * GRANULE)
-            for b in range(2, plan.granules):
-                chip, where = plan.place[(j, b)]
-                source = second.at[chip, :, pl.ds(where * GRANULE, GRANULE)]
-                move(source, j, narrow + b * GRANULE, GRANULE)
-        for copy in copies:
-            copy.start()
-        for copy in copies:
-            copy.wait()
+    extra = range(2, plan.granules)
+    chips = [plan.heavy[j] for j in range(count)]
+    places = [plan.place[(j, b)] for b in extra for j in range(count)]
+    table = np.array(chips + [c for c, _ in places] + [w for _, w in places], np.int32)
+
+    def kernel(order, where, first, own, *refs):
+        out = refs[-1]
+        out[0, :, :narrow] = first[0]
+        out[0, :, narrow : narrow + 2 * GRANULE] = own[0]
+        for k, ref in enumerate(refs[:-1]):
+            at = narrow + (2 + k) * GRANULE
+            out[0, :, at : at + GRANULE] = ref[0]
+
+    def granule(k):
+        def index(j, order, where):
+            at = (1 + k) * count + j
+            return where[at], 0, where[len(extra) * count + at]
+
+        return pl.BlockSpec((1, rows, GRANULE), index)
 
     return pl.pallas_call(
         kernel,
-        in_specs=[pl.BlockSpec(memory_space=pltpu.SMEM)] + [pl.BlockSpec(memory_space=pl.ANY)] * 2,
-        out_specs=pl.BlockSpec(memory_space=pl.ANY),
+        grid_spec=pltpu.PrefetchScalarGridSpec(
+            num_scalar_prefetch=2,
+            grid=(count,),
+            in_specs=[
+                pl.BlockSpec((1, rows, narrow), lambda j, order, where: (where[j], 0, 0)),
+                pl.BlockSpec((1, rows, 2 * GRANULE), lambda j, order, where: (where[j], 0, 0)),
+            ]
+            + [granule(k) for k in range(len(extra))],
+            out_specs=pl.BlockSpec((1, rows, wide), lambda j, order, where: (order[j], 0, 0)),
+        ),
         out_shape=jax.ShapeDtypeStruct((count, rows, wide), jnp.bfloat16),
-        scratch_shapes=[pltpu.SemaphoreType.DMA((count * plan.granules,))],
         name="assemble_swiglu",
-    )(swiglu_order, first_back, second_back)
+    )(swiglu_order, jnp.asarray(table), first_back, *([second_back] * (1 + len(extra))))
+
+
+def spread(value, chips, chip):
+    known = jnp.where(jnp.arange(chips, dtype=jnp.int32) == chip, value, 0.0)
+    step = 1
+    while step < chips:
+        known = known + lax.ppermute(known, "dp", [(s, s ^ step) for s in range(chips)])
+        step *= 2
+    return known
 
 
 def lookup(table, positions):
@@ -468,28 +605,49 @@
     extra = plan.granules * GRANULE
     second_shape = jax.ShapeDtypeStruct((D, extra), jnp.bfloat16)
     square_buffer = pltpu.VMEM((D, D), jnp.bfloat16)
+    packed_buffer = pltpu.VMEM(packed.shape, jnp.float32)
+    matrix_buffer = pltpu.VMEM((D, narrow + extra), jnp.bfloat16)
+    first_buffer = pltpu.VMEM((D, narrow), jnp.bfloat16)
+    second_buffer = pltpu.VMEM((D, extra), jnp.bfloat16)
+    sems = lambda *shape: pltpu.SemaphoreType.DMA(shape)
     half = D * D * (narrow + extra)
+    parts = [first_got, second_got, *relayed]
     (own,) = call(
-        gram_kernel, "gram", [flag], [first_got, second_got, *relayed], [packed], flops=half
+        gram_kernel,
+        "gram",
+        [flag],
+        parts,
+        [packed],
+        [matrix_buffer, packed_buffer, sems(len(parts)), sems(GROUPS)],
+        18,
+        half,
     )
     first_mid, second_mid, own_mid, scale = call(
         middle_kernel,
         "middle",
         [flag],
-        [own, other_core(own), first_got, second_got, *relayed],
+        [own, other_core(own), *parts],
         [first_shape, second_shape, packed, jax.ShapeDtypeStruct((8, LANE), jnp.float32)],
-        [square_buffer, square_buffer],
-        flops=3 * half + D * D * D,
-    )
-    logs = lax.all_gather(scale, "dp")
+        [packed_buffer] * 2
+        + [matrix_buffer] * 2
+        + [square_buffer] * 2
+        + [sems(GROUPS), sems(GROUPS), sems(len(parts)), sems(2), sems(GROUPS)],
+        44,
+        3 * half + D * D * D,
+        small_outs=1,
+    )
     polynomial, first_done = call(
         last_kernel,
         "last",
         [factor],
         [own_mid, other_core(own_mid), first_mid],
         [whole_square, first_shape],
-        [square_buffer],
-        flops=D * D * D + 2 * D * D * narrow,
+        [packed_buffer] * 2
+        + [first_buffer] * 2
+        + [square_buffer] * 2
+        + [sems(GROUPS), sems(GROUPS), sems(), sems(), sems(EDGE)],
+        34,
+        D * D * D + 2 * D * D * narrow,
     )
     piece_shape = jax.ShapeDtypeStruct((D, GRANULE), jnp.bfloat16)
     rest = call(
@@ -498,8 +656,11 @@
         [flag, factor],
         [polynomial, second_mid],
         [jax.ShapeDtypeStruct((D, 2 * GRANULE), jnp.bfloat16)] + [piece_shape] * plan.passes,
-        flops=2 * D * D * extra,
-    )
+        [second_buffer] * 2 + [square_buffer, sems(), sems(EDGE), sems(1 + plan.passes, EDGE)],
+        20,
+        2 * D * D * extra,
+    )
+    logs = spread(0.5 * jnp.log(scale[0, 0]), chips, chip)
 
     def send_back(x):
         return lax.all_to_all(
@@ -531,7 +692,7 @@
     slot_owner = jnp.concatenate(
         [lookup(owners[:square_count], square_order), lookup(owners[square_count:], swiglu_order)]
     )
-    slot_logs = 0.5 * jnp.log(logs[:, 0, 0])[slot_chips]
+    slot_logs = logs[slot_chips]
     owner_norms = jnp.sum(jnp.where(slot_owner == chip, slot_logs, 0.0)).reshape(1)
 
     vector_step, first_vector, second_vector = adamw_terms(

time: 491 us -> 344 us (0.70)
  Pallas kernels: 196 us -> 67.8 us
  blocking collectives: 91.7 us -> 42.9 us
  waiting for transfers between devices: 98.4 us -> 122 us
  local copies, waits for them, and re-layouts: 10.7 us -> 20.4 us
  other arithmetic: 15.5 us -> 10.4 us
    pallas_call x6, Pallas kernels: 175 us -> 53.4 us  [the longest x4 41.8 us: call(): pl.pallas_call(kernel, in_specs=[smem] * len(scalars) + [anywhere] * len(...]
    all_gather x1 -> x0, blocking collectives: 48.9 us -> none  [local(): logs = lax.all_gather(scale, 'dp')]
    ppermute x0 -> x4, waiting for transfers between devices: none -> 22.4 us  [spread(): lax.ppermute(known, 'dp', [(s, s ^ step) for s in range(chips)])]
    unnamed x41 -> x48, local copies, waits for them, and re-layouts: 5.02 us -> 16.3 us
    all_to_all x2, starting transfers between devices: 59.5 us -> 53.2 us  [send_back(): lax.all_to_all(x.reshape(chips, chip_rows, -1), 'dp', split_axis=0, conca...]
    pallas_call x1, Pallas kernels: 20.7 us -> 14.4 us  [prepare(): pl.pallas_call(lambda *refs: prepare_kernel(plan, cores, *refs), grid=(ro...]
    ppermute x0 -> x4, starting transfers between devices: none -> 5.52 us  [spread(): lax.ppermute(known, 'dp', [(s, s ^ step) for s in range(chips)])]
  transfers between devices with their start and end apart: 11 -> 15, of which waited for: 6 -> 11; matrix products, arithmetic and copies ran while one was open for 4% -> 4% of each run, Pallas kernels for 9% -> 2%
where the time goes in v4:
time: 344 us; the launch traced here: 339 us
  waiting for transfers between devices  122 us (35%)
  starting transfers between devices  73 us (21%)
  Pallas kernels  67.8 us (20%)
  blocking collectives  42.9 us (12%)
  local copies, waits for them, and re-layouts  20.4 us (6%)
  other arithmetic  10.4 us (3%)
    all_to_all x2, starting transfers between devices, send_back(): lax.all_to_all(x.reshape(chips, chip_rows, -1), 'dp', split_axis=0, conca...  53.2 us
    all_to_all x1, blocking collectives, local(): lax.all_to_all(second_send.reshape(D, 2 * GRANULE), both, split_axis=0, c...  42.9 us
    pallas_call x4, Pallas kernels, call(): pl.pallas_call(kernel, in_specs=[smem] * len(scalars) + [anywhere] * len(...  41.8 us
    ppermute x3, waiting for transfers between devices, local(): handed.append(lax.ppermute(rest[1 + p], 'dp', pairs))  39.3 us
    ppermute x3, waiting for transfers between devices, local(): lax.ppermute(jnp.where(pick, pieces[1], pieces[0]), 'dp', pairs)  30.1 us
    ppermute x4, waiting for transfers between devices, spread(): lax.ppermute(known, 'dp', [(s, s ^ step) for s in range(chips)])  22.4 us
    ppermute x2, waiting for transfers between devices, other_core(): return lax.ppermute(x, 'tensor', [(0, 1), (1, 0)])  17.5 us
    unnamed x48, local copies, waits for them, and re-layouts  16.3 us
  transfers between devices with their start and end apart: 15, of which 11 were waited for; matrix products, arithmetic and copies ran while one was open for 4% of the time, Pallas kernels for 2%

profile of v4, /device:TPU:12, one launch (start us, length us, event | category | flops | bytes accessed | tf_op | source)
XLA Modules:
  0.0 339.3 jit_solution(15163391655461803419)
XLA Ops:
  0.6 14.4 %prepare.1 = (f32[48,12,8,128]{3,2,1,0:T(8,128)}, f32[48,32,6,128]{3,2,1,0:T(8,128)}, bf16[32,48,768]{2,1,0:T(8,128)(2,1)}, bf16[32,48,512]{2,1,0:T(8,128)(2,1)}) custom-call(f32[48,12,8,128]{3,2,1,0:T(8,128)} %bitcast.39, f32[48,12,8,128]{3,2,1,0:T(8,128)} %bitcast.40, f32[48,32,6,128]{3,2,1,0:T(8,128)} %bitcast.36, f32[48,32,6,128]{3,2,1,0:T(8,128)} %bitcast.37), custom_call_target="tpu_custom_call" | custom-call | tf_op jit(solution)/shard_map/prepare/pallas_call | solution.py:166
  15.1 42.9 %all_to_all.26 = bf16[32,48,512]{2,1,0:T(8,128)(2,1)S(1)} all-to-all(bf16[32,48,512]{2,1,0:T(8,128)(2,1)} %get-tuple-element.30), channel_id=1, replica_groups=mesh['dp'=16,'tensor'=2] {'dp','tensor'}, dimensions={0} | all-to-all | bytes 3145728 | tf_op jit(solution)/shard_map/all_to_all | solution.py:587
  57.9 4.7 %all-to-all-start = ((bf16[32,48,768]{2,1,0:T(8,128)(2,1)}), bf16[32,48,768]{2,1,0:T(8,128)(2,1)}, u32[]{:S(2)}, u32[]{:S(2)}) async-start(bf16[32,48,768]{2,1,0:T(8,128)(2,1)} %get-tuple-element.29), calls=%async_computation | async-start | bytes 4718592 | tf_op jit(solution)/shard_map/all_to_all | solution.py:590
  65.3 2.5 collective-permute-start
  68.5 2.8 collective-permute-start.2
  72.6 30.1 %collective-permute-done.refs_2_ = bf16[1536,256]{1,0:T(8,128)(2,1)S(1)} collective-permute-done((bf16[1536,256]{1,0:T(8,128)(2,1)S(1)}, bf16[1536,256]{1,0:T(8,128)(2,1)S(1)}, u32[]{:S(2)}, u32[]{:S(2)}) %collective-permute-start) | collective-permute-done | bytes 786464 | tf_op jit(solution)/shard_map/ppermute | solution.py:599
  103.6 11.2 %all-to-all-done = bf16[32,48,768]{2,1,0:T(8,128)(2,1)} async-done(((bf16[32,48,768]{2,1,0:T(8,128)(2,1)}), bf16[32,48,768]{2,1,0:T(8,128)(2,1)}, u32[]{:S(2)}, u32[]{:S(2)}) %all-to-all-start) | async-done | bytes 2359328 | tf_op jit(solution)/shard_map/all_to_all | solution.py:590
  115.9 5.8 %gram.1.own_in = f32[21,256,256]{2,1,0:T(8,128)S(1)} custom-call(s32[1]{0:T(128)S(6)} %convert_element_type.7.flag, bf16[1536,768]{1,0:T(8,128)(2,1)} %bitcast.13.refs_0_, bf16[1536,512]{1,0:T(8,128)(2,1)S(1)} %bitcast.34, bf16[1536,256]{1,0:T(8,128)(2,1)S(1)} %collective-permute-done.refs_2_, bf16[1536,256]{1,0:T(8,128)(2,1)S(1)} %collective-permute-done.1.refs_3_, ...), custom_call_target="tpu_custom_call" | custom-call | flops 4831838208 | bytes 11796480 | tf_op jit(solution)/shard_map/gram/pallas_call | solution.py:469
  121.8 9.0 %collective-permute-done.3.other_in = f32[21,256,256]{2,1,0:T(8,128)S(1)} collective-permute-done((f32[21,256,256]{2,1,0:T(8,128)S(1)}, f32[21,256,256]{2,1,0:T(8,128)S(1)}, u32[]{:S(2)}, u32[]{:S(2)}) %collective-permute-start.3) | collective-permute-done | bytes 5505056 | tf_op jit(solution)/shard_map/ppermute | solution.py:193
  133.3 21.6 %middle.1 = (bf16[1536,768]{1,0:T(8,128)(2,1)S(1)}, bf16[1536,1280]{1,0:T(8,128)(2,1)}, f32[21,256,256]{2,1,0:T(8,128)}, f32[8,128]{1,0:T(8,128)S(1)}) custom-call(s32[1]{0:T(128)S(6)} %convert_element_type.7.flag, f32[21,256,256]{2,1,0:T(8,128)} %copy-done.1, f32[21,256,256]{2,1,0:T(8,128)} %copy-done.17, bf16[1536,768]{1,0:T(8,128)(2,1)} %bitcast.13.refs_0_, ...), custom_call_target="tpu_custom_call" | custom-call | flops 18119393280 | bytes 29102080 | tf_op jit(solution)/shard_map/middle/pallas_call | solution.py:469
  155.7 8.5 %collective-permute-done.4.other_in = f32[21,256,256]{2,1,0:T(8,128)S(1)} collective-permute-done((f32[21,256,256]{2,1,0:T(8,128)}, f32[21,256,256]{2,1,0:T(8,128)S(1)}, u32[]{:S(2)}, u32[]{:S(2)}) %collective-permute-start.4) | collective-permute-done | bytes 5505056 | tf_op jit(solution)/shard_map/ppermute | solution.py:193
  164.2 2.6 copy-done
  166.8 14.2 %last.1 = (bf16[1536,1536]{1,0:T(8,128)(2,1)S(1)}, bf16[1536,768]{1,0:T(8,128)(2,1)}) custom-call(f32[1]{0:T(128)S(6)} %select_n.105.factor, f32[21,256,256]{2,1,0:T(8,128)S(1)} %copy-done, f32[21,256,256]{2,1,0:T(8,128)S(1)} %collective-permute-done.4.other_in, bf16[1536,768]{1,0:T(8,128)(2,1)S(1)} %get-tuple-element.32.x_in), custom_call_target="tpu_custom_call" | custom-call | flops 7247757312 | bytes 20447232 | tf_op jit(solution)/shard_map/last/pallas_call | solution.py:469
  183.1 28.8 %all-to-all-start.2 = ((bf16[16,96,768]{2,1,0:T(8,128)(2,1)}), bf16[16,96,768]{2,1,0:T(8,128)(2,1)S(1)}, u32[]{:S(2)}, u32[]{:S(2)}) async-start(bf16[16,96,768]{2,1,0:T(8,128)(2,1)} %bitcast.18), calls=%async_computation.2 | async-start | bytes 4718592 | tf_op jit(solution)/shard_map/all_to_all | solution.py:666
  221.1 33.7 %collective-permute-done.7 = bf16[1536,256]{1,0:T(8,128)(2,1)S(1)} collective-permute-done((bf16[1536,256]{1,0:T(8,128)(2,1)S(1)}, bf16[1536,256]{1,0:T(8,128)(2,1)S(1)}, u32[]{:S(2)}, u32[]{:S(2)}) %collective-permute-start.7) | collective-permute-done | bytes 786464 | tf_op jit(solution)/shard_map/ppermute | solution.py:674
  254.8 5.6 %collective-permute-done.5 = bf16[1536,256]{1,0:T(8,128)(2,1)S(1)} collective-permute-done((bf16[1536,256]{1,0:T(8,128)(2,1)S(1)}, bf16[1536,256]{1,0:T(8,128)(2,1)S(1)}, u32[]{:S(2)}, u32[]{:S(2)}) %collective-permute-start.5) | collective-permute-done | bytes 786464 | tf_op jit(solution)/shard_map/ppermute | solution.py:674
  260.5 2.8 select_select_fusion.1
  267.2 24.4 %all-to-all-start.3 = ((bf16[16,96,512]{2,1,0:T(8,128)(2,1)}), bf16[16,96,512]{2,1,0:T(8,128)(2,1)S(1)}, u32[]{:S(2)}, u32[]{:S(2)}) async-start(bf16[16,96,512]{2,1,0:T(8,128)(2,1)} %bitcast.38), calls=%async_computation.3 | async-start | bytes 3145728 | tf_op jit(solution)/shard_map/all_to_all | solution.py:666
  301.2 2.8 collective-permute-done.9
  304.7 12.6 %collective-permute-done.10 = f32[16]{0:T(128)S(1)} collective-permute-done((f32[16]{0:T(128)S(1)}, f32[16]{0:T(128)S(1)}, u32[]{:S(2)}, u32[]{:S(2)}) %collective-permute-start.10) | collective-permute-done | bytes 96 | tf_op jit(solution)/shard_map/ppermute | solution.py:546
  317.3 2.9 collective-permute-start.11
  320.2 5.1 %collective-permute-done.11 = f32[16]{0:T(128)S(1)} collective-permute-done((f32[16]{0:T(128)S(1)}, f32[16]{0:T(128)S(1)}, u32[]{:S(2)}, u32[]{:S(2)}) %collective-permute-start.11) | collective-permute-done | bytes 96 | tf_op jit(solution)/shard_map/ppermute | solution.py:546
  326.6 5.9 %assemble_squares.1 = bf16[8,96,768]{2,1,0:T(8,128)(2,1)} custom-call(s32[8]{0:T(128)} %order.2, s32[8]{0:T(128)} %constant.76.clone.chip_of, bf16[16,96,768]{2,1,0:T(8,128)(2,1)} %copy-done.8), custom_call_target="tpu_custom_call" | custom-call | tf_op jit(solution)/shard_map/assemble_squares/pallas_call | solution.py:488
  333.7 5.6 %assemble_swiglu.1 = bf16[6,96,2048]{2,1,0:T(8,128)(2,1)} custom-call(s32[6]{0:T(128)} %order.3, s32[42]{0:T(128)} %constant.77.clone.where, bf16[16,96,768]{2,1,0:T(8,128)(2,1)} %copy-done.8, bf16[16,96,512]{2,1,0:T(8,128)(2,1)} %copy-done.7, bf16[16,96,512]{2,1,0:T(8,128)(2,1)} %copy-done.7, bf16[16,96,512]{2,1,0:T(8,128)(2,1)} %copy-done.7, ...), custom_call_target="tpu_custom_call" | custom-call | tf_op jit(solution)/shard_map/assemble_swiglu/pallas_call | solution.py:525
  (88 shorter events, 36.0 us)
Async XLA Ops:
  57.9 56.8 %all-to-all-start = ((bf16[32,48,768]{2,1,0:T(8,128)(2,1)}), bf16[32,48,768]{2,1,0:T(8,128)(2,1)}, u32[]{:S(2)}, u32[]{:S(2)}) async-start(bf16[32,48,768]{2,1,0:T(8,128)(2,1)} %get-tuple-element.29), calls=%async_computation | async-start | bytes 4718592 | tf_op jit(solution)/shard_map/all_to_all | solution.py:590
  65.3 37.4 %collective-permute-start = (bf16[1536,256]{1,0:T(8,128)(2,1)S(1)}, bf16[1536,256]{1,0:T(8,128)(2,1)S(1)}, u32[]{:S(2)}, u32[]{:S(2)}) collective-permute-start(bf16[1536,256]{1,0:T(8,128)(2,1)S(1)} %get-tuple-element.50), channel_id=1, source_target_pairs={{12,8},{22,18},{10,14},{16,20},{6,2},{28,24},{13,9},{23,19},{11,15... | collective-permute-start | bytes 2359304 | tf_op jit(solution)/shard_map/ppermute | solution.py:599
  67.8 34.9 %collective-permute-start.1 = (bf16[1536,256]{1,0:T(8,128)(2,1)S(1)}, bf16[1536,256]{1,0:T(8,128)(2,1)S(1)}, u32[]{:S(2)}, u32[]{:S(2)}) collective-permute-start(bf16[1536,256]{1,0:T(8,128)(2,1)S(1)} %get-tuple-element.49), channel_id=1, source_target_pairs={{0,8},{26,18},{6,14},{28,20},{4,2},{30,24},{1,9},{27,19},{7,15},{2... | collective-permute-start | bytes 2359304 | tf_op jit(solution)/shard_map/ppermute | solution.py:599
  68.5 34.2 %collective-permute-start.2 = (bf16[1536,256]{1,0:T(8,128)(2,1)S(1)}, bf16[1536,256]{1,0:T(8,128)(2,1)S(1)}, u32[]{:S(2)}, u32[]{:S(2)}) collective-permute-start(bf16[1536,256]{1,0:T(8,128)(2,1)S(1)} %get-tuple-element.48), channel_id=1, source_target_pairs={{10,8},{16,18},{12,14},{22,20},{0,2},{26,24},{11,9},{17,19},{13,15... | collective-permute-start | bytes 2359304 | tf_op jit(solution)/shard_map/ppermute | solution.py:599
  121.7 9.1 %copy-start.1 = (f32[21,256,256]{2,1,0:T(8,128)}, f32[21,256,256]{2,1,0:T(8,128)S(1)}, u32[]{:S(2)}) copy-start(f32[21,256,256]{2,1,0:T(8,128)S(1)} %gram.1.own_in) | copy-start | bytes 16515076
  121.7 9.1 %collective-permute-start.3 = (f32[21,256,256]{2,1,0:T(8,128)S(1)}, f32[21,256,256]{2,1,0:T(8,128)S(1)}, u32[]{:S(2)}, u32[]{:S(2)}) collective-permute-start(f32[21,256,256]{2,1,0:T(8,128)S(1)} %gram.1.own_in), channel_id=1, source_target_pairs={{0,1},{1,0},{2,3},{3,2},{4,5},{5,4},{6,7},{7,6},{8,9},{9,8},{10,11... | collective-permute-start | bytes 16515080 | tf_op jit(solution)/shard_map/ppermute | solution.py:193
  154.9 9.3 %collective-permute-start.4 = (f32[21,256,256]{2,1,0:T(8,128)}, f32[21,256,256]{2,1,0:T(8,128)S(1)}, u32[]{:S(2)}, u32[]{:S(2)}) collective-permute-start(f32[21,256,256]{2,1,0:T(8,128)} %get-tuple-element.31.own_in), channel_id=1, source_target_pairs={{0,1},{1,0},{2,3},{3,2},{4,5},{5,4},{6,7},{7,6},{8,9},{9,8},{10,11... | collective-permute-start | bytes 16515080 | tf_op jit(solution)/shard_map/ppermute | solution.py:193
  183.1 82.7 %all-to-all-start.2 = ((bf16[16,96,768]{2,1,0:T(8,128)(2,1)}), bf16[16,96,768]{2,1,0:T(8,128)(2,1)S(1)}, u32[]{:S(2)}, u32[]{:S(2)}) async-start(bf16[16,96,768]{2,1,0:T(8,128)(2,1)} %bitcast.18), calls=%async_computation.2 | async-start | bytes 4718592 | tf_op jit(solution)/shard_map/all_to_all | solution.py:666
  216.6 4.5 %collective-permute-start.6 = (bf16[1536,256]{1,0:T(8,128)(2,1)S(1)}, bf16[1536,256]{1,0:T(8,128)(2,1)S(1)}, u32[]{:S(2)}, u32[]{:S(2)}) collective-permute-start(bf16[1536,256]{1,0:T(8,128)(2,1)S(1)} %get-tuple-element.36), channel_id=1, source_target_pairs={{8,0},{18,26},{14,6},{20,28},{2,4},{24,30},{9,1},{19,27},{15,7},{2... | collective-permute-start | bytes 2359304 | tf_op jit(solution)/shard_map/ppermute | solution.py:674
  217.3 37.5 %collective-permute-start.7 = (bf16[1536,256]{1,0:T(8,128)(2,1)S(1)}, bf16[1536,256]{1,0:T(8,128)(2,1)S(1)}, u32[]{:S(2)}, u32[]{:S(2)}) collective-permute-start(bf16[1536,256]{1,0:T(8,128)(2,1)S(1)} %get-tuple-element.37), channel_id=1, source_target_pairs={{8,12},{18,22},{14,10},{20,16},{2,6},{24,28},{9,13},{19,23},{15,11... | collective-permute-start | bytes 2359304 | tf_op jit(solution)/shard_map/ppermute | solution.py:674
  218.6 41.8 %collective-permute-start.5 = (bf16[1536,256]{1,0:T(8,128)(2,1)S(1)}, bf16[1536,256]{1,0:T(8,128)(2,1)S(1)}, u32[]{:S(2)}, u32[]{:S(2)}) collective-permute-start(bf16[1536,256]{1,0:T(8,128)(2,1)S(1)} %get-tuple-element.35), channel_id=1, source_target_pairs={{8,10},{18,16},{14,12},{20,22},{2,0},{24,26},{9,11},{19,17},{15,13... | collective-permute-start | bytes 2359304 | tf_op jit(solution)/shard_map/ppermute | solution.py:674
  264.5 27.2 %copy-start.13 = (s32[16,2]{0,1:T(2,128)S(1)}, s32[16,2]{0,1:T(2,128)}, u32[]{:S(2)}) copy-start(s32[16,2]{0,1:T(2,128)} %param.45) | copy-start | bytes 388
  264.5 27.3 %copy-start.12 = (f32[1344]{0:T(1024)S(1)}, f32[1344]{0:T(1024)}, u32[]{:S(2)}) copy-start(f32[1344]{0:T(1024)} %param.37) | copy-start | bytes 16132
  264.5 28.7 %copy-start.9 = (f32[128,768]{1,0:T(8,128)S(1)}, f32[128,768]{1,0:T(8,128)}, u32[]{:S(2)}) copy-start(f32[128,768]{1,0:T(8,128)} %param.44) | copy-start | bytes 1179652
  264.5 28.7 %copy-start.10 = (f32[128,768]{1,0:T(8,128)S(1)}, f32[128,768]{1,0:T(8,128)}, u32[]{:S(2)}) copy-start(f32[128,768]{1,0:T(8,128)} %param.42) | copy-start | bytes 1179652
  264.5 28.7 %copy-start.11 = (f32[128,768]{1,0:T(8,128)S(1)}, f32[128,768]{1,0:T(8,128)}, u32[]{:S(2)}) copy-start(f32[128,768]{1,0:T(8,128)} %param.41) | copy-start | bytes 1179652
  267.2 65.3 %all-to-all-start.3 = ((bf16[16,96,512]{2,1,0:T(8,128)(2,1)}), bf16[16,96,512]{2,1,0:T(8,128)(2,1)S(1)}, u32[]{:S(2)}, u32[]{:S(2)}) async-start(bf16[16,96,512]{2,1,0:T(8,128)(2,1)} %bitcast.38), calls=%async_computation.3 | async-start | bytes 3145728 | tf_op jit(solution)/shard_map/all_to_all | solution.py:666
  291.6 9.4 %copy-start.15 = (s32[6]{0:T(128)S(1)}, s32[6]{0:T(128)}, u32[]{:S(2)}) copy-start(s32[6]{0:T(128)} %order.3) | copy-start | bytes 76
  291.6 12.9 %copy-start.14 = (s32[8]{0:T(128)S(1)}, s32[8]{0:T(128)}, u32[]{:S(2)}) copy-start(s32[8]{0:T(128)} %order.2) | copy-start | bytes 100
  291.6 28.5 %copy-start.16 = (s32[14]{0:T(128)S(1)}, s32[14]{0:T(128)}, u32[]{:S(2)}) copy-start(s32[14]{0:T(128)} %constant.80) | copy-start | bytes 172
  296.8 3.6 %collective-permute-start.8 = (f32[16]{0:T(128)S(1)}, f32[16]{0:T(128)S(1)}, u32[]{:S(2)}, u32[]{:S(2)}) collective-permute-start(f32[16]{0:T(128)S(1)} %compare_select_fusion), channel_id=1, source_target_pairs={{0,2},{2,0},{4,6},{6,4},{8,10},{10,8},{12,14},{14,12},{16,18},{18,... | collective-permute-start | bytes 200 | tf_op jit(solution)/shard_map/ppermute | solution.py:546
  300.4 3.5 %collective-permute-start.9 = (f32[16]{0:T(128)S(1)}, f32[16]{0:T(128)S(1)}, u32[]{:S(2)}, u32[]{:S(2)}) collective-permute-start(f32[16]{0:T(128)S(1)} %fusion.6), channel_id=1, source_target_pairs={{0,4},{2,6},{4,0},{6,2},{8,12},{10,14},{12,8},{14,10},{16,20},{18,... | collective-permute-start | bytes 200 | tf_op jit(solution)/shard_map/ppermute | solution.py:546
  304.0 13.3 %collective-permute-start.10 = (f32[16]{0:T(128)S(1)}, f32[16]{0:T(128)S(1)}, u32[]{:S(2)}, u32[]{:S(2)}) collective-permute-start(f32[16]{0:T(128)S(1)} %fusion.7), channel_id=1, source_target_pairs={{0,8},{2,10},{4,12},{6,14},{8,0},{10,2},{12,4},{14,6},{16,24},{18,... | collective-permute-start | bytes 200 | tf_op jit(solution)/shard_map/ppermute | solution.py:546
  317.3 8.0 %collective-permute-start.11 = (f32[16]{0:T(128)S(1)}, f32[16]{0:T(128)S(1)}, u32[]{:S(2)}, u32[]{:S(2)}) collective-permute-start(f32[16]{0:T(128)S(1)} %add.70), channel_id=1, source_target_pairs={{0,16},{2,18},{4,20},{6,22},{8,24},{10,26},{12,28},{14,30},{16,0},... | collective-permute-start | bytes 200 | tf_op jit(solution)/shard_map/ppermute | solution.py:546
  (15 other events, 49.5 us)

commit v5 on v4

--- a/solution.py
+++ b/solution.py
@@ -105,26 +105,24 @@
         self.idle = [c for c in range(chips) if c not in self.heavy and c not in self.light]
 
 
-def prepare_kernel(plan, cores, sg, ss, wg, ws, sn, wn, first, second, sv, wv):
+def momentum_rows(grad, state, following, sent):
+    def row(r, carry):
+        after = MOMENTUM * state[r] + grad[r]
+        following[r] = after
+        sent[r] = grad[r] + MOMENTUM * after
+        return carry
+
+    lax.fori_loop(0, grad.shape[0], row, 0)
+
+
+def wide_kernel(plan, cores, grad, state, following, first, second, sent):
     narrow_tiles = D // cores // LANE
     wide_tiles = FF // cores // LANE
-    for grad, state, following, sent in ((wg, ws, wn, wv), (sg, ss, sn, sv)):
-
-        def row(r, carry):
-            after = MOMENTUM * state[r] + grad[r]
-            following[r] = after
-            sent[r] = grad[r] + MOMENTUM * after
-            return carry
-
-        lax.fori_loop(0, grad.shape[0], row, 0)
-
-    def piece(sent, row_tile, slot):
-        return sent[:, row_tile, slot, :].astype(jnp.bfloat16)
-
+    momentum_rows(grad, state, following, sent)
     for j, owner in enumerate(plan.heavy):
         for core in range(cores):
             for t in range(wide_tiles):
-                value = piece(wv, core * wide_tiles + t, j)
+                value = sent[:, core * wide_tiles + t, j, :].astype(jnp.bfloat16)
                 if t < narrow_tiles:
                     first[owner * cores + core, :, t * LANE : (t + 1) * LANE] = value
                 else:
@@ -132,11 +130,6 @@
                     chip, where = plan.place[(j, b)]
                     at = where * GRANULE + part * LANE
                     second[chip * cores + core, :, at : at + LANE] = value
-    for j, owner in enumerate(plan.light):
-        for core in range(cores):
-            for t in range(narrow_tiles):
-                value = piece(sv, core * narrow_tiles + t, j)
-                first[owner * cores + core, :, t * LANE : (t + 1) * LANE] = value
     for chip in range(len(plan.is_heavy)):
         for core in range(cores):
             if chip in plan.idle:
@@ -147,46 +140,89 @@
                 )
 
 
-def prepare(plan, chips, cores, square_grad, square_state, swiglu_grad, swiglu_state):
+def narrow_kernel(plan, cores, grad, state, given, following, first, sent, stage, sems):
+    narrow_tiles = D // cores // LANE
+    momentum_rows(grad, state, following, sent)
+    copies = []
+    for j, owner in enumerate(plan.light):
+        for core in range(cores):
+            for t in range(narrow_tiles):
+                value = sent[:, core * narrow_tiles + t, j, :].astype(jnp.bfloat16)
+                stage[j * cores + core, :, t * LANE : (t + 1) * LANE] = value
+        copies.append(
+            pltpu.make_async_copy(
+                stage.at[pl.ds(j * cores, cores)], first.at[pl.ds(owner * cores, cores)], sems.at[j]
+            )
+        )
+        copies[-1].start()
+    for copy in copies:
+        copy.wait()
+
+
+def tiles_of(x, rows, width):
+    return x.reshape(x.shape[0], rows, width // LANE, LANE).transpose(1, 2, 0, 3)
+
+
+def flat_of(x):
+    return x.transpose(2, 0, 1, 3).reshape(x.shape[2], -1)
+
+
+def prepare_wide(plan, chips, cores, grad, state):
     rows = D // (chips * cores)
     chunk = 16 if rows % 16 == 0 else rows
-    square_count, swiglu_count = square_grad.shape[0], swiglu_grad.shape[0]
-
-    def tiles(x, width):
-        count = x.shape[0]
-        return x.reshape(count, rows, width // LANE, LANE).transpose(1, 2, 0, 3)
-
-    def flat(x, width):
-        return x.transpose(2, 0, 1, 3).reshape(x.shape[2], rows * width)
-
+    count = grad.shape[0]
     narrow = D // cores
-    square_block = pl.BlockSpec((chunk, D // LANE, square_count, LANE), lambda i: (i, 0, 0, 0))
-    swiglu_block = pl.BlockSpec((chunk, FF // LANE, swiglu_count, LANE), lambda i: (i, 0, 0, 0))
     devices = chips * cores
-    out = pl.pallas_call(
-        lambda *refs: prepare_kernel(plan, cores, *refs),
+    block = (chunk, FF // LANE, count, LANE)
+    spec = pl.BlockSpec(block, lambda i: (i, 0, 0, 0))
+    following, first, second = pl.pallas_call(
+        lambda *refs: wide_kernel(plan, cores, *refs),
         grid=(rows // chunk,),
-        in_specs=[square_block, square_block, swiglu_block, swiglu_block],
+        in_specs=[spec, spec],
         out_specs=[
-            square_block,
-            swiglu_block,
+            spec,
             pl.BlockSpec((devices, chunk, narrow), lambda i: (0, i, 0)),
             pl.BlockSpec((devices, chunk, 2 * GRANULE), lambda i: (0, i, 0)),
         ],
         out_shape=[
-            jax.ShapeDtypeStruct((rows, D // LANE, square_count, LANE), jnp.float32),
-            jax.ShapeDtypeStruct((rows, FF // LANE, swiglu_count, LANE), jnp.float32),
+            jax.ShapeDtypeStruct((rows,) + block[1:], jnp.float32),
             jax.ShapeDtypeStruct((devices, rows, narrow), jnp.bfloat16),
             jax.ShapeDtypeStruct((devices, rows, 2 * GRANULE), jnp.bfloat16),
         ],
+        scratch_shapes=[pltpu.VMEM(block, jnp.float32)],
+        compiler_params=pltpu.CompilerParams(vmem_limit_bytes=48 * 1024 * 1024),
+        name="prepare_wide",
+    )(tiles_of(grad, rows, FF), tiles_of(state, rows, FF))
+    return flat_of(following), first, second
+
+
+def prepare_narrow(plan, chips, cores, grad, state, first):
+    rows = D // (chips * cores)
+    count = grad.shape[0]
+    block = (rows, D // LANE, count, LANE)
+    vmem = pl.BlockSpec(memory_space=pltpu.VMEM)
+    anywhere = pl.BlockSpec(memory_space=pl.ANY)
+    following, first = pl.pallas_call(
+        lambda *refs: narrow_kernel(plan, cores, *refs),
+        in_specs=[vmem, vmem, anywhere],
+        out_specs=[vmem, anywhere],
+        out_shape=[
+            jax.ShapeDtypeStruct(block, jnp.float32),
+            jax.ShapeDtypeStruct(first.shape, first.dtype),
+        ],
+        input_output_aliases={2: 1},
         scratch_shapes=[
-            pltpu.VMEM((chunk, D // LANE, square_count, LANE), jnp.float32),
-            pltpu.VMEM((chunk, FF // LANE, swiglu_count, LANE), jnp.float32),
+            pltpu.VMEM(block, jnp.float32),
+            pltpu.VMEM((count * cores, rows, D // cores), jnp.bfloat16),
+            pltpu.SemaphoreType.DMA((count,)),
         ],
-        compiler_params=pltpu.CompilerParams(vmem_limit_bytes=56 * 1024 * 1024),
-        name="prepare",
-    )(tiles(square_grad, D), tiles(square_state, D), tiles(swiglu_grad, FF), tiles(swiglu_state, FF))
-    return flat(out[0], D), flat(out[1], FF), out[2], out[3]
+        compiler_params=pltpu.CompilerParams(vmem_limit_bytes=32 * 1024 * 1024),
+        cost_estimate=pl.CostEstimate(
+            flops=0, bytes_accessed=3 * grad.size * 4 + grad.size * 2, transcendentals=0
+        ),
+        name="prepare_narrow",
+    )(tiles_of(grad, rows, D), tiles_of(state, rows, D), first)
+    return flat_of(following), first
 
 
 def other_core(x):
@@ -392,16 +428,23 @@
     wait_all(group_copies(other, packed_out, packed_sems))
 
 
-def last_kernel(factor, own_in, other_in, x_in, polynomial_out, out, *refs):
-    own, other, x, mixed, normed, polynomial = refs[:6]
-    own_sems, other_sems, x_sem, polynomial_sem, out_sems = refs[6:]
+def last_kernel(flag, factor, own_in, other_in, x_in, *refs):
+    count = len(refs) - 11
+    polynomial_out, outs = refs[0], refs[1:count]
+    own, other, x, mixed, normed, polynomial = refs[count : count + 6]
+    own_sems, other_sems, x_sem, polynomial_sem, out_sems = refs[count + 6 :]
     own_copies = group_copies(own_in, own, own_sems)
     other_copies = group_copies(other_in, other, other_sems)
     for a, b in zip(own_copies, other_copies):
         a.start()
         b.start()
     x_copy = pltpu.make_async_copy(x_in, x, x_sem)
-    x_copy.start()
+    heavy = flag[0] > 0
+
+    @pl.when(heavy)
+    def _():
+        x_copy.start()
+
     for g in range(GROUPS):
         own_copies[g].wait()
         other_copies[g].wait()
@@ -412,26 +455,6 @@
     polynomial_blocks(normed, polynomial)
     polynomial_copy = pltpu.make_async_copy(polynomial, polynomial_out, polynomial_sem)
     polynomial_copy.start()
-    x_copy.wait()
-
-    def out_copy(i):
-        return pltpu.make_async_copy(rows_of(mixed, i), rows_of(out, i), out_sems.at[i])
-
-    mixed_rows(
-        polynomial, x, x.shape[1], factor[0], mixed, after=lambda i: out_copy(i).start()
-    )
-    wait_all([out_copy(i) for i in range(EDGE)])
-    polynomial_copy.wait()
-
-
-def rest_kernel(flag, factor, polynomial_in, x_in, *refs):
-    outs, (x, mixed, polynomial, x_sem, polynomial_sems, out_sems) = refs[:-6], refs[-6:]
-    x_copy = pltpu.make_async_copy(x_in, x, x_sem)
-
-    def polynomial_copy(i):
-        return pltpu.make_async_copy(
-            rows_of(polynomial_in, i), rows_of(polynomial, i), polynomial_sems.at[i]
-        )
 
     def out_copies(i):
         copies, at = [], 0
@@ -442,10 +465,8 @@
             at += width
         return copies
 
-    @pl.when(flag[0] > 0)
+    @pl.when(heavy)
     def _():
-        x_copy.start()
-        start_all([polynomial_copy(i) for i in range(EDGE)])
         x_copy.wait()
         mixed_rows(
             polynomial,
@@ -453,11 +474,55 @@
             x.shape[1],
             factor[0],
             mixed,
-            before=lambda i: polynomial_copy(i).wait(),
             after=lambda i: start_all(out_copies(i)),
         )
         for i in range(EDGE):
             wait_all(out_copies(i))
+
+    polynomial_copy.wait()
+
+
+def finish_kernel(factor, polynomial_in, x_in, out, x, mixed, polynomial, x_sem, in_sems, out_sems):
+    x_copy = pltpu.make_async_copy(x_in, x, x_sem)
+    x_copy.start()
+
+    def in_copy(i):
+        return pltpu.make_async_copy(rows_of(polynomial_in, i), rows_of(polynomial, i), in_sems.at[i])
+
+    def out_copy(i):
+        return pltpu.make_async_copy(rows_of(mixed, i), rows_of(out, i), out_sems.at[i])
+
+    start_all([in_copy(i) for i in range(EDGE)])
+    x_copy.wait()
+    mixed_rows(
+        polynomial,
+        x,
+        x.shape[1],
+        factor[0],
+        mixed,
+        before=lambda i: in_copy(i).wait(),
+        after=lambda i: out_copy(i).start(),
+    )
+    wait_all([out_copy(i) for i in range(EDGE)])
+
+
+def join_kernel(pick, own, *refs):
+    handed, (out, stage, in_sems, out_sem) = refs[:-4], refs[-4:]
+    for where in range(2):
+        target = columns_of(stage, where * GRANULE, GRANULE)
+        for k in range(1 + len(handed)):
+            source = columns_of(own, where * GRANULE, GRANULE) if k == 0 else handed[k - 1]
+
+            @pl.when(pick[where] == k)
+            def _():
+                pltpu.make_async_copy(source, target, in_sems.at[where]).start()
+
+    for where in range(2):
+        target = columns_of(stage, where * GRANULE, GRANULE)
+        pltpu.make_async_copy(columns_of(own, 0, GRANULE), target, in_sems.at[where]).wait()
+    copy = pltpu.make_async_copy(stage, out, out_sem)
+    copy.start()
+    copy.wait()
 
 
 def call(kernel, name, scalars, arrays, outs, scratch, limit, flops, small_outs=0):
@@ -478,65 +543,77 @@
     )(*scalars, *arrays)
 
 
+def assemble(kernel, name, order, arrays, shape, copies):
+    anywhere = pl.BlockSpec(memory_space=pl.ANY)
+    return pl.pallas_call(
+        kernel,
+        in_specs=[pl.BlockSpec(memory_space=pltpu.SMEM)] + [anywhere] * len(arrays),
+        out_specs=anywhere,
+        out_shape=jax.ShapeDtypeStruct(shape, jnp.bfloat16),
+        scratch_shapes=[
+            pltpu.VMEM(shape, jnp.bfloat16),
+            pltpu.SemaphoreType.DMA((copies,)),
+            pltpu.SemaphoreType.DMA((shape[0],)),
+        ],
+        compiler_params=pltpu.CompilerParams(vmem_limit_bytes=8 * MIB),
+        name=name,
+    )(order, *arrays)
+
+
+def place_slots(order, stage, out, copies, out_sems):
+    for slot in copies:
+        start_all(slot)
+    outs = []
+    for j, slot in enumerate(copies):
+        wait_all(slot)
+        outs.append(pltpu.make_async_copy(stage.at[j], out.at[order[j]], out_sems.at[j]))
+        outs[-1].start()
+    wait_all(outs)
+
+
 def assemble_squares(plan, square_order, first_back):
     count = square_order.shape[0]
-    shape = first_back.shape[1:]
-
-    def kernel(order, chip_of, source, out):
-        out[...] = source[...]
-
-    return pl.pallas_call(
-        kernel,
-        grid_spec=pltpu.PrefetchScalarGridSpec(
-            num_scalar_prefetch=2,
-            grid=(count,),
-            in_specs=[pl.BlockSpec((1,) + shape, lambda j, order, chip_of: (chip_of[j], 0, 0))],
-            out_specs=pl.BlockSpec((1,) + shape, lambda j, order, chip_of: (order[j], 0, 0)),
-        ),
-        out_shape=jax.ShapeDtypeStruct((count,) + shape, jnp.bfloat16),
-        name="assemble_squares",
-    )(square_order, jnp.asarray(plan.light, jnp.int32), first_back)
+
+    def kernel(order, source, out, stage, in_sems, out_sems):
+        copies = [
+            [pltpu.make_async_copy(source.at[plan.light[j]], stage.at[j], in_sems.at[j])]
+            for j in range(count)
+        ]
+        place_slots(order, stage, out, copies, out_sems)
+
+    shape = (count,) + first_back.shape[1:]
+    return assemble(kernel, "assemble_squares", square_order, [first_back], shape, count)
 
 
 def assemble_swiglu(plan, swiglu_order, first_back, second_back):
     count = swiglu_order.shape[0]
     rows, narrow = first_back.shape[1:]
     wide = narrow + plan.granules * GRANULE
-    extra = range(2, plan.granules)
-    chips = [plan.heavy[j] for j in range(count)]
-    places = [plan.place[(j, b)] for b in extra for j in range(count)]
-    table = np.array(chips + [c for c, _ in places] + [w for _, w in places], np.int32)
-
-    def kernel(order, where, first, own, *refs):
-        out = refs[-1]
-        out[0, :, :narrow] = first[0]
-        out[0, :, narrow : narrow + 2 * GRANULE] = own[0]
-        for k, ref in enumerate(refs[:-1]):
-            at = narrow + (2 + k) * GRANULE
-            out[0, :, at : at + GRANULE] = ref[0]
-
-    def granule(k):
-        def index(j, order, where):
-            at = (1 + k) * count + j
-            return where[at], 0, where[len(extra) * count + at]
-
-        return pl.BlockSpec((1, rows, GRANULE), index)
-
-    return pl.pallas_call(
-        kernel,
-        grid_spec=pltpu.PrefetchScalarGridSpec(
-            num_scalar_prefetch=2,
-            grid=(count,),
-            in_specs=[
-                pl.BlockSpec((1, rows, narrow), lambda j, order, where: (where[j], 0, 0)),
-                pl.BlockSpec((1, rows, 2 * GRANULE), lambda j, order, where: (where[j], 0, 0)),
+
+    def kernel(order, first, second, out, stage, in_sems, out_sems):
+        copies = []
+        for j in range(count):
+            moves = [
+                (first.at[plan.heavy[j]], 0, narrow),
+                (second.at[plan.heavy[j]], narrow, 2 * GRANULE),
             ]
-            + [granule(k) for k in range(len(extra))],
-            out_specs=pl.BlockSpec((1, rows, wide), lambda j, order, where: (order[j], 0, 0)),
-        ),
-        out_shape=jax.ShapeDtypeStruct((count, rows, wide), jnp.bfloat16),
-        name="assemble_swiglu",
-    )(swiglu_order, jnp.asarray(table), first_back, *([second_back] * (1 + len(extra))))
+            for b in range(2, plan.granules):
+                chip, where = plan.place[(j, b)]
+                source = second.at[chip, :, pl.ds(where * GRANULE, GRANULE)]
+                moves.append((source, narrow + b * GRANULE, GRANULE))
+            copies.append(
+                [
+                    pltpu.make_async_copy(
+                        source, stage.at[j, :, pl.ds(at, width)], in_sems.at[j * len(moves) + k]
+                    )
+                    for k, (source, at, width) in enumerate(moves)
+                ]
+            )
+        place_slots(order, stage, out, copies, out_sems)
+
+    arrays = [first_back, second_back]
+    shape = (count, rows, wide)
+    return assemble(kernel, "assemble_swiglu", swiglu_order, arrays, shape, count * plan.granules)
 
 
 def spread(value, chips, chip):
@@ -580,8 +657,11 @@
     narrow = D // cores
     plan = Plan(chips, cores, square_count, swiglu_count)
 
-    square_next, swiglu_next, first_send, second_send = prepare(
-        plan, chips, cores, square_grad, square_state, swiglu_grad, swiglu_state
+    swiglu_next, first_send, second_send = prepare_wide(
+        plan, chips, cores, swiglu_grad, swiglu_state
+    )
+    square_next, first_send = prepare_narrow(
+        plan, chips, cores, square_grad, square_state, first_send
     )
     both = ("dp", "tensor")
     second_got = lax.all_to_all(
@@ -619,7 +699,7 @@
         parts,
         [packed],
         [matrix_buffer, packed_buffer, sems(len(parts)), sems(GROUPS)],
-        18,
+        15,
         half,
     )
     first_mid, second_mid, own_mid, scale = call(
@@ -632,34 +712,40 @@
         + [matrix_buffer] * 2
         + [square_buffer] * 2
         + [sems(GROUPS), sems(GROUPS), sems(len(parts)), sems(2), sems(GROUPS)],
-        44,
+        37,
         3 * half + D * D * D,
         small_outs=1,
     )
-    polynomial, first_done = call(
+    piece_shape = jax.ShapeDtypeStruct((D, GRANULE), jnp.bfloat16)
+    pair_shape = jax.ShapeDtypeStruct((D, 2 * GRANULE), jnp.bfloat16)
+    polynomial, kept, *rest = call(
         last_kernel,
         "last",
+        [flag, factor],
+        [own_mid, other_core(own_mid), second_mid],
+        [whole_square, pair_shape] + [piece_shape] * plan.passes,
+        [packed_buffer] * 2
+        + [second_buffer] * 2
+        + [square_buffer] * 2
+        + [sems(GROUPS), sems(GROUPS), sems(), sems(), sems(1 + plan.passes, EDGE)],
+        32,
+        D * D * D + 2 * D * D * extra,
+    )
+    handed = []
+    for p in range(plan.passes):
+        pairs = [(plan.heavy[k], plan.take[p][k]) for k in range(swiglu_count)]
+        handed.append(lax.ppermute(rest[p], "dp", pairs))
+    (first_done,) = call(
+        finish_kernel,
+        "finish",
         [factor],
-        [own_mid, other_core(own_mid), first_mid],
-        [whole_square, first_shape],
-        [packed_buffer] * 2
-        + [first_buffer] * 2
-        + [square_buffer] * 2
-        + [sems(GROUPS), sems(GROUPS), sems(), sems(), sems(EDGE)],
-        34,
-        D * D * D + 2 * D * D * narrow,
-    )
-    piece_shape = jax.ShapeDtypeStruct((D, GRANULE), jnp.bfloat16)
-    rest = call(
-        rest_kernel,
-        "rest",
-        [flag, factor],
-        [polynomial, second_mid],
-        [jax.ShapeDtypeStruct((D, 2 * GRANULE), jnp.bfloat16)] + [piece_shape] * plan.passes,
-        [second_buffer] * 2 + [square_buffer, sems(), sems(EDGE), sems(1 + plan.passes, EDGE)],
-        20,
-        2 * D * D * extra,
-    )
+        [polynomial, first_mid],
+        [first_shape],
+        [first_buffer] * 2 + [square_buffer, sems(), sems(EDGE), sems(EDGE)],
+        14,
+        2 * D * D * narrow,
+    )
+    scale, _ = lax.optimization_barrier((scale, first_done))
     logs = spread(0.5 * jnp.log(scale[0, 0]), chips, chip)
 
     def send_back(x):
@@ -668,21 +754,21 @@
         )
 
     first_back = send_back(first_done)
-    handed = []
+    choice = np.zeros((chips, 2), np.int32)
     for p in range(plan.passes):
-        pairs = [(plan.heavy[k], plan.take[p][k]) for k in range(swiglu_count)]
-        handed.append(lax.ppermute(rest[1 + p], "dp", pairs))
-    halves = []
-    for where in range(2):
-        value = rest[0][:, where * GRANULE : (where + 1) * GRANULE]
-        for p in range(plan.passes):
-            mine = np.zeros((chips,), np.bool_)
-            for k in range(swiglu_count):
-                if plan.place[(k, 2 + p)][1] == where:
-                    mine[plan.take[p][k]] = True
-            value = jnp.where(jnp.asarray(mine)[chip], handed[p], value)
-        halves.append(value)
-    second_out, first_back = lax.optimization_barrier((jnp.concatenate(halves, axis=1), first_back))
+        for k in range(swiglu_count):
+            choice[plan.take[p][k], plan.place[(k, 2 + p)][1]] = 1 + p
+    (second_out,) = call(
+        join_kernel,
+        "join",
+        [jnp.asarray(choice)[chip]],
+        [kept, *handed],
+        [pair_shape],
+        [pltpu.VMEM(pair_shape.shape, jnp.bfloat16), sems(2), sems()],
+        4,
+        0,
+    )
+    second_out, first_back, logs = lax.optimization_barrier((second_out, first_back, logs))
     second_back = send_back(second_out)
 
     square_update = assemble_squares(plan, square_order, first_back)

time: 344 us -> 344 us (level); the launches traced: 339 us -> 343 us
  blocking collectives: 42.9 us -> 0 us
  starting transfers between devices: 73 us -> 102 us
  waiting for transfers between devices: 122 us -> 147 us
  other arithmetic: 10.4 us -> 5.8 us
    all_to_all x1 -> x0, blocking collectives: 42.9 us -> none  [local(): lax.all_to_all(second_send.reshape(D, 2 * GRANULE), both, split_axis=0, c...]
    ppermute x3, waiting for transfers between devices: 39.3 us -> 0.01 us  [local(): handed.append(lax.ppermute(rest[p], 'dp', pairs))]
    ppermute x4, starting transfers between devices: 5.52 us -> 34.2 us  [spread(): lax.ppermute(known, 'dp', [(s, s ^ step) for s in range(chips)])]
    all_to_all x0 -> x1, waiting for transfers between devices: none -> 27.3 us  [local(): lax.all_to_all(second_send.reshape(D, 2 * GRANULE), both, split_axis=0, c...]
    all_to_all x2, waiting for transfers between devices: 1.26 us -> 24.8 us  [send_back(): lax.all_to_all(x.reshape(chips, chip_rows, -1), 'dp', split_axis=0, conca...]
    ppermute x4, waiting for transfers between devices: 22.4 us -> 35.9 us  [spread(): lax.ppermute(known, 'dp', [(s, s ^ step) for s in range(chips)])]
    all_to_all x2, starting transfers between devices: 53.2 us -> 46.1 us  [send_back(): lax.all_to_all(x.reshape(chips, chip_rows, -1), 'dp', split_axis=0, conca...]
    all_to_all x0 -> x1, starting transfers between devices: none -> 5.99 us  [local(): lax.all_to_all(second_send.reshape(D, 2 * GRANULE), both, split_axis=0, c...]
  transfers between devices with their start and end apart: 15 -> 16, of which waited for: 11 -> 10; matrix products, arithmetic and copies ran while one was open for 4% -> 3% of each run, Pallas kernels for 2% -> 3%
where the time goes in v5:
time: 344 us; the launch traced here: 343 us
  waiting for transfers between devices  147 us (43%)
  starting transfers between devices  102 us (30%)
  Pallas kernels  67.7 us (20%)
  local copies, waits for them, and re-layouts  18.1 us (5%)
  other arithmetic  5.8 us (2%)
    all_to_all x2, starting transfers between devices, send_back(): lax.all_to_all(x.reshape(chips, chip_rows, -1), 'dp', split_axis=0, conca...  46.1 us
    pallas_call x5, Pallas kernels, call(): pl.pallas_call(kernel, in_specs=[smem] * len(scalars) + [anywhere] * len(...  44.6 us
    ppermute x4, waiting for transfers between devices, spread(): lax.ppermute(known, 'dp', [(s, s ^ step) for s in range(chips)])  35.9 us
    ppermute x4, starting transfers between devices, spread(): lax.ppermute(known, 'dp', [(s, s ^ step) for s in range(chips)])  34.2 us
    ppermute x3, waiting for transfers between devices, local(): lax.ppermute(jnp.where(pick, pieces[1], pieces[0]), 'dp', pairs)  30.1 us
    all_to_all x1, waiting for transfers between devices, local(): lax.all_to_all(second_send.reshape(D, 2 * GRANULE), both, split_axis=0, c...  27.3 us
    all_to_all x2, waiting for transfers between devices, send_back(): lax.all_to_all(x.reshape(chips, chip_rows, -1), 'dp', split_axis=0, conca...  24.8 us
    ppermute x2, waiting for transfers between devices, other_core(): return lax.ppermute(x, 'tensor', [(0, 1), (1, 0)])  17.6 us
  transfers between devices with their start and end apart: 16, of which 10 were waited for; matrix products, arithmetic and copies ran while one was open for 3% of the time, Pallas kernels for 3%

profile of v5, /device:TPU:12, one launch (start us, length us, event | category | flops | bytes accessed | tf_op | source)
XLA Modules:
  0.0 343.5 jit_solution(2579584465776967564)
XLA Ops:
  0.6 11.7 %prepare_wide.1 = (f32[48,32,6,128]{3,2,1,0:T(8,128)}, bf16[32,48,768]{2,1,0:T(8,128)(2,1)}, bf16[32,48,512]{2,1,0:T(8,128)(2,1)}) custom-call(f32[48,32,6,128]{3,2,1,0:T(8,128)} %bitcast.40, f32[48,32,6,128]{3,2,1,0:T(8,128)} %bitcast.41), custom_call_target="tpu_custom_call" | custom-call | tf_op jit(solution)/shard_map/prepare_wide/pallas_call | solution.py:178
  12.3 6.0 %all-to-all-start.1 = ((bf16[32,48,512]{2,1,0:T(8,128)(2,1)}), bf16[32,48,512]{2,1,0:T(8,128)(2,1)S(1)}, u32[]{:S(2)}, u32[]{:S(2)}) async-start(bf16[32,48,512]{2,1,0:T(8,128)(2,1)} %get-tuple-element.33), calls=%async_computation.1 | async-start | bytes 3145728 | tf_op jit(solution)/shard_map/all_to_all | solution.py:667
  21.7 5.1 %prepare_narrow.1 = (f32[48,12,8,128]{3,2,1,0:T(8,128)}, bf16[32,48,768]{2,1,0:T(8,128)(2,1)}) custom-call(f32[48,12,8,128]{3,2,1,0:T(8,128)S(1)} %bitcast.37, f32[48,12,8,128]{3,2,1,0:T(8,128)S(1)} %bitcast.38, bf16[32,48,768]{2,1,0:T(8,128)(2,1)} %get-tuple-element.29.refs_2_), custom_call_target="tpu_custom_call", output_to_operand_aliasing={{1}: (2, {})} | custom-call | bytes 8257536 | tf_op jit(solution)/shard_map/prepare_narrow/pallas_call | solution.py:205
  26.7 27.3 %all-to-all-done.1 = bf16[32,48,512]{2,1,0:T(8,128)(2,1)S(1)} async-done(((bf16[32,48,512]{2,1,0:T(8,128)(2,1)}), bf16[32,48,512]{2,1,0:T(8,128)(2,1)S(1)}, u32[]{:S(2)}, u32[]{:S(2)}) %all-to-all-start.1) | async-done | bytes 1572896 | tf_op jit(solution)/shard_map/all_to_all | solution.py:667
  54.0 5.8 %all-to-all-start = ((bf16[32,48,768]{2,1,0:T(8,128)(2,1)}), bf16[32,48,768]{2,1,0:T(8,128)(2,1)}, u32[]{:S(2)}, u32[]{:S(2)}) async-start(bf16[32,48,768]{2,1,0:T(8,128)(2,1)} %get-tuple-element.32), calls=%async_computation | async-start | bytes 4718592 | tf_op jit(solution)/shard_map/all_to_all | solution.py:670
  65.8 2.8 collective-permute-start.2
  69.8 30.1 %collective-permute-done.refs_2_ = bf16[1536,256]{1,0:T(8,128)(2,1)S(1)} collective-permute-done((bf16[1536,256]{1,0:T(8,128)(2,1)S(1)}, bf16[1536,256]{1,0:T(8,128)(2,1)S(1)}, u32[]{:S(2)}, u32[]{:S(2)}) %collective-permute-start) | collective-permute-done | bytes 786464 | tf_op jit(solution)/shard_map/ppermute | solution.py:679
  100.9 11.1 %all-to-all-done = bf16[32,48,768]{2,1,0:T(8,128)(2,1)} async-done(((bf16[32,48,768]{2,1,0:T(8,128)(2,1)}), bf16[32,48,768]{2,1,0:T(8,128)(2,1)}, u32[]{:S(2)}, u32[]{:S(2)}) %all-to-all-start) | async-done | bytes 2359328 | tf_op jit(solution)/shard_map/all_to_all | solution.py:670
  113.1 5.9 %gram.1.own_in = f32[21,256,256]{2,1,0:T(8,128)S(1)} custom-call(s32[1]{0:T(128)S(6)} %convert_element_type.7.flag, bf16[1536,768]{1,0:T(8,128)(2,1)} %bitcast.13.refs_0_, bf16[1536,512]{1,0:T(8,128)(2,1)S(1)} %bitcast.34, bf16[1536,256]{1,0:T(8,128)(2,1)S(1)} %collective-permute-done.refs_2_, bf16[1536,256]{1,0:T(8,128)(2,1)S(1)} %collective-permute-done.1.refs_3_, ...), custom_call_target="tpu_custom_call" | custom-call | flops 4831838208 | bytes 11796480 | tf_op jit(solution)/shard_map/gram/pallas_call | solution.py:534
  119.1 9.2 %collective-permute-done.3.other_in = f32[21,256,256]{2,1,0:T(8,128)} collective-permute-done((f32[21,256,256]{2,1,0:T(8,128)S(1)}, f32[21,256,256]{2,1,0:T(8,128)}, u32[]{:S(2)}, u32[]{:S(2)}) %collective-permute-start.3) | collective-permute-done | bytes 5505056 | tf_op jit(solution)/shard_map/ppermute | solution.py:229
  128.2 21.7 %middle.1 = (bf16[1536,768]{1,0:T(8,128)(2,1)S(1)}, bf16[1536,1280]{1,0:T(8,128)(2,1)S(1)}, f32[21,256,256]{2,1,0:T(8,128)}, f32[8,128]{1,0:T(8,128)S(1)}) custom-call(s32[1]{0:T(128)S(6)} %convert_element_type.7.flag, f32[21,256,256]{2,1,0:T(8,128)} %copy-done.9, f32[21,256,256]{2,1,0:T(8,128)} %collective-permute-done.3.other_in, ...), custom_call_target="tpu_custom_call" | custom-call | flops 18119393280 | bytes 29102080 | tf_op jit(solution)/shard_map/middle/pallas_call | solution.py:534
  150.8 8.5 %collective-permute-done.4.other_in = f32[21,256,256]{2,1,0:T(8,128)S(1)} collective-permute-done((f32[21,256,256]{2,1,0:T(8,128)}, f32[21,256,256]{2,1,0:T(8,128)S(1)}, u32[]{:S(2)}, u32[]{:S(2)}) %collective-permute-start.4) | collective-permute-done | bytes 5505056 | tf_op jit(solution)/shard_map/ppermute | solution.py:229
  164.2 9.8 %last.1 = (bf16[1536,1536]{1,0:T(8,128)(2,1)S(1)}, bf16[1536,512]{1,0:T(8,128)(2,1)S(1)}, bf16[1536,256]{1,0:T(8,128)(2,1)S(1)}, bf16[1536,256]{1,0:T(8,128)(2,1)S(1)}, bf16[1536,256]{1,0:T(8,128)(2,1)S(1)}) custom-call(s32[1]{0:T(128)S(6)} %convert_element_type.7.flag, f32[1]{0:T(128)S(6)} %select_n.63.factor, f32[21,256,256]{2,1,0:T(8,128)S(1)} %copy-done.8, ...), custom_call_target="tpu_custom_call" | custom-call | flops 9663676416 | bytes 23592960 | tf_op jit(solution)/shard_map/last/pallas_call | solution.py:534
  174.0 6.5 %finish.1 = bf16[1536,768]{1,0:T(8,128)(2,1)S(1)} custom-call(f32[1]{0:T(128)S(6)} %select_n.63.factor, bf16[1536,1536]{1,0:T(8,128)(2,1)S(1)} %get-tuple-element.40.polynomial_in, bf16[1536,768]{1,0:T(8,128)(2,1)S(1)} %get-tuple-element.41.x_in), custom_call_target="tpu_custom_call" | custom-call | flops 3623878656 | bytes 9437184 | tf_op jit(solution)/shard_map/finish/pallas_call | solution.py:534
  181.9 36.8 %all-to-all-start.2 = ((bf16[16,96,768]{2,1,0:T(8,128)(2,1)}), bf16[16,96,768]{2,1,0:T(8,128)(2,1)S(1)}, u32[]{:S(2)}, u32[]{:S(2)}) async-start(bf16[16,96,768]{2,1,0:T(8,128)(2,1)} %bitcast.39), calls=%async_computation.2 | async-start | bytes 4718592 | tf_op jit(solution)/shard_map/all_to_all | solution.py:752
  223.3 3.4 collective-permute-start.8
  226.7 30.1 %collective-permute-done.8 = f32[16]{0:T(128)S(1)} collective-permute-done((f32[16]{0:T(128)S(1)}, f32[16]{0:T(128)S(1)}, u32[]{:S(2)}, u32[]{:S(2)}) %collective-permute-start.8) | collective-permute-done | bytes 96 | tf_op jit(solution)/shard_map/ppermute | solution.py:623
  256.8 3.5 %collective-permute-done.9 = f32[16]{0:T(128)S(1)} collective-permute-done((f32[16]{0:T(128)S(1)}, f32[16]{0:T(128)S(1)}, u32[]{:S(2)}, u32[]{:S(2)}) %collective-permute-start.9) | collective-permute-done | bytes 96 | tf_op jit(solution)/shard_map/ppermute | solution.py:623
  260.3 27.0 %collective-permute-start.10 = (f32[16]{0:T(128)S(1)}, f32[16]{0:T(128)S(1)}, u32[]{:S(2)}, u32[]{:S(2)}) collective-permute-start(f32[16]{0:T(128)S(1)} %fusion.7), channel_id=1, source_target_pairs={{0,8},{2,10},{4,12},{6,14},{8,0},{10,2},{12,4},{14,6},{16,24},{18,... | collective-permute-start | bytes 200 | tf_op jit(solution)/shard_map/ppermute | solution.py:623
  288.8 3.8 %collective-permute-start.11 = (f32[16]{0:T(128)S(1)}, f32[16]{0:T(128)S(1)}, u32[]{:S(2)}, u32[]{:S(2)}) collective-permute-start(f32[16]{0:T(128)S(1)} %add.65), channel_id=1, source_target_pairs={{0,16},{2,18},{4,20},{6,22},{8,24},{10,26},{12,28},{14,30},{16,0},... | collective-permute-start | bytes 200 | tf_op jit(solution)/shard_map/ppermute | solution.py:623
  297.8 9.2 %all-to-all-start.3 = ((bf16[16,96,512]{2,1,0:T(8,128)(2,1)}), bf16[16,96,512]{2,1,0:T(8,128)(2,1)}, u32[]{:S(2)}, u32[]{:S(2)}) async-start(bf16[16,96,512]{2,1,0:T(8,128)(2,1)} %bitcast.36), calls=%async_computation.3 | async-start | bytes 3145728 | tf_op jit(solution)/shard_map/all_to_all | solution.py:752
  310.8 3.2 assemble_squares.1
  315.3 24.8 %all-to-all-done.3.second = bf16[16,96,512]{2,1,0:T(8,128)(2,1)} async-done(((bf16[16,96,512]{2,1,0:T(8,128)(2,1)}), bf16[16,96,512]{2,1,0:T(8,128)(2,1)}, u32[]{:S(2)}, u32[]{:S(2)}) %all-to-all-start.3) | async-done | bytes 1572896 | tf_op jit(solution)/shard_map/all_to_all | solution.py:752
  340.1 3.2 assemble_swiglu.1
  (96 shorter events, 33.9 us)
Async XLA Ops:
  12.3 41.7 %all-to-all-start.1 = ((bf16[32,48,512]{2,1,0:T(8,128)(2,1)}), bf16[32,48,512]{2,1,0:T(8,128)(2,1)S(1)}, u32[]{:S(2)}, u32[]{:S(2)}) async-start(bf16[32,48,512]{2,1,0:T(8,128)(2,1)} %get-tuple-element.33), calls=%async_computation.1 | async-start | bytes 3145728 | tf_op jit(solution)/shard_map/all_to_all | solution.py:667
  54.0 57.9 %all-to-all-start = ((bf16[32,48,768]{2,1,0:T(8,128)(2,1)}), bf16[32,48,768]{2,1,0:T(8,128)(2,1)}, u32[]{:S(2)}, u32[]{:S(2)}) async-start(bf16[32,48,768]{2,1,0:T(8,128)(2,1)} %get-tuple-element.32), calls=%async_computation | async-start | bytes 4718592 | tf_op jit(solution)/shard_map/all_to_all | solution.py:670
  62.6 37.4 %collective-permute-start = (bf16[1536,256]{1,0:T(8,128)(2,1)S(1)}, bf16[1536,256]{1,0:T(8,128)(2,1)S(1)}, u32[]{:S(2)}, u32[]{:S(2)}) collective-permute-start(bf16[1536,256]{1,0:T(8,128)(2,1)S(1)} %get-tuple-element.52), channel_id=1, source_target_pairs={{12,8},{22,18},{10,14},{16,20},{6,2},{28,24},{13,9},{23,19},{11,15... | collective-permute-start | bytes 2359304 | tf_op jit(solution)/shard_map/ppermute | solution.py:679
  65.1 34.9 %collective-permute-start.1 = (bf16[1536,256]{1,0:T(8,128)(2,1)S(1)}, bf16[1536,256]{1,0:T(8,128)(2,1)S(1)}, u32[]{:S(2)}, u32[]{:S(2)}) collective-permute-start(bf16[1536,256]{1,0:T(8,128)(2,1)S(1)} %get-tuple-element.51), channel_id=1, source_target_pairs={{0,8},{26,18},{6,14},{28,20},{4,2},{30,24},{1,9},{27,19},{7,15},{2... | collective-permute-start | bytes 2359304 | tf_op jit(solution)/shard_map/ppermute | solution.py:679
  65.8 34.2 %collective-permute-start.2 = (bf16[1536,256]{1,0:T(8,128)(2,1)S(1)}, bf16[1536,256]{1,0:T(8,128)(2,1)S(1)}, u32[]{:S(2)}, u32[]{:S(2)}) collective-permute-start(bf16[1536,256]{1,0:T(8,128)(2,1)S(1)} %get-tuple-element.50), channel_id=1, source_target_pairs={{10,8},{16,18},{12,14},{22,20},{0,2},{26,24},{11,9},{17,19},{13,15... | collective-permute-start | bytes 2359304 | tf_op jit(solution)/shard_map/ppermute | solution.py:679
  113.1 15.1 %copy-start.14 = (bf16[1536,256]{1,0:T(8,128)(2,1)S(1)}, bf16[1536,256]{1,0:T(8,128)(2,1)}, u32[]{:S(2)}) copy-start(bf16[1536,256]{1,0:T(8,128)(2,1)} %copy-done.12) | copy-start | bytes 2359300
  119.0 9.2 %collective-permute-start.3 = (f32[21,256,256]{2,1,0:T(8,128)S(1)}, f32[21,256,256]{2,1,0:T(8,128)}, u32[]{:S(2)}, u32[]{:S(2)}) collective-permute-start(f32[21,256,256]{2,1,0:T(8,128)S(1)} %gram.1.own_in), channel_id=1, source_target_pairs={{0,1},{1,0},{2,3},{3,2},{4,5},{5,4},{6,7},{7,6},{8,9},{9,8},{10,11... | collective-permute-start | bytes 16515080 | tf_op jit(solution)/shard_map/ppermute | solution.py:229
  149.9 9.3 %collective-permute-start.4 = (f32[21,256,256]{2,1,0:T(8,128)}, f32[21,256,256]{2,1,0:T(8,128)S(1)}, u32[]{:S(2)}, u32[]{:S(2)}) collective-permute-start(f32[21,256,256]{2,1,0:T(8,128)} %get-tuple-element.34.own_in), channel_id=1, source_target_pairs={{0,1},{1,0},{2,3},{3,2},{4,5},{5,4},{6,7},{7,6},{8,9},{9,8},{10,11... | collective-permute-start | bytes 16515080 | tf_op jit(solution)/shard_map/ppermute | solution.py:229
  181.9 115.8 %all-to-all-start.2 = ((bf16[16,96,768]{2,1,0:T(8,128)(2,1)}), bf16[16,96,768]{2,1,0:T(8,128)(2,1)S(1)}, u32[]{:S(2)}, u32[]{:S(2)}) async-start(bf16[16,96,768]{2,1,0:T(8,128)(2,1)} %bitcast.39), calls=%async_computation.2 | async-start | bytes 4718592 | tf_op jit(solution)/shard_map/all_to_all | solution.py:752
  218.8 75.4 %collective-permute-start.5 = (bf16[1536,256]{1,0:T(8,128)(2,1)}, bf16[1536,256]{1,0:T(8,128)(2,1)S(1)}, u32[]{:S(2)}, u32[]{:S(2)}) collective-permute-start(bf16[1536,256]{1,0:T(8,128)(2,1)} %copy-done.11), channel_id=1, source_target_pairs={{8,12},{18,22},{14,10},{20,16},{2,6},{24,28},{9,13},{19,23},{15,11... | collective-permute-start | bytes 2359304 | tf_op jit(solution)/shard_map/ppermute | solution.py:737
  220.1 74.1 %collective-permute-start.6 = (bf16[1536,256]{1,0:T(8,128)(2,1)}, bf16[1536,256]{1,0:T(8,128)(2,1)S(1)}, u32[]{:S(2)}, u32[]{:S(2)}) collective-permute-start(bf16[1536,256]{1,0:T(8,128)(2,1)} %copy-done.10), channel_id=1, source_target_pairs={{8,0},{18,26},{14,6},{20,28},{2,4},{24,30},{9,1},{19,27},{15,7},{2... | collective-permute-start | bytes 2359304 | tf_op jit(solution)/shard_map/ppermute | solution.py:737
  220.8 73.4 %collective-permute-start.7 = (bf16[1536,256]{1,0:T(8,128)(2,1)S(1)}, bf16[1536,256]{1,0:T(8,128)(2,1)S(1)}, u32[]{:S(2)}, u32[]{:S(2)}) collective-permute-start(bf16[1536,256]{1,0:T(8,128)(2,1)S(1)} %get-tuple-element.39), channel_id=1, source_target_pairs={{8,10},{18,16},{14,12},{20,22},{2,0},{24,26},{9,11},{19,17},{15,13... | collective-permute-start | bytes 2359304 | tf_op jit(solution)/shard_map/ppermute | solution.py:737
  223.3 33.5 %collective-permute-start.8 = (f32[16]{0:T(128)S(1)}, f32[16]{0:T(128)S(1)}, u32[]{:S(2)}, u32[]{:S(2)}) collective-permute-start(f32[16]{0:T(128)S(1)} %compare_select_fusion.1), channel_id=1, source_target_pairs={{0,2},{2,0},{4,6},{6,4},{8,10},{10,8},{12,14},{14,12},{16,18},{18,... | collective-permute-start | bytes 200 | tf_op jit(solution)/shard_map/ppermute | solution.py:623
  256.8 3.5 %collective-permute-start.9 = (f32[16]{0:T(128)S(1)}, f32[16]{0:T(128)S(1)}, u32[]{:S(2)}, u32[]{:S(2)}) collective-permute-start(f32[16]{0:T(128)S(1)} %fusion.6), channel_id=1, source_target_pairs={{0,4},{2,6},{4,0},{6,2},{8,12},{10,14},{12,8},{14,10},{16,20},{18,... | collective-permute-start | bytes 200 | tf_op jit(solution)/shard_map/ppermute | solution.py:623
  260.3 28.5 %collective-permute-start.10 = (f32[16]{0:T(128)S(1)}, f32[16]{0:T(128)S(1)}, u32[]{:S(2)}, u32[]{:S(2)}) collective-permute-start(f32[16]{0:T(128)S(1)} %fusion.7), channel_id=1, source_target_pairs={{0,8},{2,10},{4,12},{6,14},{8,0},{10,2},{12,4},{14,6},{16,24},{18,... | collective-permute-start | bytes 200 | tf_op jit(solution)/shard_map/ppermute | solution.py:623
  288.8 5.4 %collective-permute-start.11 = (f32[16]{0:T(128)S(1)}, f32[16]{0:T(128)S(1)}, u32[]{:S(2)}, u32[]{:S(2)}) collective-permute-start(f32[16]{0:T(128)S(1)} %add.65), channel_id=1, source_target_pairs={{0,16},{2,18},{4,20},{6,22},{8,24},{10,26},{12,28},{14,30},{16,0},... | collective-permute-start | bytes 200 | tf_op jit(solution)/shard_map/ppermute | solution.py:623
  297.7 9.8 %copy-start.21 = (s32[16,2]{0,1:T(2,128)S(1)}, s32[16,2]{0,1:T(2,128)}, u32[]{:S(2)}) copy-start(s32[16,2]{0,1:T(2,128)} %param.38) | copy-start | bytes 388
  297.7 9.9 %copy-start.17 = (f32[1344]{0:T(1024)S(1)}, f32[1344]{0:T(1024)}, u32[]{:S(2)}) copy-start(f32[1344]{0:T(1024)} %param.30) | copy-start | bytes 16132
  297.7 9.9 %copy-start.18 = (f32[1344]{0:T(1024)S(1)}, f32[1344]{0:T(1024)}, u32[]{:S(2)}) copy-start(f32[1344]{0:T(1024)} %param.31) | copy-start | bytes 16132
  297.7 9.9 %copy-start.19 = (f32[1344]{0:T(1024)S(1)}, f32[1344]{0:T(1024)}, u32[]{:S(2)}) copy-start(f32[1344]{0:T(1024)} %param.32) | copy-start | bytes 16132
  297.7 9.9 %copy-start.20 = (f32[1344]{0:T(1024)S(1)}, f32[1344]{0:T(1024)}, u32[]{:S(2)}) copy-start(f32[1344]{0:T(1024)} %param.33) | copy-start | bytes 16132
  297.7 10.5 %copy-start.15 = (f32[128,768]{1,0:T(8,128)S(1)}, f32[128,768]{1,0:T(8,128)}, u32[]{:S(2)}) copy-start(f32[128,768]{1,0:T(8,128)} %param.37) | copy-start | bytes 1179652
  297.7 10.5 %copy-start.16 = (f32[128,768]{1,0:T(8,128)S(1)}, f32[128,768]{1,0:T(8,128)}, u32[]{:S(2)}) copy-start(f32[128,768]{1,0:T(8,128)} %param.35) | copy-start | bytes 1179652
  297.8 42.4 %all-to-all-start.3 = ((bf16[16,96,512]{2,1,0:T(8,128)(2,1)}), bf16[16,96,512]{2,1,0:T(8,128)(2,1)}, u32[]{:S(2)}, u32[]{:S(2)}) async-start(bf16[16,96,512]{2,1,0:T(8,128)(2,1)} %bitcast.36), calls=%async_computation.3 | async-start | bytes 3145728 | tf_op jit(solution)/shard_map/all_to_all | solution.py:752
  (20 other events, 101.9 us)

commit v6 on v5

--- a/solution.py
+++ b/solution.py
@@ -58,36 +58,58 @@
         order = [c for pair in zip(low, high) for c in pair]
         self.heavy = order[:swiglu_count]
         rest = order[swiglu_count:]
-        self.light = rest[:square_count]
+        near = lambda c: sum(hops(c, o) == 1 for o in self.heavy)
+        half = lambda c: coords(c)[2] < planes // 2
+        spare = len(rest) - square_count
+        self.idle = []
+        for want in (True, False):
+            pool = sorted((c for c in rest if half(c) == want), key=lambda c: -near(c))
+            self.idle += pool[: spare // 2 if want else spare - spare // 2]
+        self.light = [c for c in rest if c not in self.idle]
         helpers = rest
         narrow = D // cores
         wide = FF // cores
         self.granules = (wide - narrow) // GRANULE
         self.passes = self.granules - 2
         count = len(helpers)
-        take = [
-            [helpers[(k + p * swiglu_count) % count] for k in range(swiglu_count)]
-            for p in range(self.passes)
-        ]
-        cost = lambda p, k, h: hops(h, self.heavy[k]) ** 2
-        better = True
-        while better:
-            better = False
-            places = [(p, k) for p in range(self.passes) for k in range(swiglu_count)]
-            for p, k in places:
-                for h in helpers:
-                    used = sum(row.count(h) for row in take)
-                    if used < 2 and h not in take[p] and cost(p, k, h) < cost(p, k, take[p][k]):
-                        take[p][k] = h
-                        better = True
-                for q, m in places:
-                    a, b = take[p][k], take[q][m]
-                    if a == b or (q != p and (b in take[p] or a in take[q])):
-                        continue
-                    if cost(p, k, b) + cost(q, m, a) < cost(p, k, a) + cost(q, m, b):
-                        take[p][k], take[q][m] = b, a
-                        better = True
-        self.take = take
+        cost = lambda k, h: hops(h, self.heavy[k]) ** 2
+        places = [(p, k) for p in range(self.passes) for k in range(swiglu_count)]
+
+        def search(room):
+            take = [
+                [helpers[(k + p * swiglu_count) % count] for k in range(swiglu_count)]
+                for p in range(self.passes)
+            ]
+            better = True
+            while better:
+                better = False
+                for p, k in places:
+                    for h in helpers:
+                        used = sum(row.count(h) for row in take)
+                        if used < room(h) and h not in take[p] and cost(k, h) < cost(k, take[p][k]):
+                            take[p][k] = h
+                            better = True
+                    for q, m in places:
+                        a, b = take[p][k], take[q][m]
+                        if a == b or (q != p and (b in take[p] or a in take[q])):
+                            continue
+                        if cost(k, b) + cost(m, a) < cost(k, a) + cost(m, b):
+                            take[p][k], take[q][m] = b, a
+                            better = True
+            return take
+
+        self.take = take = search(lambda h: 2)
+        self.back = search(lambda h: 3 if h in self.idle else 2)
+        self.column = {}
+        self.choice = np.zeros((chips, 3), np.int32)
+        for j, o in enumerate(self.heavy):
+            self.column[(j, 0)], self.column[(j, 1)] = (o, narrow), (o, narrow + GRANULE)
+        taken = {}
+        for p, k in places:
+            h = self.back[p][k]
+            where = taken[h] = taken.get(h, -1) + 1
+            self.choice[h, where] = 1 + p
+            self.column[(k, 2 + p)] = (h, narrow + where * GRANULE if where < 2 else 0)
         self.held = {o: [(j, 0), (j, 1)] for j, o in enumerate(self.heavy)}
         self.place = {}
         for p in range(self.passes):
@@ -102,7 +124,6 @@
         for p in range(self.passes):
             for k in range(swiglu_count):
                 self.slot_in_pass[p, take[p][k]] = self.place[(k, 2 + p)][1] == 1
-        self.idle = [c for c in range(chips) if c not in self.heavy and c not in self.light]
 
 
 def momentum_rows(grad, state, following, sent):
@@ -490,7 +511,8 @@
         return pltpu.make_async_copy(rows_of(polynomial_in, i), rows_of(polynomial, i), in_sems.at[i])
 
     def out_copy(i):
-        return pltpu.make_async_copy(rows_of(mixed, i), rows_of(out, i), out_sems.at[i])
+        target = out.at[span(i), pl.ds(0, x.shape[1])]
+        return pltpu.make_async_copy(rows_of(mixed, i), target, out_sems.at[i])
 
     start_all([in_copy(i) for i in range(EDGE)])
     x_copy.wait()
@@ -507,25 +529,43 @@
 
 
 def join_kernel(pick, own, *refs):
-    handed, (out, stage, in_sems, out_sem) = refs[:-4], refs[-4:]
-    for where in range(2):
+    handed, (given, out, stage, in_sems, out_sems) = refs[:-5], refs[-5:]
+    narrow = out.shape[1] - 2 * GRANULE
+
+    def incoming(where, source):
         target = columns_of(stage, where * GRANULE, GRANULE)
+        return pltpu.make_async_copy(source, target, in_sems.at[where])
+
+    def outgoing(where):
+        at = narrow + where * GRANULE if where < 2 else 0
+        source = columns_of(stage, where * GRANULE, GRANULE)
+        return pltpu.make_async_copy(source, columns_of(out, at, GRANULE), out_sems.at[where])
+
+    for where in range(3):
         for k in range(1 + len(handed)):
+            if where == 2 and k == 0:
+                continue
             source = columns_of(own, where * GRANULE, GRANULE) if k == 0 else handed[k - 1]
 
             @pl.when(pick[where] == k)
             def _():
-                pltpu.make_async_copy(source, target, in_sems.at[where]).start()
+                incoming(where, source).start()
 
     for where in range(2):
-        target = columns_of(stage, where * GRANULE, GRANULE)
-        pltpu.make_async_copy(columns_of(own, 0, GRANULE), target, in_sems.at[where]).wait()
-    copy = pltpu.make_async_copy(stage, out, out_sem)
-    copy.start()
-    copy.wait()
-
-
-def call(kernel, name, scalars, arrays, outs, scratch, limit, flops, small_outs=0):
+        incoming(where, columns_of(own, 0, GRANULE)).wait()
+        outgoing(where).start()
+
+    @pl.when(pick[2] > 0)
+    def _():
+        incoming(2, columns_of(own, 0, GRANULE)).wait()
+        outgoing(2).start()
+        outgoing(2).wait()
+
+    for where in range(2):
+        outgoing(where).wait()
+
+
+def call(kernel, name, scalars, arrays, outs, scratch, limit, flops, small_outs=0, aliases=None):
     moved = sum(x.size * x.dtype.itemsize for x in arrays)
     moved += sum(math.prod(o.shape) * o.dtype.itemsize for o in outs)
     smem = pl.BlockSpec(memory_space=pltpu.SMEM)
@@ -537,83 +577,75 @@
         out_specs=[anywhere] * (len(outs) - small_outs) + [vmem] * small_outs,
         out_shape=list(outs),
         scratch_shapes=list(scratch),
+        input_output_aliases=aliases or {},
         compiler_params=pltpu.CompilerParams(vmem_limit_bytes=limit * MIB),
         cost_estimate=pl.CostEstimate(flops=flops, bytes_accessed=moved, transcendentals=0),
         name=name,
     )(*scalars, *arrays)
 
 
-def assemble(kernel, name, order, arrays, shape, copies):
+def assemble(plan, square_order, swiglu_order, back):
+    squares, wides = square_order.shape[0], swiglu_order.shape[0]
+    rows, both = back.shape[1:]
+    narrow = both - 2 * GRANULE
+    wide = narrow + plan.granules * GRANULE
+    parts = 1 + plan.passes
+
+    def kernel(
+        square_to, wide_to, source, square_out, wide_out, square_stage, wide_stage, *sems
+    ):
+        square_in, wide_in, square_sems, wide_sems = sems
+        square_copies = [
+            [
+                pltpu.make_async_copy(
+                    source.at[plan.light[j], :, pl.ds(0, narrow)], square_stage.at[j], square_in.at[j]
+                )
+            ]
+            for j in range(squares)
+        ]
+        wide_copies = []
+        for j in range(wides):
+            moves = [(plan.heavy[j], 0, 0, both)]
+            for b in range(2, plan.granules):
+                chip, at = plan.column[(j, b)]
+                moves.append((chip, at, narrow + b * GRANULE, GRANULE))
+            wide_copies.append(
+                [
+                    pltpu.make_async_copy(
+                        source.at[chip, :, pl.ds(at, width)],
+                        wide_stage.at[j, :, pl.ds(to, width)],
+                        wide_in.at[j * parts + n],
+                    )
+                    for n, (chip, at, to, width) in enumerate(moves)
+                ]
+            )
+        for slot in square_copies + wide_copies:
+            start_all(slot)
+        outs = []
+        for copies, stage, out, order, out_sems in (
+            (square_copies, square_stage, square_out, square_to, square_sems),
+            (wide_copies, wide_stage, wide_out, wide_to, wide_sems),
+        ):
+            for j, slot in enumerate(copies):
+                wait_all(slot)
+                outs.append(pltpu.make_async_copy(stage.at[j], out.at[order[j]], out_sems.at[j]))
+                outs[-1].start()
+        wait_all(outs)
+
+    smem = pl.BlockSpec(memory_space=pltpu.SMEM)
     anywhere = pl.BlockSpec(memory_space=pl.ANY)
+    shapes = [(squares, rows, narrow), (wides, rows, wide)]
+    dma = pltpu.SemaphoreType.DMA
     return pl.pallas_call(
         kernel,
-        in_specs=[pl.BlockSpec(memory_space=pltpu.SMEM)] + [anywhere] * len(arrays),
-        out_specs=anywhere,
-        out_shape=jax.ShapeDtypeStruct(shape, jnp.bfloat16),
-        scratch_shapes=[
-            pltpu.VMEM(shape, jnp.bfloat16),
-            pltpu.SemaphoreType.DMA((copies,)),
-            pltpu.SemaphoreType.DMA((shape[0],)),
-        ],
-        compiler_params=pltpu.CompilerParams(vmem_limit_bytes=8 * MIB),
-        name=name,
-    )(order, *arrays)
-
-
-def place_slots(order, stage, out, copies, out_sems):
-    for slot in copies:
-        start_all(slot)
-    outs = []
-    for j, slot in enumerate(copies):
-        wait_all(slot)
-        outs.append(pltpu.make_async_copy(stage.at[j], out.at[order[j]], out_sems.at[j]))
-        outs[-1].start()
-    wait_all(outs)
-
-
-def assemble_squares(plan, square_order, first_back):
-    count = square_order.shape[0]
-
-    def kernel(order, source, out, stage, in_sems, out_sems):
-        copies = [
-            [pltpu.make_async_copy(source.at[plan.light[j]], stage.at[j], in_sems.at[j])]
-            for j in range(count)
-        ]
-        place_slots(order, stage, out, copies, out_sems)
-
-    shape = (count,) + first_back.shape[1:]
-    return assemble(kernel, "assemble_squares", square_order, [first_back], shape, count)
-
-
-def assemble_swiglu(plan, swiglu_order, first_back, second_back):
-    count = swiglu_order.shape[0]
-    rows, narrow = first_back.shape[1:]
-    wide = narrow + plan.granules * GRANULE
-
-    def kernel(order, first, second, out, stage, in_sems, out_sems):
-        copies = []
-        for j in range(count):
-            moves = [
-                (first.at[plan.heavy[j]], 0, narrow),
-                (second.at[plan.heavy[j]], narrow, 2 * GRANULE),
-            ]
-            for b in range(2, plan.granules):
-                chip, where = plan.place[(j, b)]
-                source = second.at[chip, :, pl.ds(where * GRANULE, GRANULE)]
-                moves.append((source, narrow + b * GRANULE, GRANULE))
-            copies.append(
-                [
-                    pltpu.make_async_copy(
-                        source, stage.at[j, :, pl.ds(at, width)], in_sems.at[j * len(moves) + k]
-                    )
-                    for k, (source, at, width) in enumerate(moves)
-                ]
-            )
-        place_slots(order, stage, out, copies, out_sems)
-
-    arrays = [first_back, second_back]
-    shape = (count, rows, wide)
-    return assemble(kernel, "assemble_swiglu", swiglu_order, arrays, shape, count * plan.granules)
+        in_specs=[smem, smem, anywhere],
+        out_specs=[anywhere, anywhere],
+        out_shape=[jax.ShapeDtypeStruct(shape, jnp.bfloat16) for shape in shapes],
+        scratch_shapes=[pltpu.VMEM(shape, jnp.bfloat16) for shape in shapes]
+        + [dma((squares,)), dma((wides * parts,)), dma((squares,)), dma((wides,))],
+        compiler_params=pltpu.CompilerParams(vmem_limit_bytes=12 * MIB),
+        name="assemble",
+    )(square_order, swiglu_order, back)
 
 
 def spread(value, chips, chip):
@@ -728,51 +760,42 @@
         + [second_buffer] * 2
         + [square_buffer] * 2
         + [sems(GROUPS), sems(GROUPS), sems(), sems(), sems(1 + plan.passes, EDGE)],
-        32,
+        56,
         D * D * D + 2 * D * D * extra,
     )
     handed = []
     for p in range(plan.passes):
-        pairs = [(plan.heavy[k], plan.take[p][k]) for k in range(swiglu_count)]
+        pairs = [(plan.heavy[k], plan.back[p][k]) for k in range(swiglu_count)]
         handed.append(lax.ppermute(rest[p], "dp", pairs))
-    (first_done,) = call(
+    back_shape = jax.ShapeDtypeStruct((D, narrow + 2 * GRANULE), jnp.bfloat16)
+    (back_out,) = call(
         finish_kernel,
         "finish",
         [factor],
         [polynomial, first_mid],
-        [first_shape],
+        [back_shape],
         [first_buffer] * 2 + [square_buffer, sems(), sems(EDGE), sems(EDGE)],
-        14,
+        56,
         2 * D * D * narrow,
     )
-    scale, _ = lax.optimization_barrier((scale, first_done))
+    scale, _ = lax.optimization_barrier((scale, kept))
     logs = spread(0.5 * jnp.log(scale[0, 0]), chips, chip)
-
-    def send_back(x):
-        return lax.all_to_all(
-            x.reshape(chips, chip_rows, -1), "dp", split_axis=0, concat_axis=0, tiled=True
-        )
-
-    first_back = send_back(first_done)
-    choice = np.zeros((chips, 2), np.int32)
-    for p in range(plan.passes):
-        for k in range(swiglu_count):
-            choice[plan.take[p][k], plan.place[(k, 2 + p)][1]] = 1 + p
-    (second_out,) = call(
+    (back_out,) = call(
         join_kernel,
         "join",
-        [jnp.asarray(choice)[chip]],
-        [kept, *handed],
-        [pair_shape],
-        [pltpu.VMEM(pair_shape.shape, jnp.bfloat16), sems(2), sems()],
-        4,
+        [jnp.asarray(plan.choice)[chip]],
+        [kept, *handed, back_out],
+        [back_shape],
+        [pltpu.VMEM((D, 3 * GRANULE), jnp.bfloat16), sems(3), sems(3)],
+        56,
         0,
-    )
-    second_out, first_back, logs = lax.optimization_barrier((second_out, first_back, logs))
-    second_back = send_back(second_out)
-
-    square_update = assemble_squares(plan, square_order, first_back)
-    swiglu_update = assemble_swiglu(plan, swiglu_order, first_back, second_back)
+        aliases={2 + plan.passes: 0},
+    )
+    back_out, logs = lax.optimization_barrier((back_out, logs))
+    back = lax.all_to_all(
+        back_out.reshape(chips, chip_rows, -1), "dp", split_axis=0, concat_axis=0, tiled=True
+    )
+    square_update, swiglu_update = assemble(plan, square_order, swiglu_order, back)
 
     slot_chips = np.array(plan.light + plan.heavy, np.int32)
     slot_owner = jnp.concatenate(

time: 344 us -> 342 us (level)
  starting transfers between devices: 102 us -> 62.2 us
  waiting for transfers between devices: 147 us -> 182 us
  Pallas kernels: 67.7 us -> 73.2 us
    all_to_all x2 -> x1, waiting for transfers between devices: 24.8 us -> 82.3 us  [local(): lax.all_to_all(back_out.reshape(chips, chip_rows, -1), 'dp', split_axis=0...]
    all_to_all x2 -> x1, starting transfers between devices: 46.1 us -> 4.56 us  [local(): lax.all_to_all(back_out.reshape(chips, chip_rows, -1), 'dp', split_axis=0...]
    ppermute x4, waiting for transfers between devices: 35.9 us -> 13.9 us  [spread(): lax.ppermute(known, 'dp', [(s, s ^ step) for s in range(chips)])]
    pallas_call x5, Pallas kernels: 44.6 us -> 52 us  [call(): pl.pallas_call(kernel, in_specs=[smem] * len(scalars) + [anywhere] * len(...]
    unnamed x56 -> x54, local copies, waits for them, and re-layouts: 14.4 us -> 11.6 us
  transfers between devices with their start and end apart: 16 -> 15, of which waited for: 10 -> 9; matrix products, arithmetic and copies ran while one was open for 3% -> 3% of each run, Pallas kernels for 3% -> 4%
where the time goes in v6:
time: 342 us
  waiting for transfers between devices  182 us (53%)
  Pallas kernels  73.2 us (21%)
  starting transfers between devices  62.2 us (18%)
  local copies, waits for them, and re-layouts  15.9 us (5%)
  other arithmetic  4.66 us (1%)
    all_to_all x1, waiting for transfers between devices, local(): lax.all_to_all(back_out.reshape(chips, chip_rows, -1), 'dp', split_axis=0...  82.3 us
    pallas_call x5, Pallas kernels, call(): pl.pallas_call(kernel, in_specs=[smem] * len(scalars) + [anywhere] * len(...  52 us
    ppermute x4, starting transfers between devices, spread(): lax.ppermute(known, 'dp', [(s, s ^ step) for s in range(chips)])  36.3 us
    ppermute x3, waiting for transfers between devices, local(): lax.ppermute(jnp.where(pick, pieces[1], pieces[0]), 'dp', pairs)  30.1 us
    all_to_all x1, waiting for transfers between devices, local(): lax.all_to_all(second_send.reshape(D, 2 * GRANULE), both, split_axis=0, c...  27.3 us
    ppermute x2, waiting for transfers between devices, other_core(): return lax.ppermute(x, 'tensor', [(0, 1), (1, 0)])  17.6 us
    ppermute x4, waiting for transfers between devices, spread(): lax.ppermute(known, 'dp', [(s, s ^ step) for s in range(chips)])  13.9 us
    pallas_call x1, Pallas kernels, prepare_wide(): pl.pallas_call(lambda *refs: wide_kernel(plan, cores, *refs), grid=(rows...  11.7 us
  transfers between devices with their start and end apart: 15, of which 9 were waited for; matrix products, arithmetic and copies ran while one was open for 3% of the time, Pallas kernels for 4%

profile of v6, /device:TPU:12, one launch (start us, length us, event | category | flops | bytes accessed | tf_op | source)
XLA Modules:
  0.0 341.6 jit_solution(5349501037645899489)
XLA Ops:
  0.6 11.7 %prepare_wide.1 = (f32[48,32,6,128]{3,2,1,0:T(8,128)}, bf16[32,48,768]{2,1,0:T(8,128)(2,1)}, bf16[32,48,512]{2,1,0:T(8,128)(2,1)}) custom-call(f32[48,32,6,128]{3,2,1,0:T(8,128)} %bitcast.38, f32[48,32,6,128]{3,2,1,0:T(8,128)} %bitcast.39), custom_call_target="tpu_custom_call" | custom-call | tf_op jit(solution)/shard_map/prepare_wide/pallas_call | solution.py:199
  12.3 6.0 %all-to-all-start.1 = ((bf16[32,48,512]{2,1,0:T(8,128)(2,1)}), bf16[32,48,512]{2,1,0:T(8,128)(2,1)S(1)}, u32[]{:S(2)}, u32[]{:S(2)}) async-start(bf16[32,48,512]{2,1,0:T(8,128)(2,1)} %get-tuple-element.34), calls=%async_computation.1 | async-start | bytes 3145728 | tf_op jit(solution)/shard_map/all_to_all | solution.py:699
  21.7 5.1 %prepare_narrow.1 = (f32[48,12,8,128]{3,2,1,0:T(8,128)}, bf16[32,48,768]{2,1,0:T(8,128)(2,1)}) custom-call(f32[48,12,8,128]{3,2,1,0:T(8,128)S(1)} %bitcast.35, f32[48,12,8,128]{3,2,1,0:T(8,128)S(1)} %bitcast.36, bf16[32,48,768]{2,1,0:T(8,128)(2,1)} %get-tuple-element.30.refs_2_), custom_call_target="tpu_custom_call", output_to_operand_aliasing={{1}: (2, {})} | custom-call | bytes 8257536 | tf_op jit(solution)/shard_map/prepare_narrow/pallas_call | solution.py:226
  26.8 27.3 %all-to-all-done.1 = bf16[32,48,512]{2,1,0:T(8,128)(2,1)S(1)} async-done(((bf16[32,48,512]{2,1,0:T(8,128)(2,1)}), bf16[32,48,512]{2,1,0:T(8,128)(2,1)S(1)}, u32[]{:S(2)}, u32[]{:S(2)}) %all-to-all-start.1) | async-done | bytes 1572896 | tf_op jit(solution)/shard_map/all_to_all | solution.py:699
  54.1 5.8 %all-to-all-start = ((bf16[32,48,768]{2,1,0:T(8,128)(2,1)}), bf16[32,48,768]{2,1,0:T(8,128)(2,1)}, u32[]{:S(2)}, u32[]{:S(2)}) async-start(bf16[32,48,768]{2,1,0:T(8,128)(2,1)} %get-tuple-element.33), calls=%async_computation | async-start | bytes 4718592 | tf_op jit(solution)/shard_map/all_to_all | solution.py:702
  62.6 2.5 collective-permute-start
  65.8 2.8 collective-permute-start.2
  69.8 30.1 %collective-permute-done.refs_2_ = bf16[1536,256]{1,0:T(8,128)(2,1)S(1)} collective-permute-done((bf16[1536,256]{1,0:T(8,128)(2,1)S(1)}, bf16[1536,256]{1,0:T(8,128)(2,1)S(1)}, u32[]{:S(2)}, u32[]{:S(2)}) %collective-permute-start) | collective-permute-done | bytes 786464 | tf_op jit(solution)/shard_map/ppermute | solution.py:711
  100.9 11.1 %all-to-all-done = bf16[32,48,768]{2,1,0:T(8,128)(2,1)} async-done(((bf16[32,48,768]{2,1,0:T(8,128)(2,1)}), bf16[32,48,768]{2,1,0:T(8,128)(2,1)}, u32[]{:S(2)}, u32[]{:S(2)}) %all-to-all-start) | async-done | bytes 2359328 | tf_op jit(solution)/shard_map/all_to_all | solution.py:702
  113.1 5.8 %gram.1.own_in = f32[21,256,256]{2,1,0:T(8,128)S(1)} custom-call(s32[1]{0:T(128)S(6)} %convert_element_type.7.flag, bf16[1536,768]{1,0:T(8,128)(2,1)} %bitcast.13.refs_0_, bf16[1536,512]{1,0:T(8,128)(2,1)S(1)} %bitcast.33, bf16[1536,256]{1,0:T(8,128)(2,1)S(1)} %collective-permute-done.refs_2_, bf16[1536,256]{1,0:T(8,128)(2,1)S(1)} %collective-permute-done.1.refs_3_, ...), custom_call_target="tpu_custom_call" | custom-call | flops 4831838208 | bytes 11796480 | tf_op jit(solution)/shard_map/gram/pallas_call | solution.py:574
  119.0 9.0 %collective-permute-done.3.other_in = f32[21,256,256]{2,1,0:T(8,128)S(1)} collective-permute-done((f32[21,256,256]{2,1,0:T(8,128)S(1)}, f32[21,256,256]{2,1,0:T(8,128)S(1)}, u32[]{:S(2)}, u32[]{:S(2)}) %collective-permute-start.3) | collective-permute-done | bytes 5505056 | tf_op jit(solution)/shard_map/ppermute | solution.py:250
  128.0 2.4 copy-done.22
  130.4 21.6 %middle.1 = (bf16[1536,768]{1,0:T(8,128)(2,1)S(1)}, bf16[1536,1280]{1,0:T(8,128)(2,1)S(1)}, f32[21,256,256]{2,1,0:T(8,128)}, f32[8,128]{1,0:T(8,128)S(1)}) custom-call(s32[1]{0:T(128)S(6)} %convert_element_type.7.flag, f32[21,256,256]{2,1,0:T(8,128)} %copy-done.4, f32[21,256,256]{2,1,0:T(8,128)} %copy-done.22, bf16[1536,768]{1,0:T(8,128)(2,1)} %bitcast.13.refs_0_, ...), custom_call_target="tpu_custom_call" | custom-call | flops 18119393280 | bytes 29102080 | tf_op jit(solution)/shard_map/middle/pallas_call | solution.py:574
  154.7 8.5 %collective-permute-done.4.other_in = f32[21,256,256]{2,1,0:T(8,128)} collective-permute-done((f32[21,256,256]{2,1,0:T(8,128)}, f32[21,256,256]{2,1,0:T(8,128)}, u32[]{:S(2)}, u32[]{:S(2)}) %collective-permute-start.4) | collective-permute-done | bytes 5505056 | tf_op jit(solution)/shard_map/ppermute | solution.py:250
  163.2 12.9 %last.1 = (bf16[1536,1536]{1,0:T(8,128)(2,1)}, bf16[1536,512]{1,0:T(8,128)(2,1)}, bf16[1536,256]{1,0:T(8,128)(2,1)}, bf16[1536,256]{1,0:T(8,128)(2,1)}, bf16[1536,256]{1,0:T(8,128)(2,1)}) custom-call(s32[1]{0:T(128)S(6)} %convert_element_type.7.flag, f32[1]{0:T(128)S(6)} %select_n.63.factor, f32[21,256,256]{2,1,0:T(8,128)} %get-tuple-element.35.own_in, ...), custom_call_target="tpu_custom_call" | custom-call | flops 9663676416 | bytes 23592960 | tf_op jit(solution)/shard_map/last/pallas_call | solution.py:574
  179.4 27.4 %collective-permute-start.8 = (f32[16]{0:T(128)S(1)}, f32[16]{0:T(128)S(1)}, u32[]{:S(2)}, u32[]{:S(2)}) collective-permute-start(f32[16]{0:T(128)S(1)} %compare_select_fusion.1), channel_id=1, source_target_pairs={{0,2},{2,0},{4,6},{6,4},{8,10},{10,8},{12,14},{14,12},{16,18},{18,... | collective-permute-start | bytes 200 | tf_op jit(solution)/shard_map/ppermute | solution.py:655
  210.2 11.4 %collective-permute-done.9 = f32[16]{0:T(128)S(1)} collective-permute-done((f32[16]{0:T(128)S(1)}, f32[16]{0:T(128)S(1)}, u32[]{:S(2)}, u32[]{:S(2)}) %collective-permute-start.9) | collective-permute-done | bytes 96 | tf_op jit(solution)/shard_map/ppermute | solution.py:655
  222.8 2.3 collective-permute-done.10
  225.1 7.1 %collective-permute-start.11 = (f32[16]{0:T(128)S(1)}, f32[16]{0:T(128)S(1)}, u32[]{:S(2)}, u32[]{:S(2)}) collective-permute-start(f32[16]{0:T(128)S(1)} %add.65), channel_id=1, source_target_pairs={{0,16},{2,18},{4,20},{6,22},{8,24},{10,26},{12,28},{14,30},{16,0},... | collective-permute-start | bytes 200 | tf_op jit(solution)/shard_map/ppermute | solution.py:655
  232.2 8.5 %finish.1.refs_3_ = bf16[1536,1280]{1,0:T(8,128)(2,1)} custom-call(f32[1]{0:T(128)S(6)} %select_n.63.factor, bf16[1536,1536]{1,0:T(8,128)(2,1)} %get-tuple-element.41.polynomial_in, bf16[1536,768]{1,0:T(8,128)(2,1)} %copy-done.7), custom_call_target="tpu_custom_call" | custom-call | flops 3623878656 | bytes 11010048 | tf_op jit(solution)/shard_map/finish/pallas_call | solution.py:574
  242.7 3.2 join.1
  246.1 4.6 %all-to-all-start.2 = ((bf16[16,96,1280]{2,1,0:T(8,128)(2,1)}), bf16[16,96,1280]{2,1,0:T(8,128)(2,1)}, u32[]{:S(2)}, u32[]{:S(2)}) async-start(bf16[16,96,1280]{2,1,0:T(8,128)(2,1)} %bitcast.37), calls=%async_computation.2 | async-start | bytes 7864320 | tf_op jit(solution)/shard_map/all_to_all | solution.py:795
  254.7 82.3 %all-to-all-done.2.source = bf16[16,96,1280]{2,1,0:T(8,128)(2,1)} async-done(((bf16[16,96,1280]{2,1,0:T(8,128)(2,1)}), bf16[16,96,1280]{2,1,0:T(8,128)(2,1)}, u32[]{:S(2)}, u32[]{:S(2)}) %all-to-all-start.2) | async-done | bytes 3932192 | tf_op jit(solution)/shard_map/all_to_all | solution.py:795
  337.0 4.5 %assemble.1 = (bf16[8,96,768]{2,1,0:T(8,128)(2,1)}, bf16[6,96,2048]{2,1,0:T(8,128)(2,1)}) custom-call(s32[8]{0:T(128)S(1)} %copy-done.2, s32[6]{0:T(128)S(1)} %copy-done.3, bf16[16,96,1280]{2,1,0:T(8,128)(2,1)} %all-to-all-done.2.source), custom_call_target="tpu_custom_call" | custom-call | tf_op jit(solution)/shard_map/assemble/pallas_call | solution.py:639
  (91 shorter events, 24.5 us)
Async XLA Ops:
  12.3 41.7 %all-to-all-start.1 = ((bf16[32,48,512]{2,1,0:T(8,128)(2,1)}), bf16[32,48,512]{2,1,0:T(8,128)(2,1)S(1)}, u32[]{:S(2)}, u32[]{:S(2)}) async-start(bf16[32,48,512]{2,1,0:T(8,128)(2,1)} %get-tuple-element.34), calls=%async_computation.1 | async-start | bytes 3145728 | tf_op jit(solution)/shard_map/all_to_all | solution.py:699
  54.1 5.9 %copy-start.26 = (pred[16]{0:T(512)(128)(4,1)S(1)}, pred[16]{0:T(512)(128)(4,1)}, u32[]{:S(2)}) copy-start(pred[16]{0:T(512)(128)(4,1)} %constant.67.clone) | copy-start | bytes 52
  54.1 6.5 %copy-start.25 = (pred[16]{0:T(512)(128)(4,1)S(1)}, pred[16]{0:T(512)(128)(4,1)}, u32[]{:S(2)}) copy-start(pred[16]{0:T(512)(128)(4,1)} %constant.66.clone) | copy-start | bytes 52
  54.1 57.9 %all-to-all-start = ((bf16[32,48,768]{2,1,0:T(8,128)(2,1)}), bf16[32,48,768]{2,1,0:T(8,128)(2,1)}, u32[]{:S(2)}, u32[]{:S(2)}) async-start(bf16[32,48,768]{2,1,0:T(8,128)(2,1)} %get-tuple-element.33), calls=%async_computation | async-start | bytes 4718592 | tf_op jit(solution)/shard_map/all_to_all | solution.py:702
  59.9 8.7 %copy-start.24 = (pred[16]{0:T(512)(128)(4,1)S(1)}, pred[16]{0:T(512)(128)(4,1)}, u32[]{:S(2)}) copy-start(pred[16]{0:T(512)(128)(4,1)} %constant.64.clone) | copy-start | bytes 52
  62.6 37.4 %collective-permute-start = (bf16[1536,256]{1,0:T(8,128)(2,1)S(1)}, bf16[1536,256]{1,0:T(8,128)(2,1)S(1)}, u32[]{:S(2)}, u32[]{:S(2)}) collective-permute-start(bf16[1536,256]{1,0:T(8,128)(2,1)S(1)} %get-tuple-element.54), channel_id=1, source_target_pairs={{12,8},{22,18},{10,14},{16,20},{6,2},{28,24},{13,9},{23,19},{11,15... | collective-permute-start | bytes 2359304 | tf_op jit(solution)/shard_map/ppermute | solution.py:711
  65.1 34.9 %collective-permute-start.1 = (bf16[1536,256]{1,0:T(8,128)(2,1)S(1)}, bf16[1536,256]{1,0:T(8,128)(2,1)S(1)}, u32[]{:S(2)}, u32[]{:S(2)}) collective-permute-start(bf16[1536,256]{1,0:T(8,128)(2,1)S(1)} %get-tuple-element.53), channel_id=1, source_target_pairs={{0,8},{26,18},{6,14},{28,20},{4,2},{30,24},{1,9},{27,19},{7,15},{2... | collective-permute-start | bytes 2359304 | tf_op jit(solution)/shard_map/ppermute | solution.py:711
  65.8 34.2 %collective-permute-start.2 = (bf16[1536,256]{1,0:T(8,128)(2,1)S(1)}, bf16[1536,256]{1,0:T(8,128)(2,1)S(1)}, u32[]{:S(2)}, u32[]{:S(2)}) collective-permute-start(bf16[1536,256]{1,0:T(8,128)(2,1)S(1)} %get-tuple-element.52), channel_id=1, source_target_pairs={{10,8},{16,18},{12,14},{22,20},{0,2},{26,24},{11,9},{17,19},{13,15... | collective-permute-start | bytes 2359304 | tf_op jit(solution)/shard_map/ppermute | solution.py:711
  118.9 9.1 %copy-start.4 = (f32[21,256,256]{2,1,0:T(8,128)}, f32[21,256,256]{2,1,0:T(8,128)S(1)}, u32[]{:S(2)}) copy-start(f32[21,256,256]{2,1,0:T(8,128)S(1)} %gram.1.own_in) | copy-start | bytes 16515076
  118.9 9.1 %collective-permute-start.3 = (f32[21,256,256]{2,1,0:T(8,128)S(1)}, f32[21,256,256]{2,1,0:T(8,128)S(1)}, u32[]{:S(2)}, u32[]{:S(2)}) collective-permute-start(f32[21,256,256]{2,1,0:T(8,128)S(1)} %gram.1.own_in), channel_id=1, source_target_pairs={{0,1},{1,0},{2,3},{3,2},{4,5},{5,4},{6,7},{7,6},{8,9},{9,8},{10,11... | collective-permute-start | bytes 16515080 | tf_op jit(solution)/shard_map/ppermute | solution.py:250
  153.9 22.3 %copy-start.7 = (bf16[1536,768]{1,0:T(8,128)(2,1)}, bf16[1536,768]{1,0:T(8,128)(2,1)S(1)}, u32[]{:S(2)}) copy-start(bf16[1536,768]{1,0:T(8,128)(2,1)S(1)} %get-tuple-element.42.x_in) | copy-start | bytes 7077892
  153.9 9.4 %collective-permute-start.4 = (f32[21,256,256]{2,1,0:T(8,128)}, f32[21,256,256]{2,1,0:T(8,128)}, u32[]{:S(2)}, u32[]{:S(2)}) collective-permute-start(f32[21,256,256]{2,1,0:T(8,128)} %get-tuple-element.35.own_in), channel_id=1, source_target_pairs={{0,1},{1,0},{2,3},{3,2},{4,5},{5,4},{6,7},{7,6},{8,9},{9,8},{10,11... | collective-permute-start | bytes 16515080 | tf_op jit(solution)/shard_map/ppermute | solution.py:250
  176.2 64.5 %collective-permute-start.5 = (bf16[1536,256]{1,0:T(8,128)(2,1)}, bf16[1536,256]{1,0:T(8,128)(2,1)S(1)}, u32[]{:S(2)}, u32[]{:S(2)}) collective-permute-start(bf16[1536,256]{1,0:T(8,128)(2,1)} %get-tuple-element.38), channel_id=1, source_target_pairs={{8,12},{18,22},{14,10},{20,16},{2,6},{24,28},{9,13},{19,23},{15,11... | collective-permute-start | bytes 2359304 | tf_op jit(solution)/shard_map/ppermute | solution.py:769
  177.5 63.2 %collective-permute-start.6 = (bf16[1536,256]{1,0:T(8,128)(2,1)}, bf16[1536,256]{1,0:T(8,128)(2,1)S(1)}, u32[]{:S(2)}, u32[]{:S(2)}) collective-permute-start(bf16[1536,256]{1,0:T(8,128)(2,1)} %get-tuple-element.39), channel_id=1, source_target_pairs={{8,0},{18,26},{14,6},{20,28},{2,10},{24,16},{9,1},{19,27},{15,7},{... | collective-permute-start | bytes 2359304 | tf_op jit(solution)/shard_map/ppermute | solution.py:769
  179.4 28.9 %collective-permute-start.8 = (f32[16]{0:T(128)S(1)}, f32[16]{0:T(128)S(1)}, u32[]{:S(2)}, u32[]{:S(2)}) collective-permute-start(f32[16]{0:T(128)S(1)} %compare_select_fusion.1), channel_id=1, source_target_pairs={{0,2},{2,0},{4,6},{6,4},{8,10},{10,8},{12,14},{14,12},{16,18},{18,... | collective-permute-start | bytes 200 | tf_op jit(solution)/shard_map/ppermute | solution.py:655
  206.8 34.0 %collective-permute-start.7 = (bf16[1536,256]{1,0:T(8,128)(2,1)}, bf16[1536,256]{1,0:T(8,128)(2,1)S(1)}, u32[]{:S(2)}, u32[]{:S(2)}) collective-permute-start(bf16[1536,256]{1,0:T(8,128)(2,1)} %get-tuple-element.40), channel_id=1, source_target_pairs={{8,10},{18,16},{14,12},{20,22},{2,0},{24,26},{9,11},{19,17},{15,13... | collective-permute-start | bytes 2359304 | tf_op jit(solution)/shard_map/ppermute | solution.py:769
  208.3 13.2 %collective-permute-start.9 = (f32[16]{0:T(128)S(1)}, f32[16]{0:T(128)S(1)}, u32[]{:S(2)}, u32[]{:S(2)}) collective-permute-start(f32[16]{0:T(128)S(1)} %fusion.6), channel_id=1, source_target_pairs={{0,4},{2,6},{4,0},{6,2},{8,12},{10,14},{12,8},{14,10},{16,20},{18,... | collective-permute-start | bytes 200 | tf_op jit(solution)/shard_map/ppermute | solution.py:655
  221.6 3.5 %collective-permute-start.10 = (f32[16]{0:T(128)S(1)}, f32[16]{0:T(128)S(1)}, u32[]{:S(2)}, u32[]{:S(2)}) collective-permute-start(f32[16]{0:T(128)S(1)} %fusion.7), channel_id=1, source_target_pairs={{0,8},{2,10},{4,12},{6,14},{8,0},{10,2},{12,4},{14,6},{16,24},{18,... | collective-permute-start | bytes 200 | tf_op jit(solution)/shard_map/ppermute | solution.py:655
  225.1 15.6 %collective-permute-start.11 = (f32[16]{0:T(128)S(1)}, f32[16]{0:T(128)S(1)}, u32[]{:S(2)}, u32[]{:S(2)}) collective-permute-start(f32[16]{0:T(128)S(1)} %add.65), channel_id=1, source_target_pairs={{0,16},{2,18},{4,20},{6,22},{8,24},{10,26},{12,28},{14,30},{16,0},... | collective-permute-start | bytes 200 | tf_op jit(solution)/shard_map/ppermute | solution.py:655
  246.0 5.9 %copy-start.12 = (f32[128,768]{1,0:T(8,128)S(1)}, f32[128,768]{1,0:T(8,128)}, u32[]{:S(2)}) copy-start(f32[128,768]{1,0:T(8,128)} %param.37) | copy-start | bytes 1179652
  246.0 5.9 %copy-start.13 = (f32[128,768]{1,0:T(8,128)S(1)}, f32[128,768]{1,0:T(8,128)}, u32[]{:S(2)}) copy-start(f32[128,768]{1,0:T(8,128)} %param.35) | copy-start | bytes 1179652
  246.1 5.8 %copy-start.14 = (f32[128,768]{1,0:T(8,128)S(1)}, f32[128,768]{1,0:T(8,128)}, u32[]{:S(2)}) copy-start(f32[128,768]{1,0:T(8,128)} %param.34) | copy-start | bytes 1179652
  246.1 5.8 %copy-start.15 = (f32[128,768]{1,0:T(8,128)S(1)}, f32[128,768]{1,0:T(8,128)}, u32[]{:S(2)}) copy-start(f32[128,768]{1,0:T(8,128)} %param.36) | copy-start | bytes 1179652
  246.1 90.9 %all-to-all-start.2 = ((bf16[16,96,1280]{2,1,0:T(8,128)(2,1)}), bf16[16,96,1280]{2,1,0:T(8,128)(2,1)}, u32[]{:S(2)}, u32[]{:S(2)}) async-start(bf16[16,96,1280]{2,1,0:T(8,128)(2,1)} %bitcast.37), calls=%async_computation.2 | async-start | bytes 7864320 | tf_op jit(solution)/shard_map/all_to_all | solution.py:795
  (18 other events, 57.9 us)

commit v7 on v6

--- a/solution.py
+++ b/solution.py
@@ -648,12 +648,9 @@
     )(square_order, swiglu_order, back)
 
 
-def spread(value, chips, chip):
-    known = jnp.where(jnp.arange(chips, dtype=jnp.int32) == chip, value, 0.0)
-    step = 1
-    while step < chips:
+def spread(known, chips, steps):
+    for step in steps:
         known = known + lax.ppermute(known, "dp", [(s, s ^ step) for s in range(chips)])
-        step *= 2
     return known
 
 
@@ -748,13 +745,19 @@
         3 * half + D * D * D,
         small_outs=1,
     )
+    steps = [1 << n for n in range(chips.bit_length() - 1)]
+    logs = jnp.where(
+        jnp.arange(chips, dtype=jnp.int32) == chip, 0.5 * jnp.log(scale[0, 0]), 0.0
+    )
+    logs = spread(logs, chips, steps[len(steps) // 2 :])
+    other_mid, logs = lax.optimization_barrier((other_core(own_mid), logs))
     piece_shape = jax.ShapeDtypeStruct((D, GRANULE), jnp.bfloat16)
     pair_shape = jax.ShapeDtypeStruct((D, 2 * GRANULE), jnp.bfloat16)
     polynomial, kept, *rest = call(
         last_kernel,
         "last",
         [flag, factor],
-        [own_mid, other_core(own_mid), second_mid],
+        [own_mid, other_mid, second_mid],
         [whole_square, pair_shape] + [piece_shape] * plan.passes,
         [packed_buffer] * 2
         + [second_buffer] * 2
@@ -778,8 +781,8 @@
         56,
         2 * D * D * narrow,
     )
-    scale, _ = lax.optimization_barrier((scale, kept))
-    logs = spread(0.5 * jnp.log(scale[0, 0]), chips, chip)
+    logs, back_out = lax.optimization_barrier((logs, back_out))
+    logs = spread(logs, chips, steps[: len(steps) // 2])
     (back_out,) = call(
         join_kernel,
         "join",

time: 342 us -> 338 us (0.988)
  waiting for transfers between devices: 182 us -> 172 us
    ppermute x2, waiting for transfers between devices: 17.6 us -> 9.02 us  [other_core(): return lax.ppermute(x, 'tensor', [(0, 1), (1, 0)])]
    all_to_all x1, starting transfers between devices: 4.56 us -> 10.2 us  [local(): lax.all_to_all(back_out.reshape(chips, chip_rows, -1), 'dp', split_axis=0...]
    unnamed x54 -> x56, local copies, waits for them, and re-layouts: 11.6 us -> 14.9 us
where the time goes in v7:
time: 338 us
  waiting for transfers between devices  172 us (51%)
  Pallas kernels  73.1 us (22%)
  starting transfers between devices  65.5 us (19%)
  local copies, waits for them, and re-layouts  19.1 us (6%)
  other arithmetic  4.66 us (1%)
    all_to_all x1, waiting for transfers between devices, local(): lax.all_to_all(back_out.reshape(chips, chip_rows, -1), 'dp', split_axis=0...  82 us
    pallas_call x5, Pallas kernels, call(): pl.pallas_call(kernel, in_specs=[smem] * len(scalars) + [anywhere] * len(...  51.9 us
    ppermute x4, starting transfers between devices, spread(): lax.ppermute(known, 'dp', [(s, s ^ step) for s in range(chips)])  33.9 us
    ppermute x3, waiting for transfers between devices, local(): lax.ppermute(jnp.where(pick, pieces[1], pieces[0]), 'dp', pairs)  30.1 us
    all_to_all x1, waiting for transfers between devices, local(): lax.all_to_all(second_send.reshape(D, 2 * GRANULE), both, split_axis=0, c...  27.3 us
    unnamed x56, local copies, waits for them, and re-layouts  14.9 us
    ppermute x4, waiting for transfers between devices, spread(): lax.ppermute(known, 'dp', [(s, s ^ step) for s in range(chips)])  12.5 us
    pallas_call x1, Pallas kernels, prepare_wide(): pl.pallas_call(lambda *refs: wide_kernel(plan, cores, *refs), grid=(rows...  11.7 us
  transfers between devices with their start and end apart: 15, of which 9 were waited for; matrix products, arithmetic and copies ran while one was open for 3% of the time, Pallas kernels for 4%

profile of v7, /device:TPU:12, one launch (start us, length us, event | category | flops | bytes accessed | tf_op | source)
XLA Modules:
  0.0 337.7 jit_solution(2485190367063363897)
XLA Ops:
  0.6 11.7 %prepare_wide.1 = (f32[48,32,6,128]{3,2,1,0:T(8,128)}, bf16[32,48,768]{2,1,0:T(8,128)(2,1)}, bf16[32,48,512]{2,1,0:T(8,128)(2,1)}) custom-call(f32[48,32,6,128]{3,2,1,0:T(8,128)} %bitcast.38, f32[48,32,6,128]{3,2,1,0:T(8,128)} %bitcast.39), custom_call_target="tpu_custom_call" | custom-call | tf_op jit(solution)/shard_map/prepare_wide/pallas_call | solution.py:199
  12.3 6.0 %all-to-all-start.1 = ((bf16[32,48,512]{2,1,0:T(8,128)(2,1)}), bf16[32,48,512]{2,1,0:T(8,128)(2,1)S(1)}, u32[]{:S(2)}, u32[]{:S(2)}) async-start(bf16[32,48,512]{2,1,0:T(8,128)(2,1)} %get-tuple-element.37), calls=%async_computation.1 | async-start | bytes 3145728 | tf_op jit(solution)/shard_map/all_to_all | solution.py:696
  21.6 5.1 %prepare_narrow.1 = (f32[48,12,8,128]{3,2,1,0:T(8,128)}, bf16[32,48,768]{2,1,0:T(8,128)(2,1)}) custom-call(f32[48,12,8,128]{3,2,1,0:T(8,128)S(1)} %bitcast.35, f32[48,12,8,128]{3,2,1,0:T(8,128)S(1)} %bitcast.36, bf16[32,48,768]{2,1,0:T(8,128)(2,1)} %get-tuple-element.33.refs_2_), custom_call_target="tpu_custom_call", output_to_operand_aliasing={{1}: (2, {})} | custom-call | bytes 8257536 | tf_op jit(solution)/shard_map/prepare_narrow/pallas_call | solution.py:226
  26.7 27.3 %all-to-all-done.1 = bf16[32,48,512]{2,1,0:T(8,128)(2,1)S(1)} async-done(((bf16[32,48,512]{2,1,0:T(8,128)(2,1)}), bf16[32,48,512]{2,1,0:T(8,128)(2,1)S(1)}, u32[]{:S(2)}, u32[]{:S(2)}) %all-to-all-start.1) | async-done | bytes 1572896 | tf_op jit(solution)/shard_map/all_to_all | solution.py:696
  54.0 5.8 %all-to-all-start = ((bf16[32,48,768]{2,1,0:T(8,128)(2,1)}), bf16[32,48,768]{2,1,0:T(8,128)(2,1)}, u32[]{:S(2)}, u32[]{:S(2)}) async-start(bf16[32,48,768]{2,1,0:T(8,128)(2,1)} %get-tuple-element.36), calls=%async_computation | async-start | bytes 4718592 | tf_op jit(solution)/shard_map/all_to_all | solution.py:699
  62.5 2.5 collective-permute-start
  65.8 2.8 collective-permute-start.2
  69.8 30.1 %collective-permute-done.refs_2_ = bf16[1536,256]{1,0:T(8,128)(2,1)S(1)} collective-permute-done((bf16[1536,256]{1,0:T(8,128)(2,1)S(1)}, bf16[1536,256]{1,0:T(8,128)(2,1)S(1)}, u32[]{:S(2)}, u32[]{:S(2)}) %collective-permute-start) | collective-permute-done | bytes 786464 | tf_op jit(solution)/shard_map/ppermute | solution.py:708
  100.8 11.1 %all-to-all-done = bf16[32,48,768]{2,1,0:T(8,128)(2,1)} async-done(((bf16[32,48,768]{2,1,0:T(8,128)(2,1)}), bf16[32,48,768]{2,1,0:T(8,128)(2,1)}, u32[]{:S(2)}, u32[]{:S(2)}) %all-to-all-start) | async-done | bytes 2359328 | tf_op jit(solution)/shard_map/all_to_all | solution.py:699
  113.1 5.8 %gram.1.own_in = f32[21,256,256]{2,1,0:T(8,128)S(1)} custom-call(s32[1]{0:T(128)S(6)} %convert_element_type.7.flag, bf16[1536,768]{1,0:T(8,128)(2,1)} %bitcast.13.refs_0_, bf16[1536,512]{1,0:T(8,128)(2,1)S(1)} %bitcast.33, bf16[1536,256]{1,0:T(8,128)(2,1)S(1)} %collective-permute-done.refs_2_, bf16[1536,256]{1,0:T(8,128)(2,1)S(1)} %collective-permute-done.1.refs_3_, ...), custom_call_target="tpu_custom_call" | custom-call | flops 4831838208 | bytes 11796480 | tf_op jit(solution)/shard_map/gram/pallas_call | solution.py:574
  119.0 9.0 %collective-permute-done.3.other_in = f32[21,256,256]{2,1,0:T(8,128)S(1)} collective-permute-done((f32[21,256,256]{2,1,0:T(8,128)S(1)}, f32[21,256,256]{2,1,0:T(8,128)S(1)}, u32[]{:S(2)}, u32[]{:S(2)}) %collective-permute-start.3) | collective-permute-done | bytes 5505056 | tf_op jit(solution)/shard_map/ppermute | solution.py:250
  128.0 2.4 copy-done.23
  130.3 21.6 %middle.1 = (bf16[1536,768]{1,0:T(8,128)(2,1)S(1)}, bf16[1536,1280]{1,0:T(8,128)(2,1)S(1)}, f32[21,256,256]{2,1,0:T(8,128)}, f32[8,128]{1,0:T(8,128)S(1)}) custom-call(s32[1]{0:T(128)S(6)} %convert_element_type.7.flag, f32[21,256,256]{2,1,0:T(8,128)} %copy-done.4, f32[21,256,256]{2,1,0:T(8,128)} %copy-done.23, bf16[1536,768]{1,0:T(8,128)(2,1)} %bitcast.13.refs_0_, ...), custom_call_target="tpu_custom_call" | custom-call | flops 18119393280 | bytes 29102080 | tf_op jit(solution)/shard_map/middle/pallas_call | solution.py:574
  156.6 2.7 collective-permute-start.5
  160.8 20.8 %collective-permute-start.6 = (f32[16]{0:T(128)S(1)}, f32[16]{0:T(128)S(1)}, u32[]{:S(2)}, u32[]{:S(2)}) collective-permute-start(f32[16]{0:T(128)S(1)} %fusion.6), channel_id=1, source_target_pairs={{0,16},{2,18},{4,20},{6,22},{8,24},{10,26},{12,28},{14,30},{16,0},... | collective-permute-start | bytes 200 | tf_op jit(solution)/shard_map/ppermute | solution.py:653
  183.2 2.4 copy-done.22
  185.6 12.9 %last.1 = (bf16[1536,1536]{1,0:T(8,128)(2,1)}, bf16[1536,512]{1,0:T(8,128)(2,1)}, bf16[1536,256]{1,0:T(8,128)(2,1)}, bf16[1536,256]{1,0:T(8,128)(2,1)}, bf16[1536,256]{1,0:T(8,128)(2,1)}) custom-call(s32[1]{0:T(128)S(6)} %convert_element_type.7.flag, f32[1]{0:T(128)S(6)} %select_n.63.factor, f32[21,256,256]{2,1,0:T(8,128)} %get-tuple-element.38.own_in, ...), custom_call_target="tpu_custom_call" | custom-call | flops 9663676416 | bytes 23592960 | tf_op jit(solution)/shard_map/last/pallas_call | solution.py:574
  201.9 8.5 %finish.1.refs_3_ = bf16[1536,1280]{1,0:T(8,128)(2,1)} custom-call(f32[1]{0:T(128)S(6)} %select_n.63.factor, bf16[1536,1536]{1,0:T(8,128)(2,1)} %get-tuple-element.47.polynomial_in, bf16[1536,768]{1,0:T(8,128)(2,1)} %copy-done.7), custom_call_target="tpu_custom_call" | custom-call | flops 3623878656 | bytes 11010048 | tf_op jit(solution)/shard_map/finish/pallas_call | solution.py:574
  210.3 8.9 %collective-permute-start.10 = (f32[16]{0:T(128)S(1)}, f32[16]{0:T(128)S(1)}, u32[]{:S(2)}, u32[]{:S(2)}) collective-permute-start(f32[16]{0:T(128)S(1)} %fusion.7), channel_id=1, source_target_pairs={{0,2},{2,0},{4,6},{6,4},{8,10},{10,8},{12,14},{14,12},{16,18},{18,... | collective-permute-start | bytes 200 | tf_op jit(solution)/shard_map/ppermute | solution.py:653
  219.3 9.3 %collective-permute-done.10 = f32[16]{0:T(128)S(1)} collective-permute-done((f32[16]{0:T(128)S(1)}, f32[16]{0:T(128)S(1)}, u32[]{:S(2)}, u32[]{:S(2)}) %collective-permute-start.10) | collective-permute-done | bytes 96 | tf_op jit(solution)/shard_map/ppermute | solution.py:653
  233.6 3.1 join.1
  236.8 10.2 %all-to-all-start.2 = ((bf16[16,96,1280]{2,1,0:T(8,128)(2,1)}), bf16[16,96,1280]{2,1,0:T(8,128)(2,1)}, u32[]{:S(2)}, u32[]{:S(2)}) async-start(bf16[16,96,1280]{2,1,0:T(8,128)(2,1)} %bitcast.37), calls=%async_computation.2 | async-start | bytes 7864320 | tf_op jit(solution)/shard_map/all_to_all | solution.py:798
  251.1 82.0 %all-to-all-done.2.source = bf16[16,96,1280]{2,1,0:T(8,128)(2,1)} async-done(((bf16[16,96,1280]{2,1,0:T(8,128)(2,1)}), bf16[16,96,1280]{2,1,0:T(8,128)(2,1)}, u32[]{:S(2)}, u32[]{:S(2)}) %all-to-all-start.2) | async-done | bytes 3932192 | tf_op jit(solution)/shard_map/all_to_all | solution.py:798
  333.1 4.5 %assemble.1 = (bf16[8,96,768]{2,1,0:T(8,128)(2,1)}, bf16[6,96,2048]{2,1,0:T(8,128)(2,1)}) custom-call(s32[8]{0:T(128)S(1)} %copy-done.2, s32[6]{0:T(128)S(1)} %copy-done.3, bf16[16,96,1280]{2,1,0:T(8,128)(2,1)} %all-to-all-done.2.source), custom_call_target="tpu_custom_call" | custom-call | tf_op jit(solution)/shard_map/assemble/pallas_call | solution.py:639
  (93 shorter events, 27.9 us)
Async XLA Ops:
  12.3 41.7 %all-to-all-start.1 = ((bf16[32,48,512]{2,1,0:T(8,128)(2,1)}), bf16[32,48,512]{2,1,0:T(8,128)(2,1)S(1)}, u32[]{:S(2)}, u32[]{:S(2)}) async-start(bf16[32,48,512]{2,1,0:T(8,128)(2,1)} %get-tuple-element.37), calls=%async_computation.1 | async-start | bytes 3145728 | tf_op jit(solution)/shard_map/all_to_all | solution.py:696
  54.0 57.9 %all-to-all-start = ((bf16[32,48,768]{2,1,0:T(8,128)(2,1)}), bf16[32,48,768]{2,1,0:T(8,128)(2,1)}, u32[]{:S(2)}, u32[]{:S(2)}) async-start(bf16[32,48,768]{2,1,0:T(8,128)(2,1)} %get-tuple-element.36), calls=%async_computation | async-start | bytes 4718592 | tf_op jit(solution)/shard_map/all_to_all | solution.py:699
  62.5 37.4 %collective-permute-start = (bf16[1536,256]{1,0:T(8,128)(2,1)S(1)}, bf16[1536,256]{1,0:T(8,128)(2,1)S(1)}, u32[]{:S(2)}, u32[]{:S(2)}) collective-permute-start(bf16[1536,256]{1,0:T(8,128)(2,1)S(1)} %get-tuple-element.60), channel_id=1, source_target_pairs={{12,8},{22,18},{10,14},{16,20},{6,2},{28,24},{13,9},{23,19},{11,15... | collective-permute-start | bytes 2359304 | tf_op jit(solution)/shard_map/ppermute | solution.py:708
  65.1 34.9 %collective-permute-start.1 = (bf16[1536,256]{1,0:T(8,128)(2,1)S(1)}, bf16[1536,256]{1,0:T(8,128)(2,1)S(1)}, u32[]{:S(2)}, u32[]{:S(2)}) collective-permute-start(bf16[1536,256]{1,0:T(8,128)(2,1)S(1)} %get-tuple-element.59), channel_id=1, source_target_pairs={{0,8},{26,18},{6,14},{28,20},{4,2},{30,24},{1,9},{27,19},{7,15},{2... | collective-permute-start | bytes 2359304 | tf_op jit(solution)/shard_map/ppermute | solution.py:708
  65.8 34.2 %collective-permute-start.2 = (bf16[1536,256]{1,0:T(8,128)(2,1)S(1)}, bf16[1536,256]{1,0:T(8,128)(2,1)S(1)}, u32[]{:S(2)}, u32[]{:S(2)}) collective-permute-start(bf16[1536,256]{1,0:T(8,128)(2,1)S(1)} %get-tuple-element.58), channel_id=1, source_target_pairs={{10,8},{16,18},{12,14},{22,20},{0,2},{26,24},{11,9},{17,19},{13,15... | collective-permute-start | bytes 2359304 | tf_op jit(solution)/shard_map/ppermute | solution.py:708
  118.9 9.1 %collective-permute-start.3 = (f32[21,256,256]{2,1,0:T(8,128)S(1)}, f32[21,256,256]{2,1,0:T(8,128)S(1)}, u32[]{:S(2)}, u32[]{:S(2)}) collective-permute-start(f32[21,256,256]{2,1,0:T(8,128)S(1)} %gram.1.own_in), channel_id=1, source_target_pairs={{0,1},{1,0},{2,3},{3,2},{4,5},{5,4},{6,7},{7,6},{8,9},{9,8},{10,11... | collective-permute-start | bytes 16515080 | tf_op jit(solution)/shard_map/ppermute | solution.py:250
  155.3 27.9 %collective-permute-start.4 = (f32[21,256,256]{2,1,0:T(8,128)}, f32[21,256,256]{2,1,0:T(8,128)S(1)}, u32[]{:S(2)}, u32[]{:S(2)}) collective-permute-start(f32[21,256,256]{2,1,0:T(8,128)} %get-tuple-element.38.own_in), channel_id=1, source_target_pairs={{0,1},{1,0},{2,3},{3,2},{4,5},{5,4},{6,7},{7,6},{8,9},{9,8},{10,11... | collective-permute-start | bytes 16515080 | tf_op jit(solution)/shard_map/ppermute | solution.py:250
  156.6 4.2 %collective-permute-start.5 = (f32[16]{0:T(128)S(1)}, f32[16]{0:T(128)S(1)}, u32[]{:S(2)}, u32[]{:S(2)}) collective-permute-start(f32[16]{0:T(128)S(1)} %compare_select_fusion.1), channel_id=1, source_target_pairs={{0,8},{2,10},{4,12},{6,14},{8,0},{10,2},{12,4},{14,6},{16,24},{18,... | collective-permute-start | bytes 200 | tf_op jit(solution)/shard_map/ppermute | solution.py:653
  160.8 22.3 %collective-permute-start.6 = (f32[16]{0:T(128)S(1)}, f32[16]{0:T(128)S(1)}, u32[]{:S(2)}, u32[]{:S(2)}) collective-permute-start(f32[16]{0:T(128)S(1)} %fusion.6), channel_id=1, source_target_pairs={{0,16},{2,18},{4,20},{6,22},{8,24},{10,26},{12,28},{14,30},{16,0},... | collective-permute-start | bytes 200 | tf_op jit(solution)/shard_map/ppermute | solution.py:653
  198.6 33.6 %collective-permute-start.7 = (bf16[1536,256]{1,0:T(8,128)(2,1)}, bf16[1536,256]{1,0:T(8,128)(2,1)S(1)}, u32[]{:S(2)}, u32[]{:S(2)}) collective-permute-start(bf16[1536,256]{1,0:T(8,128)(2,1)} %get-tuple-element.43), channel_id=1, source_target_pairs={{8,12},{18,22},{14,10},{20,16},{2,6},{24,28},{9,13},{19,23},{15,11... | collective-permute-start | bytes 2359304 | tf_op jit(solution)/shard_map/ppermute | solution.py:772
  199.9 32.3 %collective-permute-start.8 = (bf16[1536,256]{1,0:T(8,128)(2,1)}, bf16[1536,256]{1,0:T(8,128)(2,1)S(1)}, u32[]{:S(2)}, u32[]{:S(2)}) collective-permute-start(bf16[1536,256]{1,0:T(8,128)(2,1)} %get-tuple-element.44), channel_id=1, source_target_pairs={{8,0},{18,26},{14,6},{20,28},{2,10},{24,16},{9,1},{19,27},{15,7},{... | collective-permute-start | bytes 2359304 | tf_op jit(solution)/shard_map/ppermute | solution.py:772
  200.6 31.6 %collective-permute-start.9 = (bf16[1536,256]{1,0:T(8,128)(2,1)}, bf16[1536,256]{1,0:T(8,128)(2,1)S(1)}, u32[]{:S(2)}, u32[]{:S(2)}) collective-permute-start(bf16[1536,256]{1,0:T(8,128)(2,1)} %get-tuple-element.45), channel_id=1, source_target_pairs={{8,10},{18,16},{14,12},{20,22},{2,0},{24,26},{9,11},{19,17},{15,13... | collective-permute-start | bytes 2359304 | tf_op jit(solution)/shard_map/ppermute | solution.py:772
  210.3 18.3 %collective-permute-start.10 = (f32[16]{0:T(128)S(1)}, f32[16]{0:T(128)S(1)}, u32[]{:S(2)}, u32[]{:S(2)}) collective-permute-start(f32[16]{0:T(128)S(1)} %fusion.7), channel_id=1, source_target_pairs={{0,2},{2,0},{4,6},{6,4},{8,10},{10,8},{12,14},{14,12},{16,18},{18,... | collective-permute-start | bytes 200 | tf_op jit(solution)/shard_map/ppermute | solution.py:653
  228.6 3.5 %collective-permute-start.11 = (f32[16]{0:T(128)S(1)}, f32[16]{0:T(128)S(1)}, u32[]{:S(2)}, u32[]{:S(2)}) collective-permute-start(f32[16]{0:T(128)S(1)} %add.65), channel_id=1, source_target_pairs={{0,4},{2,6},{4,0},{6,2},{8,12},{10,14},{12,8},{14,10},{16,20},{18,... | collective-permute-start | bytes 200 | tf_op jit(solution)/shard_map/ppermute | solution.py:653
  236.7 10.8 %copy-start.20 = (s32[16,2]{0,1:T(2,128)S(1)}, s32[16,2]{0,1:T(2,128)}, u32[]{:S(2)}) copy-start(s32[16,2]{0,1:T(2,128)} %param.38) | copy-start | bytes 388
  236.7 10.9 %copy-start.16 = (f32[1344]{0:T(1024)S(1)}, f32[1344]{0:T(1024)}, u32[]{:S(2)}) copy-start(f32[1344]{0:T(1024)} %param.30) | copy-start | bytes 16132
  236.7 10.9 %copy-start.17 = (f32[1344]{0:T(1024)S(1)}, f32[1344]{0:T(1024)}, u32[]{:S(2)}) copy-start(f32[1344]{0:T(1024)} %param.31) | copy-start | bytes 16132
  236.7 10.9 %copy-start.18 = (f32[1344]{0:T(1024)S(1)}, f32[1344]{0:T(1024)}, u32[]{:S(2)}) copy-start(f32[1344]{0:T(1024)} %param.32) | copy-start | bytes 16132
  236.7 10.9 %copy-start.19 = (f32[1344]{0:T(1024)S(1)}, f32[1344]{0:T(1024)}, u32[]{:S(2)}) copy-start(f32[1344]{0:T(1024)} %param.33) | copy-start | bytes 16132
  236.8 11.5 %copy-start.12 = (f32[128,768]{1,0:T(8,128)S(1)}, f32[128,768]{1,0:T(8,128)}, u32[]{:S(2)}) copy-start(f32[128,768]{1,0:T(8,128)} %param.37) | copy-start | bytes 1179652
  236.8 11.5 %copy-start.13 = (f32[128,768]{1,0:T(8,128)S(1)}, f32[128,768]{1,0:T(8,128)}, u32[]{:S(2)}) copy-start(f32[128,768]{1,0:T(8,128)} %param.35) | copy-start | bytes 1179652
  236.8 11.5 %copy-start.14 = (f32[128,768]{1,0:T(8,128)S(1)}, f32[128,768]{1,0:T(8,128)}, u32[]{:S(2)}) copy-start(f32[128,768]{1,0:T(8,128)} %param.34) | copy-start | bytes 1179652
  236.8 11.5 %copy-start.15 = (f32[128,768]{1,0:T(8,128)S(1)}, f32[128,768]{1,0:T(8,128)}, u32[]{:S(2)}) copy-start(f32[128,768]{1,0:T(8,128)} %param.36) | copy-start | bytes 1179652
  236.8 96.3 %all-to-all-start.2 = ((bf16[16,96,1280]{2,1,0:T(8,128)(2,1)}), bf16[16,96,1280]{2,1,0:T(8,128)(2,1)}, u32[]{:S(2)}, u32[]{:S(2)}) async-start(bf16[16,96,1280]{2,1,0:T(8,128)(2,1)} %bitcast.37), calls=%async_computation.2 | async-start | bytes 7864320 | tf_op jit(solution)/shard_map/all_to_all | solution.py:798
  (19 other events, 89.0 us)
